TPU v7x, 32 devices: a whole 2x2x4 slice. The times are simulated.
32 devices in a mesh: gx: 4 (over y, core), gy: 4 (over z), ga: 2 (over x).
Axes of the slice: x: 2, y: 2, z: 4, core: 2. Of those that a mesh axis runs over, the one named last changes fastest.
Arguments:
- offsets: float32 [3, 8, 8, 32, 128], P(None, 'gx', 'gy', 'ga'), may hold values from 0 to 1
- charge: float32 [8, 8, 32, 128], P('gx', 'gy', 'ga'), may hold values from -3 to 3
- counts: int32 [8, 8, 32], P('gx', 'gy', 'ga'), may hold values from 8 to 128, as said below
- partners: int32 [8, 8, 32, 128], P('gx', 'gy', 'ga'), may hold values from 0 to 127
Outputs:
- short_force: float32 [3, 8, 8, 32, 128], P(None, 'gx', 'gy', 'ga')
- long_force: float32 [3, 8, 8, 32, 128], P(None, 'gx', 'gy', 'ga')
Inputs may be any that keep to these rules, and one draw needn't show every extreme that they name: `counts`: each cell holds at least 8 beads and at most 128; some cell holds exactly 128.
All inputs are finite; a program needn't handle non-finite values.
Results may differ from a plain program's by a relative error of at most 0.0003.
Values sent between devices are 32-bit elements; how exact they have to be, the bound alone decides.
A program may use at most 192 MiB of HBM per device.

v0:
```python
import jax
import jax.numpy as jnp
from jax import lax
from jax.sharding import PartitionSpec as P

highest = lax.Precision.HIGHEST
cutoff_sq = 64.0
soften_sq = 1.0
bond_spring = 0.1
fine_scale = 4.0
coarse_scale = 2.0
fine_spread = 2.5
coarse_spread = 6.0


def padded_2(value, sides, width):
    for axis, dim in sides:
        size, length = (lax.axis_size(axis), value.shape[dim])
        up = [(i, (i + 1) % size) for i in range(size - 1)]
        down = [(j, i) for i, j in up]
        last = lax.slice_in_dim(value, length - width, length, axis=dim)
        initial = lax.slice_in_dim(value, 0, width, axis=dim)
        before = lax.ppermute(last, axis, up)
        after = lax.ppermute(initial, axis, down)
        value = jnp.concatenate([before, value, after], axis=dim)
    return value


def spline(shifted):
    magnitude = jnp.abs(shifted)
    margin = jnp.maximum(1.5 - magnitude, 0.0)
    return jnp.where(magnitude < 0.5, 0.75 - shifted * shifted, 0.5 * margin * margin)


def spline_slope(shifted):
    magnitude = jnp.abs(shifted)
    margin = jnp.maximum(1.5 - magnitude, 0.0)
    return jnp.where(magnitude < 0.5, -2.0 * shifted, jnp.where(shifted > 0.0, -margin, margin))


def patch_weights(offset):
    points = jnp.arange(11).astype(jnp.float32)
    shifted = 8.0 * offset[..., None] + 1.0 - points
    return (spline(shifted), spline_slope(shifted))


def charge_patches(weighted, offsets):
    weight_x, _ = patch_weights(offsets[0])
    weight_y, _ = patch_weights(offsets[1])
    weight_z, _ = patch_weights(offsets[2])
    plane_part = weighted[..., None, None] * weight_x[..., :, None] * weight_y[..., None, :]
    flattened = plane_part.reshape(plane_part.shape[:-2] + (121,))
    joined = jnp.einsum("...sp,...sc->...pc", flattened, weight_z, precision=highest)
    return joined.reshape(joined.shape[:-2] + (11, 11, 11))


def assemble(values, where_axis):
    cell_count = values.shape[where_axis]
    inner_part = lax.slice_in_dim(values, 0, 8, axis=where_axis + 1)
    overflow = lax.slice_in_dim(values, 8, 11, axis=where_axis + 1)
    inner_pad = [(0, 0)] * values.ndim
    inner_pad[where_axis] = (0, 1)
    over_pad = [(0, 0)] * values.ndim
    over_pad[where_axis] = (1, 0)
    over_pad[where_axis + 1] = (0, 5)
    merged = jnp.pad(inner_part, inner_pad) + jnp.pad(overflow, over_pad)
    new_shape = values.shape[:where_axis] + (8 * (cell_count + 1),) + values.shape[where_axis + 2 :]
    return merged.reshape(new_shape)


def cut_patches(values, where_axis):
    cell_count = (values.shape[where_axis] - 4) // 8
    split_shape = values.shape[:where_axis] + (cell_count, 8) + values.shape[where_axis + 1 :]
    head_part = lax.slice_in_dim(values, 1, 8 * cell_count + 1, axis=where_axis).reshape(
        split_shape
    )
    widths = [(0, 0)] * values.ndim
    widths[where_axis] = (0, 5)
    padded = jnp.pad(values, widths)
    tail_part = lax.slice_in_dim(padded, 9, 8 * cell_count + 9, axis=where_axis).reshape(
        split_shape
    )
    tail_part = lax.slice_in_dim(tail_part, 0, 3, axis=where_axis + 1)
    return jnp.concatenate([head_part, tail_part], axis=where_axis + 1)


def kernel_band(in_length, spread):
    row_index = jnp.arange(in_length)[:, None]
    column_index = jnp.arange(in_length - 16)[None, :]
    distance = row_index - column_index - 8
    gap = distance.astype(jnp.float32)
    return jnp.where(jnp.abs(distance) <= 8, jnp.exp(-gap * gap / (2.0 * spread * spread)), 0.0)


def along_axis(values, matrix, where_axis):
    contracted = jnp.tensordot(values, matrix, axes=([where_axis], [0]), precision=highest)
    return jnp.moveaxis(contracted, -1, where_axis)


def convolve(values, spread, strength):
    for where_axis in range(3):
        values = along_axis(values, kernel_band(values.shape[where_axis], spread), where_axis)
    return strength * values


def grid_map(fine_length, coarse_length, fine_start, coarse_start):
    fine_index = jnp.arange(fine_length)[:, None] + fine_start
    coarse_index = jnp.arange(coarse_length)[None, :] + coarse_start
    gap = fine_index - 2 * coarse_index
    return jnp.where(gap == 0, 1.0, jnp.where(jnp.abs(gap) == 1, 0.5, 0.0)).astype(jnp.float32)


def cell_positions(offsets, first_cell):
    coordinates = []
    for dimension in range(3):
        cell_count = offsets.shape[dimension + 1]
        cell_index = jnp.arange(cell_count).astype(jnp.float32) + first_cell
        broadcast_shape = [1, 1, 1, 1]
        broadcast_shape[dimension] = cell_count
        coordinates.append((cell_index.reshape(broadcast_shape) + offsets[dimension]) * 8.0)
    return jnp.stack(coordinates)


def pair_sum(own_pos, own_charge, near_pos, near_charge):
    separation = own_pos[..., :, None] - near_pos[..., None, :]
    distance_sq = jnp.sum(separation * separation, axis=0)
    reach_left = jnp.maximum(1.0 - distance_sq / cutoff_sq, 0.0)
    strength = (
        reach_left * reach_left * reach_left / (distance_sq + soften_sq) * near_charge[..., None, :]
    )
    return own_charge * jnp.sum(separation * strength, axis=-1)


def bond_force(positions, in_use, partners):
    slot_ids = jnp.arange(positions.shape[-1])
    picker = (partners[..., :, None] == slot_ids).astype(jnp.float32)
    partner_pos = jnp.einsum("...sp,d...p->d...s", picker, positions, precision=highest)
    partner_use = jnp.einsum("...sp,...p->...s", picker, in_use, precision=highest)
    return -bond_spring * (positions - partner_pos) * (in_use * partner_use)


def grid_force(patches, weighted, offsets):
    weight_x, slope_x = patch_weights(offsets[0])
    weight_y, slope_y = patch_weights(offsets[1])
    weight_z, slope_z = patch_weights(offsets[2])
    flattened = patches.reshape(patches.shape[:-3] + (121, 11))
    level_part = jnp.einsum("...pc,...sc->...sp", flattened, weight_z, precision=highest)
    rising = jnp.einsum("...pc,...sc->...sp", flattened, slope_z, precision=highest)
    level_part = level_part.reshape(level_part.shape[:-1] + (11, 11))
    rising = rising.reshape(rising.shape[:-1] + (11, 11))
    force_x = jnp.sum(slope_x[..., :, None] * weight_y[..., None, :] * level_part, axis=(-2, -1))
    force_y = jnp.sum(weight_x[..., :, None] * slope_y[..., None, :] * level_part, axis=(-2, -1))
    force_z = jnp.sum(weight_x[..., :, None] * weight_y[..., None, :] * rising, axis=(-2, -1))
    return -weighted * jnp.stack([force_x, force_y, force_z])


def inside_grid(fine_length, first_point, device_count):
    coordinate = jnp.arange(fine_length + 4) - 2 + first_point
    return ((coordinate >= 0) & (coordinate < fine_length * device_count)).astype(jnp.float32)


def per_device(offsets, charge, counts, partners):
    slot_count = charge.shape[-1]
    cells_x, cells_y, cells_z = charge.shape[:3]
    in_use = (jnp.arange(slot_count) < counts[..., None]).astype(jnp.float32)
    weighted = charge * in_use
    packed = jnp.concatenate([offsets, weighted[None]], axis=0)
    grown_tiles = padded_2(packed, (("gx", 1), ("gy", 2), ("ga", 3)), 1)
    grown_offsets = grown_tiles[:3]
    grown_charge = grown_tiles[3]
    grown_pos = cell_positions(grown_offsets, -1.0)
    positions = grown_pos[:, 1 : cells_x + 1, 1 : cells_y + 1, 1 : cells_z + 1]
    block_cells = 8

    def pair_block(start):
        pos_part = lax.dynamic_slice_in_dim(grown_pos, start, block_cells + 2, axis=3)
        charge_part = lax.dynamic_slice_in_dim(grown_charge, start, block_cells + 2, axis=2)
        own_pos = pos_part[:, 1 : cells_x + 1, 1 : cells_y + 1, 1 : block_cells + 1]
        own_charge = charge_part[1 : cells_x + 1, 1 : cells_y + 1, 1 : block_cells + 1]
        near_pos = jnp.concatenate(
            [
                pos_part[
                    :,
                    step_x : step_x + cells_x,
                    step_y : step_y + cells_y,
                    step_z : step_z + block_cells,
                ]
                for step_x in range(3)
                for step_y in range(3)
                for step_z in range(3)
            ],
            axis=-1,
        )
        near_charge = jnp.concatenate(
            [
                charge_part[
                    step_x : step_x + cells_x,
                    step_y : step_y + cells_y,
                    step_z : step_z + block_cells,
                ]
                for step_x in range(3)
                for step_y in range(3)
                for step_z in range(3)
            ],
            axis=-1,
        )
        return pair_sum(own_pos, own_charge, near_pos, near_charge)

    starts = jnp.arange(cells_z // block_cells) * block_cells
    block_forces = lax.map(pair_block, starts)
    pair_part = jnp.moveaxis(block_forces, 0, 3).reshape(positions.shape)
    short_force = pair_part + bond_force(positions, in_use, partners)
    patches = charge_patches(grown_charge, grown_offsets)
    spread_grid = jnp.transpose(patches, (0, 3, 1, 4, 2, 5))
    for where_axis in range(3):
        spread_grid = assemble(spread_grid, where_axis)
    grid_x, grid_y, grid_z = (8 * cells_x, 8 * cells_y, 8 * cells_z)
    fine_charge = spread_grid[9 : 9 + grid_x, 9 : 9 + grid_y, 9 : 9 + grid_z]
    halo_depth = 10
    widened = padded_2(fine_charge, (("gx", 0), ("gy", 1), ("ga", 2)), halo_depth)
    fine_potential = convolve(widened, fine_spread, fine_scale)
    coarse_charge = widened
    for where_axis, fine_length in enumerate((grid_x, grid_y, grid_z)):
        coarse_charge = along_axis(
            coarse_charge,
            grid_map(fine_length + 2 * halo_depth, fine_length // 2, -halo_depth, 0),
            where_axis,
        )
    grown_coarse = padded_2(coarse_charge, (("gx", 0), ("gy", 1), ("ga", 2)), 8)
    coarse_potential = convolve(grown_coarse, coarse_spread, coarse_scale)
    coarse_near = padded_2(coarse_potential, (("gx", 0), ("gy", 1), ("ga", 2)), 2)
    potential = coarse_near
    for where_axis, fine_length in enumerate((grid_x, grid_y, grid_z)):
        potential = along_axis(
            potential,
            jnp.transpose(grid_map(fine_length + 4, fine_length // 2 + 4, -2, -2)),
            where_axis,
        )
    inside_x = inside_grid(grid_x, lax.axis_index("gx") * grid_x, lax.axis_size("gx"))
    inside_y = inside_grid(grid_y, lax.axis_index("gy") * grid_y, lax.axis_size("gy"))
    inside_z = inside_grid(grid_z, lax.axis_index("ga") * grid_z, lax.axis_size("ga"))
    inside_mask = inside_x[:, None, None] * inside_y[None, :, None] * inside_z[None, None, :]
    potential = (potential + fine_potential) * inside_mask
    for where_axis in range(3):
        potential = cut_patches(potential, 2 * where_axis)
    near_grid = jnp.transpose(potential, (0, 2, 4, 1, 3, 5))
    long_force = grid_force(near_grid, weighted, offsets)
    return (short_force, long_force)


def solution(mesh):
    return jax.shard_map(
        per_device,
        mesh=mesh,
        in_specs=(
            P(None, "gx", "gy", "ga", None),
            P("gx", "gy", "ga", None),
            P("gx", "gy", "ga"),
            P("gx", "gy", "ga", None),
        ),
        out_specs=(P(None, "gx", "gy", "ga", None), P(None, "gx", "gy", "ga", None)),
        check_vma=False,
    )
```

profile of v0, /device:TPU:0, one launch (start us, length us, event | category | flops | bytes accessed | tf_op | source)
XLA Modules:
  0.0 520.6 jit_solution(7593901126076083765)
XLA Ops:
  2.5 2.8 fusion.10
  6.1 2.4 collective-permute-start
  12.7 4.6 broadcast_multiply_fusion.1
  18.3 4.3 collective-permute-start.2
  25.1 4.6 collective-permute-done.3
  29.7 3.4 collective-permute-start.4
  35.6 3.4 collective-permute-done.5
  44.3 3.6 broadcast_multiply_fusion
  47.9 30.1 %fusion.5 = f32[4,4,18,121,11]{3,4,2,1,0:T(8,128)S(1)} fusion(f32[4,4,18,128,121]{3,1,4,2,0:T(4,128)S(1)} %bitcast.113, f32[4,4,18,128]{3,2,1,0:T(8,128)S(1)} %copy.229, f32[11]{0:T(128)S(1)} %iota_convert_fusion), kind=kOutput, calls=%fused_computation.91 | convolution fusion | flops 592846848 | bytes 19522988 | tf_op jit(solution)/shard_map/...sp,...sc->...pc/dot_general | solution.py:53
  77.9 13.9 %copy.231 = f32[4,4,18,121,11]{2,1,4,3,0:T(4,128)} copy(f32[4,4,18,121,11]{3,4,2,1,0:T(8,128)S(1)} %fusion.5) | data formatting | bytes 3066624 | tf_op jit(solution)/shard_map/...sp,...sc->...pc/dot_general | solution.py:53
  91.8 7.7 %slice.358 = f32[4,8,4,11,18,11]{4,2,5,3,1,0:T(4,128)} slice(f32[4,11,4,11,18,11]{4,2,5,3,1,0:T(4,128)} %bitcast.114), slice={[0:4], [0:8], [0:4], [0:11], [0:18], [0:11]} | slice | bytes 2230272 | tf_op jit(solution)/shard_map/slice | solution.py:59
  99.5 2.4 slice.359
  101.8 9.5 %pad_add_fusion = f32[5,8,4,11,18,11]{4,2,5,3,1,0:T(4,128)} fusion(f32[4,3,4,11,18,11]{4,2,5,3,1,0:T(4,128)S(1)} %slice.359, f32[4,8,4,11,18,11]{4,2,5,3,1,0:T(4,128)} %slice.358), kind=kLoop, calls=%fused_computation.94 | loop fusion | flops 348480 | bytes 2927232 | tf_op jit(solution)/shard_map/add | solution.py:66
  111.4 4.5 copy.357
  118.0 2.6 pad_add_fusion.1
  120.6 3.6 slice.362
  125.8 6.2 %copy.262 = f32[40,40,18,8]{1,3,2,0:T(8,128)S(1)} copy(f32[40,40,18,8]{2,0,3,1:T(8,128)} %slice.362) | data formatting | bytes 1843200
  132.0 4.3 copy.263
  136.3 1.8 add_bitcast_fusion
  140.4 1.8 collective-permute-start.6
  145.8 3.4 collective-permute-done.7
  149.3 3.5 collective-permute-start.8
  156.0 4.4 collective-permute-done.9
  164.6 2.5 collective-permute-done.10
  167.5 4.7 collective-permute-done.11
  175.3 3.2 collective-permute-start.12
  179.8 242.1 %while.10 = (s32[]{:T(128)}, f32[2,3,2,2,8,128]{5,4,3,2,1,0:T(8,128)}, s32[2]{0:T(128)S(1)}, f32[4,4,18,128]{3,2,1,0:T(8,128)S(1)}, f32[3,4,4,18,128]{4,2,3,1,0:...) while((s32[]{:T(128)}, f32[2,3,2,2,8,128]{5,4,3,2,1,0:T(8,128)}, s32[2]{0:T(128)S(1)}, ...), condition=%wide.region_3.4_spmd, body=%wide.region_0.3_spmd.sunk | while | flops 353894400 | bytes 236896768 | solution.py:210
  183.5 41.3 %fusion.304 = f32[2,2,8,128,3456]{4,3,2,1,0:T(8,128)} fusion(f32[3,2,2,8,3456]{4,3,2,1,0:T(8,128)S(1)} %constant_dynamic-update-slice_fusion.132, f32[3,2,2,8,128]{4,3,2,1,0:T(8,128)S(1)} %get-tuple-element.262), kind=kLoop, calls=%fused_computation.2.clone.1 | loop fusion | flops 113246208 | bytes 57999360 | tf_op jit(solution)/shard_map/while/body/eval_jaxpr/reduce_sum | solution.py:126
  225.4 36.7 %fusion.305 = f32[2,2,8,128,3456]{4,3,2,1,0:T(8,128)} fusion(f32[2,2,8,128,3456]{4,3,2,1,0:T(8,128)} %fusion.304, f32[2,2,8,3456]{3,2,1,0:T(8,128)S(1)} %constant_dynamic-update-slice_fusion.159), kind=kLoop, calls=%fused_computation.6.clone.1 | loop fusion | flops 113246208 | bytes 113688576 | tf_op jit(solution)/shard_map/while/body/eval_jaxpr/mul | solution.py:129
  262.1 38.0 %fusion.306 = f32[3,2,2,8,128]{4,3,2,1,0:T(8,128)S(1)} fusion(f32[2,2,8,128,3456]{4,3,2,1,0:T(8,128)} %fusion.305, f32[3,2,2,8,3456]{4,3,2,1,0:T(8,128)S(1)} %constant_dynamic-update-slice_fusion.132, f32[3,2,2,8,128]{4,3,2,1,0:T(8,128)S(1)} %get-tuple-element.262), kind=kLoop, calls=%fused_computation.3.clone.1 | loop fusion | flops 127389696 | bytes 58048512 | tf_op jit(solution)/shard_map/while/body/eval_jaxpr/reduce_sum | solution.py:131
  304.5 41.3 %fusion.304 = f32[2,2,8,128,3456]{4,3,2,1,0:T(8,128)} fusion(f32[3,2,2,8,3456]{4,3,2,1,0:T(8,128)S(1)} %constant_dynamic-update-slice_fusion.132, f32[3,2,2,8,128]{4,3,2,1,0:T(8,128)S(1)} %get-tuple-element.262), kind=kLoop, calls=%fused_computation.2.clone.1 | loop fusion | flops 113246208 | bytes 57999360 | tf_op jit(solution)/shard_map/while/body/eval_jaxpr/reduce_sum | solution.py:126
  346.4 36.7 %fusion.305 = f32[2,2,8,128,3456]{4,3,2,1,0:T(8,128)} fusion(f32[2,2,8,128,3456]{4,3,2,1,0:T(8,128)} %fusion.304, f32[2,2,8,3456]{3,2,1,0:T(8,128)S(1)} %constant_dynamic-update-slice_fusion.159), kind=kLoop, calls=%fused_computation.6.clone.1 | loop fusion | flops 113246208 | bytes 113688576 | tf_op jit(solution)/shard_map/while/body/eval_jaxpr/mul | solution.py:129
  383.1 38.0 %fusion.306 = f32[3,2,2,8,128]{4,3,2,1,0:T(8,128)S(1)} fusion(f32[2,2,8,128,3456]{4,3,2,1,0:T(8,128)} %fusion.305, f32[3,2,2,8,3456]{4,3,2,1,0:T(8,128)S(1)} %constant_dynamic-update-slice_fusion.132, f32[3,2,2,8,128]{4,3,2,1,0:T(8,128)S(1)} %get-tuple-element.262), kind=kLoop, calls=%fused_computation.3.clone.1 | loop fusion | flops 127389696 | bytes 58048512 | tf_op jit(solution)/shard_map/while/body/eval_jaxpr/reduce_sum | solution.py:131
  422.7 3.5 collective-permute-start.14
  427.5 4.0 fusion.11
  434.6 1.9 collective-permute-start.16
  438.5 4.3 collective-permute-done.16
  442.8 4.1 collective-permute-done.17
  454.3 4.3 collective-permute-start.20
  460.9 3.3 collective-permute-done.21
  468.8 4.4 collective-permute-done.23
  475.5 3.6 reshape.347
  479.5 3.6 reshape.348
  483.0 6.3 %maximum_bitcast_fusion = f32[2,2,16,11,11,11]{5,2,1,4,3,0:T(8,128)} fusion(f32[2,11,2,11,16,3]{5,4,2,3,1,0:T(8,128)} %bitcast.123, f32[2,11,2,11,16,8]{5,4,2,3,1,0:T(8,128)} %reshape.347), kind=kLoop, calls=%fused_computation.106 | loop fusion | flops 85184 | bytes 681472 | tf_op jit(solution)/shard_map/transpose | solution.py:246
  489.4 7.2 %copy.250 = f32[2,2,16,11,11,11]{2,1,5,4,3,0:T(2,128)S(1)} copy(f32[2,2,16,11,11,11]{5,2,1,4,3,0:T(8,128)} %maximum_bitcast_fusion) | data formatting | bytes 681472 | tf_op jit(solution)/shard_map/transpose | solution.py:246
  496.6 3.4 copy.251
  500.0 9.6 %fusion.7 = f32[2,2,16,128]{3,2,1,0:T(8,128)S(1)} fusion(f32[2,2,16,128,121]{3,2,4,1,0:T(8,128)} %bitcast.122, f32[2,2,16,121,11]{3,4,2,1,0:T(8,128)} %copy.251, f32[2,2,16,128]{3,2,1,0:T(8,128)S(1)} %copy-done.19, f32[11]{0:T(128)S(1)} %copy-done.29), kind=kOutput, calls=%fused_computation.98 | convolution fusion | flops 133718016 | bytes 4371244 | tf_op jit(solution)/shard_map/...pc,...sc->...sp/dot_general | solution.py:148
  509.7 10.1 %fusion.9 = (f32[2,2,16,128]{3,2,1,0:T(8,128)S(1)}, f32[2,2,16,128]{3,2,1,0:T(8,128)S(1)}) fusion(f32[2,2,16,128,121]{3,2,4,1,0:T(8,128)} %bitcast.121, f32[2,2,16,128,121]{3,2,4,1,0:T(8,128)S(1)} %bitcast.120, f32[2,2,16,121,11]{3,4,2,1,0:T(8,128)S(1)} %copy-done.4, f32[2,2,16,128]{3,2,1,0:T(8,128)S(1)} %copy-done.19, f32[11]{0:T(128)S(1)} %copy-done.29), kind=kOutput, calls=%fused_computation.102 | convolution fusion | flops 135692288 | bytes 8368940 | tf_op jit(solution)/shard_map/...pc,...sc->...sp/dot_general | solution.py:147
  (317 shorter events, 69.3 us)
Async XLA Ops:
  6.1 11.8 %collective-permute-start = (f32[4,1,2,16,128]{4,2,3,1,0:T(2,128)S(1)}, f32[4,1,2,16,128]{4,2,3,1,0:T(2,128)S(1)}, u32[]{:S(2)}, u32[]{:S(2)}) collective-permute-start(f32[4,1,2,16,128]{4,2,3,1,0:T(2,128)S(1)} %get-tuple-element.148), channel_id=1, source_target_pairs={{0,8},{8,16},{16,24},{1,9},{9,17},{17,25},{2,10},{10,18},{18,26},{... | collective-permute-start | bytes 196616 | tf_op jit(solution)/shard_map/ppermute | solution.py:23
  8.5 9.5 %collective-permute-start.1 = (f32[4,1,2,16,128]{4,2,3,1,0:T(2,128)S(1)}, f32[4,1,2,16,128]{4,2,3,1,0:T(2,128)S(1)}, u32[]{:S(2)}, u32[]{:S(2)}) collective-permute-start(f32[4,1,2,16,128]{4,2,3,1,0:T(2,128)S(1)} %get-tuple-element.149), channel_id=1, source_target_pairs={{8,0},{16,8},{24,16},{9,1},{17,9},{25,17},{10,2},{18,10},{26,18},{... | collective-permute-start | bytes 196616 | tf_op jit(solution)/shard_map/ppermute | solution.py:24
  9.8 38.0 %copy-start.28 = (f32[11]{0:T(128)}, f32[11]{0:T(128)S(1)}, u32[]{:S(2)}) copy-start(f32[11]{0:T(128)S(1)} %iota_convert_fusion) | copy-start | bytes 136
  18.3 6.8 %collective-permute-start.2 = (f32[4,4,1,16,128]{4,2,3,1,0:T(1,128)S(1)}, f32[4,4,1,16,128]{4,2,3,1,0:T(1,128)S(1)}, u32[]{:S(2)}, u32[]{:S(2)}) collective-permute-start(f32[4,4,1,16,128]{4,2,3,1,0:T(1,128)S(1)} %get-tuple-element.146), channel_id=1, source_target_pairs={{0,2},{2,4},{4,6},{1,3},{3,5},{5,7},{8,10},{10,12},{12,14},{9,11},... | collective-permute-start | bytes 393224 | tf_op jit(solution)/shard_map/ppermute | solution.py:23
  22.6 7.1 %collective-permute-start.3 = (f32[4,4,1,16,128]{4,2,3,1,0:T(1,128)S(1)}, f32[4,4,1,16,128]{4,2,3,1,0:T(1,128)S(1)}, u32[]{:S(2)}, u32[]{:S(2)}) collective-permute-start(f32[4,4,1,16,128]{4,2,3,1,0:T(1,128)S(1)} %get-tuple-element.147), channel_id=1, source_target_pairs={{2,0},{4,2},{6,4},{3,1},{5,3},{7,5},{10,8},{12,10},{14,12},{11,9},... | collective-permute-start | bytes 393224 | tf_op jit(solution)/shard_map/ppermute | solution.py:24
  29.7 5.9 %collective-permute-start.4 = (f32[4,4,4,1,128]{4,2,3,1,0:T(4,128)S(1)}, f32[4,4,4,1,128]{4,2,3,1,0:T(4,128)S(1)}, u32[]{:S(2)}, u32[]{:S(2)}) collective-permute-start(f32[4,4,4,1,128]{4,2,3,1,0:T(4,128)S(1)} %get-tuple-element.135), channel_id=1, source_target_pairs={{0,1},{2,3},{4,5},{6,7},{8,9},{10,11},{12,13},{14,15},{16,17},{18,... | collective-permute-start | bytes 98312 | tf_op jit(solution)/shard_map/ppermute | solution.py:23
  33.1 5.9 %collective-permute-start.5 = (f32[4,4,4,1,128]{4,2,3,1,0:T(4,128)S(1)}, f32[4,4,4,1,128]{4,2,3,1,0:T(4,128)S(1)}, u32[]{:S(2)}, u32[]{:S(2)}) collective-permute-start(f32[4,4,4,1,128]{4,2,3,1,0:T(4,128)S(1)} %get-tuple-element.136), channel_id=1, source_target_pairs={{1,0},{3,2},{5,4},{7,6},{9,8},{11,10},{13,12},{15,14},{17,16},{19,... | collective-permute-start | bytes 98312 | tf_op jit(solution)/shard_map/ppermute | solution.py:24
  140.4 5.3 %collective-permute-start.6 = (f32[10,16,128]{2,0,1:T(8,128)S(1)}, f32[10,16,128]{2,0,1:T(8,128)S(1)}, u32[]{:S(2)}, u32[]{:S(2)}) collective-permute-start(f32[10,16,128]{2,0,1:T(8,128)S(1)} %copy.264), channel_id=1, source_target_pairs={{0,8},{8,16},{16,24},{1,9},{9,17},{17,25},{2,10},{10,18},{18,26},{... | collective-permute-start | bytes 245768 | tf_op jit(solution)/shard_map/ppermute | solution.py:23
  142.5 6.7 %collective-permute-start.7 = (f32[10,16,128]{2,0,1:T(8,128)S(1)}, f32[10,16,128]{2,0,1:T(8,128)S(1)}, u32[]{:S(2)}, u32[]{:S(2)}) collective-permute-start(f32[10,16,128]{2,0,1:T(8,128)S(1)} %copy.266), channel_id=1, source_target_pairs={{8,0},{16,8},{24,16},{9,1},{17,9},{25,17},{10,2},{18,10},{26,18},{... | collective-permute-start | bytes 245768 | tf_op jit(solution)/shard_map/ppermute | solution.py:24
  145.7 26.9 %copy-start.5 = (f32[16,16,128]{2,0,1:T(8,128)}, f32[16,16,128]{2,0,1:T(8,128)S(1)}, u32[]{:S(2)}) copy-start(f32[16,16,128]{2,0,1:T(8,128)S(1)} %copy.265) | copy-start | bytes 393220
  145.8 26.9 %copy-start.14 = (f32[10,16,128]{2,0,1:T(8,128)}, f32[10,16,128]{2,0,1:T(8,128)S(1)}, u32[]{:S(2)}) copy-start(f32[10,16,128]{2,0,1:T(8,128)S(1)} %collective-permute-done.6) | copy-start | bytes 245764
  149.2 23.4 %copy-start.16 = (f32[10,16,128]{2,0,1:T(8,128)}, f32[10,16,128]{2,0,1:T(8,128)S(1)}, u32[]{:S(2)}) copy-start(f32[10,16,128]{2,0,1:T(8,128)S(1)} %collective-permute-done.7) | copy-start | bytes 245764
  149.3 6.7 %collective-permute-start.8 = (f32[36,10,128]{2,0,1:T(8,128)S(1)}, f32[36,10,128]{2,0,1:T(8,128)S(1)}, u32[]{:S(2)}, u32[]{:S(2)}) collective-permute-start(f32[36,10,128]{2,0,1:T(8,128)S(1)} %get-tuple-element.142), channel_id=1, source_target_pairs={{0,2},{2,4},{4,6},{1,3},{3,5},{5,7},{8,10},{10,12},{12,14},{9,11},... | collective-permute-start | bytes 552968 | tf_op jit(solution)/shard_map/ppermute | solution.py:23
  152.8 7.7 %collective-permute-start.9 = (f32[36,10,128]{2,0,1:T(8,128)S(1)}, f32[36,10,128]{2,0,1:T(8,128)S(1)}, u32[]{:S(2)}, u32[]{:S(2)}) collective-permute-start(f32[36,10,128]{2,0,1:T(8,128)S(1)} %get-tuple-element.143), channel_id=1, source_target_pairs={{2,0},{4,2},{6,4},{3,1},{5,3},{7,5},{10,8},{12,10},{14,12},{11,9},... | collective-permute-start | bytes 552968 | tf_op jit(solution)/shard_map/ppermute | solution.py:24
  156.0 16.6 %copy-start.20 = (f32[36,10,128]{2,0,1:T(8,128)}, f32[36,10,128]{2,0,1:T(8,128)S(1)}, u32[]{:S(2)}) copy-start(f32[36,10,128]{2,0,1:T(8,128)S(1)} %collective-permute-done.8) | copy-start | bytes 552964
  160.4 12.2 %copy-start.22 = (f32[36,10,128]{2,0,1:T(8,128)}, f32[36,10,128]{2,0,1:T(8,128)S(1)}, u32[]{:S(2)}) copy-start(f32[36,10,128]{2,0,1:T(8,128)S(1)} %collective-permute-done.9) | copy-start | bytes 552964
  161.2 5.9 %collective-permute-start.10 = (f32[36,36,10]{1,0,2:T(8,128)S(1)}, f32[36,36,10]{1,0,2:T(8,128)S(1)}, u32[]{:S(2)}, u32[]{:S(2)}) collective-permute-start(f32[36,36,10]{1,0,2:T(8,128)S(1)} %copy.238), channel_id=1, source_target_pairs={{0,1},{2,3},{4,5},{6,7},{8,9},{10,11},{12,13},{14,15},{16,17},{18,... | collective-permute-start | bytes 155528 | tf_op jit(solution)/shard_map/ppermute | solution.py:23
  163.2 9.0 %collective-permute-start.11 = (f32[36,36,10]{1,0,2:T(8,128)S(1)}, f32[36,36,10]{1,0,2:T(8,128)S(1)}, u32[]{:S(2)}, u32[]{:S(2)}) collective-permute-start(f32[36,36,10]{1,0,2:T(8,128)S(1)} %copy.239), channel_id=1, source_target_pairs={{1,0},{3,2},{5,4},{7,6},{9,8},{11,10},{13,12},{15,14},{17,16},{19,... | collective-permute-start | bytes 155528 | tf_op jit(solution)/shard_map/ppermute | solution.py:24
  175.3 246.6 %collective-permute-start.12 = (f32[8,8,64]{2,1,0:T(8,128)}, f32[8,8,64]{2,1,0:T(8,128)}, u32[]{:S(2)}, u32[]{:S(2)}) collective-permute-start(f32[8,8,64]{2,1,0:T(8,128)} %fusion.112), channel_id=1, source_target_pairs={{0,8},{8,16},{16,24},{1,9},{9,17},{17,25},{2,10},{10,18},{18,26},{... | collective-permute-start | bytes 49160 | tf_op jit(solution)/shard_map/ppermute | solution.py:23
  178.5 243.4 %collective-permute-start.13 = (f32[8,8,64]{2,1,0:T(8,128)}, f32[8,8,64]{2,1,0:T(8,128)}, u32[]{:S(2)}, u32[]{:S(2)}) collective-permute-start(f32[8,8,64]{2,1,0:T(8,128)} %fusion.112), channel_id=1, source_target_pairs={{8,0},{16,8},{24,16},{9,1},{17,9},{25,17},{10,2},{18,10},{26,18},{... | collective-permute-start | bytes 49160 | tf_op jit(solution)/shard_map/ppermute | solution.py:24
  179.8 247.7 %copy-start.37 = (s32[2,2,16,128]{3,2,1,0:T(8,128)S(1)}, s32[2,2,16,128]{3,2,1,0:T(8,128)}, u32[]{:S(2)}) copy-start(s32[2,2,16,128]{3,2,1,0:T(8,128)} %param.9) | copy-start | bytes 98308
  262.1 38.0 %copy-start.26 = (f32[2,3,2,2,8,128]{5,4,3,2,1,0:T(8,128)S(1)}, f32[2,3,2,2,8,128]{5,4,3,2,1,0:T(8,128)}, u32[]{:S(2)}) copy-start(f32[2,3,2,2,8,128]{5,4,3,2,1,0:T(8,128)} %get-tuple-element.276) | copy-start | bytes 294916 | tf_op jit(solution)/shard_map/while
  383.1 38.0 %copy-start.26 = (f32[2,3,2,2,8,128]{5,4,3,2,1,0:T(8,128)S(1)}, f32[2,3,2,2,8,128]{5,4,3,2,1,0:T(8,128)}, u32[]{:S(2)}) copy-start(f32[2,3,2,2,8,128]{5,4,3,2,1,0:T(8,128)} %get-tuple-element.276) | copy-start | bytes 294916 | tf_op jit(solution)/shard_map/while
  421.9 15.9 %copy-start.24 = (f32[2,2,16,128]{3,1,2,0:T(2,128)S(1)}, f32[2,2,16,128]{3,1,2,0:T(2,128)}, u32[]{:S(2)}) copy-start(f32[2,2,16,128]{3,1,2,0:T(2,128)} %get-tuple-element.165) | copy-start | bytes 98308
  422.7 10.0 %collective-permute-start.14 = (f32[24,8,64]{2,1,0:T(8,128)S(1)}, f32[24,8,64]{2,1,0:T(8,128)S(1)}, u32[]{:S(2)}, u32[]{:S(2)}) collective-permute-start(f32[24,8,64]{2,1,0:T(8,128)S(1)} %pad_maximum_fusion.10), channel_id=1, source_target_pairs={{0,2},{2,4},{4,6},{1,3},{3,5},{5,7},{8,10},{10,12},{12,14},{9,11},... | collective-permute-start | bytes 147464 | tf_op jit(solution)/shard_map/ppermute | solution.py:23
  426.2 7.4 %collective-permute-start.15 = (f32[24,8,64]{2,1,0:T(8,128)S(1)}, f32[24,8,64]{2,1,0:T(8,128)S(1)}, u32[]{:S(2)}, u32[]{:S(2)}) collective-permute-start(f32[24,8,64]{2,1,0:T(8,128)S(1)} %pad_maximum_fusion.10), channel_id=1, source_target_pairs={{2,0},{4,2},{6,4},{3,1},{5,3},{7,5},{10,8},{12,10},{14,12},{11,9},... | collective-permute-start | bytes 147464 | tf_op jit(solution)/shard_map/ppermute | solution.py:24
  431.5 19.8 %copy-start.6 = (f32[16,16,128]{2,0,1:T(8,128)S(1)}, f32[16,16,128]{2,0,1:T(8,128)}, u32[]{:S(2)}) copy-start(f32[16,16,128]{2,0,1:T(8,128)} %copy-done.5) | copy-start | bytes 393220
  431.5 19.8 %copy-start.8 = (f32[36,36,10]{2,0,1:T(8,128)S(1)}, f32[36,36,10]{2,0,1:T(8,128)}, u32[]{:S(2)}) copy-start(f32[36,36,10]{2,0,1:T(8,128)} %copy-done.7) | copy-start | bytes 155524
  431.5 19.8 %copy-start.10 = (f32[36,36,10]{2,0,1:T(8,128)S(1)}, f32[36,36,10]{2,0,1:T(8,128)}, u32[]{:S(2)}) copy-start(f32[36,36,10]{2,0,1:T(8,128)} %copy-done.9) | copy-start | bytes 155524
  431.5 19.8 %copy-start.15 = (f32[10,16,128]{2,0,1:T(8,128)S(1)}, f32[10,16,128]{2,0,1:T(8,128)}, u32[]{:S(2)}) copy-start(f32[10,16,128]{2,0,1:T(8,128)} %copy-done.14) | copy-start | bytes 245764
  431.6 19.8 %copy-start.17 = (f32[10,16,128]{2,0,1:T(8,128)S(1)}, f32[10,16,128]{2,0,1:T(8,128)}, u32[]{:S(2)}) copy-start(f32[10,16,128]{2,0,1:T(8,128)} %copy-done.16) | copy-start | bytes 245764
  431.6 19.8 %copy-start.21 = (f32[36,10,128]{2,0,1:T(8,128)S(1)}, f32[36,10,128]{2,0,1:T(8,128)}, u32[]{:S(2)}) copy-start(f32[36,10,128]{2,0,1:T(8,128)} %copy-done.20) | copy-start | bytes 552964
  431.6 19.8 %copy-start.23 = (f32[36,10,128]{2,0,1:T(8,128)S(1)}, f32[36,10,128]{2,0,1:T(8,128)}, u32[]{:S(2)}) copy-start(f32[36,10,128]{2,0,1:T(8,128)} %copy-done.22) | copy-start | bytes 552964
  434.6 8.3 %collective-permute-start.16 = (f32[24,24,8]{2,1,0:T(8,128)S(1)}, f32[24,24,8]{2,1,0:T(8,128)S(1)}, u32[]{:S(2)}, u32[]{:S(2)}) collective-permute-start(f32[24,24,8]{2,1,0:T(8,128)S(1)} %get-tuple-element.144), channel_id=1, source_target_pairs={{0,1},{2,3},{4,5},{6,7},{8,9},{10,11},{12,13},{14,15},{16,17},{18,... | collective-permute-start | bytes 55304 | tf_op jit(solution)/shard_map/ppermute | solution.py:23
  436.4 10.5 %collective-permute-start.17 = (f32[24,24,8]{2,1,0:T(8,128)S(1)}, f32[24,24,8]{2,1,0:T(8,128)S(1)}, u32[]{:S(2)}, u32[]{:S(2)}) collective-permute-start(f32[24,24,8]{2,1,0:T(8,128)S(1)} %get-tuple-element.145), channel_id=1, source_target_pairs={{1,0},{3,2},{5,4},{7,6},{9,8},{11,10},{13,12},{15,14},{17,16},{19,... | collective-permute-start | bytes 55304 | tf_op jit(solution)/shard_map/ppermute | solution.py:24
  448.7 4.2 collective-permute-start.18
  450.0 4.3 collective-permute-start.19
  452.8 20.5 %copy-start.32 = (s32[12]{0:T(128)S(1)}, s32[12]{0:T(128)}, u32[]{:S(2)}) copy-start(s32[12]{0:T(128)} %add_multiply_fusion.4) | copy-start | bytes 148
  452.8 20.5 %copy-start.33 = (s32[20]{0:T(128)S(1)}, s32[20]{0:T(128)}, u32[]{:S(2)}) copy-start(s32[20]{0:T(128)} %iota_add_fusion.3) | copy-start | bytes 244
  452.8 21.4 %copy-start.30 = (f32[20,20]{1,0:T(8,128)S(1)}, f32[20,20]{1,0:T(8,128)}, u32[]{:S(2)}) copy-start(f32[20,20]{1,0:T(8,128)} %broadcast_multiply_fusion.4) | copy-start | bytes 4804
  452.8 21.4 %copy-start.34 = (s32[132]{0:T(256)S(1)}, s32[132]{0:T(256)}, u32[]{:S(2)}) copy-start(s32[132]{0:T(256)} %iota_add_fusion) | copy-start | bytes 1588
  452.8 21.4 %copy-start.35 = (f32[132]{0:T(256)S(1)}, f32[132]{0:T(256)}, u32[]{:S(2)}) copy-start(f32[132]{0:T(256)} %and_convert_fusion) | copy-start | bytes 1588
  452.9 21.4 %copy-start.36 = (s32[68]{0:T(128)S(1)}, s32[68]{0:T(128)}, u32[]{:S(2)}) copy-start(s32[68]{0:T(128)} %add_multiply_fusion.3) | copy-start | bytes 820
  454.3 6.6 %collective-permute-start.20 = (f32[12,2,64]{2,1,0:T(2,128)S(1)}, f32[12,2,64]{2,1,0:T(2,128)S(1)}, u32[]{:S(2)}, u32[]{:S(2)}) collective-permute-start(f32[12,2,64]{2,1,0:T(2,128)S(1)} %get-tuple-element.157), channel_id=1, source_target_pairs={{0,2},{2,4},{4,6},{1,3},{3,5},{5,7},{8,10},{10,12},{12,14},{9,11},... | collective-permute-start | bytes 18440 | tf_op jit(solution)/shard_map/ppermute | solution.py:23
  458.5 5.6 %collective-permute-start.21 = (f32[12,2,64]{2,1,0:T(2,128)S(1)}, f32[12,2,64]{2,1,0:T(2,128)S(1)}, u32[]{:S(2)}, u32[]{:S(2)}) collective-permute-start(f32[12,2,64]{2,1,0:T(2,128)S(1)} %get-tuple-element.158), channel_id=1, source_target_pairs={{2,0},{4,2},{6,4},{3,1},{5,3},{7,5},{10,8},{12,10},{14,12},{11,9},... | collective-permute-start | bytes 18440 | tf_op jit(solution)/shard_map/ppermute | solution.py:24
  464.3 4.5 collective-permute-start.22
  465.7 7.4 %collective-permute-start.23 = (f32[12,12,2]{2,1,0:T(8,128)S(1)}, f32[12,12,2]{2,1,0:T(8,128)S(1)}, u32[]{:S(2)}, u32[]{:S(2)}) collective-permute-start(f32[12,12,2]{2,1,0:T(8,128)S(1)} %get-tuple-element.154), channel_id=1, source_target_pairs={{1,0},{3,2},{5,4},{7,6},{9,8},{11,10},{13,12},{15,14},{17,16},{19,... | collective-permute-start | bytes 3464 | tf_op jit(solution)/shard_map/ppermute | solution.py:24
  509.7 10.1 %copy-start.25 = (f32[2,2,16,128]{3,2,1,0:T(8,128)S(1)}, f32[2,2,16,128]{3,2,1,0:T(8,128)}, u32[]{:S(2)}) copy-start(f32[2,2,16,128]{3,2,1,0:T(8,128)} %copy.221) | copy-start | bytes 98308
  (16 other events, 72.5 us)
where the time goes:
time: 528 us; the launch traced here: 521 us
  other arithmetic  273 us (52%)
  local copies, waits for them, and re-layouts  83.5 us (16%)
  matrix products  64.2 us (12%)
  starting transfers between devices  48.6 us (9%)
  waiting for transfers between devices  44.1 us (8%)
    reduce_sum x2, other arithmetic, pair_sum(): distance_sq = jnp.sum(separation * separation, axis=0)  82.6 us
    reduce_sum x2, other arithmetic, pair_sum(): return own_charge * jnp.sum(separation * strength, axis=-1)  76.1 us
    mul x2, other arithmetic, pair_sum(): reach_left * reach_left * reach_left / (distance_sq + soften_sq)  73.4 us
    ppermute x12, waiting for transfers between devices, padded_2(): after = lax.ppermute(initial, axis, down)  34.6 us
    ppermute x12, starting transfers between devices, padded_2(): before = lax.ppermute(last, axis, up)  32.5 us
    dot_general x1, matrix products, charge_patches(): jnp.einsum('...sp,...sc->...pc', flattened, weight_z, precision=highest)  30.1 us
    ppermute x12, starting transfers between devices, padded_2(): after = lax.ppermute(initial, axis, down)  16.1 us
    unnamed x80, local copies, waits for them, and re-layouts  15.6 us
  transfers between devices with their start and end apart: 24, of which 15 were waited for; matrix products, arithmetic and copies ran while one was open for 50% of the time, Pallas kernels for 0%

commit v1 on v0

--- a/solution.py
+++ b/solution.py
@@ -1,11 +1,11 @@
 import jax
 import jax.numpy as jnp
 from jax import lax
+from jax.experimental import pallas as pl
+from jax.experimental.pallas import tpu as pltpu
 from jax.sharding import PartitionSpec as P
 
 highest = lax.Precision.HIGHEST
-cutoff_sq = 64.0
-soften_sq = 1.0
 bond_spring = 0.1
 fine_scale = 4.0
 coarse_scale = 2.0
@@ -117,26 +117,74 @@
         cell_index = jnp.arange(cell_count).astype(jnp.float32) + first_cell
         broadcast_shape = [1, 1, 1, 1]
         broadcast_shape[dimension] = cell_count
-        coordinates.append((cell_index.reshape(broadcast_shape) + offsets[dimension]) * 8.0)
+        coordinates.append((cell_index.reshape(broadcast_shape) + offsets[dimension]))
     return jnp.stack(coordinates)
 
 
-def pair_sum(own_pos, own_charge, near_pos, near_charge):
-    separation = own_pos[..., :, None] - near_pos[..., None, :]
-    distance_sq = jnp.sum(separation * separation, axis=0)
-    reach_left = jnp.maximum(1.0 - distance_sq / cutoff_sq, 0.0)
-    strength = (
-        reach_left * reach_left * reach_left / (distance_sq + soften_sq) * near_charge[..., None, :]
-    )
-    return own_charge * jnp.sum(separation * strength, axis=-1)
-
-
-def bond_force(positions, in_use, partners):
-    slot_ids = jnp.arange(positions.shape[-1])
-    picker = (partners[..., :, None] == slot_ids).astype(jnp.float32)
-    partner_pos = jnp.einsum("...sp,d...p->d...s", picker, positions, precision=highest)
-    partner_use = jnp.einsum("...sp,...p->...s", picker, in_use, precision=highest)
-    return -bond_spring * (positions - partner_pos) * (in_use * partner_use)
+def short_kernel(counts_ref, grown_ref, partners_ref, out_ref, own_s, acc_s):
+    _, cells_x, cells_y, cells_z, slots = out_ref.shape
+    lane = lax.broadcasted_iota(jnp.int32, (1, slots), 1)
+
+    def cell_body(cell, carry):
+        i = cell // (cells_y * cells_z)
+        j = (cell // cells_z) % cells_y
+        k = cell % cells_z
+        count = counts_ref[cell]
+        own_rows = [grown_ref[d, i + 1, j + 1, pl.ds(k + 1, 1), :] for d in range(3)]
+        for d in range(3):
+            own_s[d] = jnp.broadcast_to(own_rows[d], (slots, slots)).T
+
+        def block_body(block, carry):
+            row = pl.multiple_of(block * 8, 8)
+            own = [own_s[d, pl.ds(row, 8), :] for d in range(3)]
+            total = [jnp.zeros((8, slots), jnp.float32) for _ in range(3)]
+            for step_x in range(3):
+                for step_y in range(3):
+                    for step_z in range(3):
+                        near = [
+                            grown_ref[d, i + step_x, j + step_y, pl.ds(k + step_z, 1), :]
+                            for d in range(4)
+                        ]
+                        gap = [own[d] - near[d] for d in range(3)]
+                        distance_sq = gap[0] * gap[0] + gap[1] * gap[1] + gap[2] * gap[2]
+                        reach = jnp.maximum(1.0 - distance_sq, 0.0)
+                        below = 1.015625 - reach
+                        inverse = pl.reciprocal(below, approx=True)
+                        inverse = inverse * (2.0 - below * inverse)
+                        strength = (reach * reach) * (reach * near[3]) * inverse
+                        total = [total[d] + strength * gap[d] for d in range(3)]
+            for d in range(3):
+                acc_s[d, pl.ds(row, 8), :] = total[d]
+            return carry
+
+        lax.fori_loop(0, (count + 7) // 8, block_body, 0)
+        charge = grown_ref[3, i + 1, j + 1, pl.ds(k + 1, 1), :]
+        partner = partners_ref[i, j, pl.ds(k, 1), :]
+        bonded = (lane < count) & (partner < count)
+        index = jnp.broadcast_to(partner, (8, slots))
+        for d in range(3):
+            pair = 0.125 * charge * jnp.sum(acc_s[d].T, axis=0, keepdims=True)
+            source = jnp.broadcast_to(own_rows[d], (8, slots))
+            other = jnp.take_along_axis(source, index, axis=1)[0:1]
+            bond = jnp.where(bonded, (-8.0 * bond_spring) * (own_rows[d] - other), 0.0)
+            out_ref[d, i, j, pl.ds(k, 1), :] = jnp.where(lane < count, pair, 0.0) + bond
+        return carry
+
+    lax.fori_loop(0, cells_x * cells_y * cells_z, cell_body, 0)
+
+
+def short_forces(counts, grown, partners):
+    cells, slots = counts.shape, partners.shape[-1]
+    return pl.pallas_call(
+        short_kernel,
+        out_shape=jax.ShapeDtypeStruct((3,) + cells + (slots,), jnp.float32),
+        in_specs=[pl.BlockSpec(memory_space=pltpu.SMEM)]
+        + [pl.BlockSpec(memory_space=pltpu.VMEM)] * 2,
+        out_specs=pl.BlockSpec(memory_space=pltpu.VMEM),
+        scratch_shapes=[pltpu.VMEM((3, slots, slots), jnp.float32)] * 2,
+        compiler_params=pltpu.CompilerParams(vmem_limit_bytes=24 * 2**20),
+        cost_estimate=pl.CostEstimate(flops=10**9, bytes_accessed=10**7, transcendentals=10**7),
+    )(counts.reshape(-1), grown, partners)
 
 
 def grid_force(patches, weighted, offsets):
@@ -168,48 +216,9 @@
     grown_tiles = padded_2(packed, (("gx", 1), ("gy", 2), ("ga", 3)), 1)
     grown_offsets = grown_tiles[:3]
     grown_charge = grown_tiles[3]
-    grown_pos = cell_positions(grown_offsets, -1.0)
-    positions = grown_pos[:, 1 : cells_x + 1, 1 : cells_y + 1, 1 : cells_z + 1]
-    block_cells = 8
-
-    def pair_block(start):
-        pos_part = lax.dynamic_slice_in_dim(grown_pos, start, block_cells + 2, axis=3)
-        charge_part = lax.dynamic_slice_in_dim(grown_charge, start, block_cells + 2, axis=2)
-        own_pos = pos_part[:, 1 : cells_x + 1, 1 : cells_y + 1, 1 : block_cells + 1]
-        own_charge = charge_part[1 : cells_x + 1, 1 : cells_y + 1, 1 : block_cells + 1]
-        near_pos = jnp.concatenate(
-            [
-                pos_part[
-                    :,
-                    step_x : step_x + cells_x,
-                    step_y : step_y + cells_y,
-                    step_z : step_z + block_cells,
-                ]
-                for step_x in range(3)
-                for step_y in range(3)
-                for step_z in range(3)
-            ],
-            axis=-1,
-        )
-        near_charge = jnp.concatenate(
-            [
-                charge_part[
-                    step_x : step_x + cells_x,
-                    step_y : step_y + cells_y,
-                    step_z : step_z + block_cells,
-                ]
-                for step_x in range(3)
-                for step_y in range(3)
-                for step_z in range(3)
-            ],
-            axis=-1,
-        )
-        return pair_sum(own_pos, own_charge, near_pos, near_charge)
-
-    starts = jnp.arange(cells_z // block_cells) * block_cells
-    block_forces = lax.map(pair_block, starts)
-    pair_part = jnp.moveaxis(block_forces, 0, 3).reshape(positions.shape)
-    short_force = pair_part + bond_force(positions, in_use, partners)
+    cell_units = cell_positions(grown_offsets, -1.0)
+    grown = jnp.concatenate([cell_units, grown_charge[None]], axis=0)
+    short_force = short_forces(counts, grown, partners)
     patches = charge_patches(grown_charge, grown_offsets)
     spread_grid = jnp.transpose(patches, (0, 3, 1, 4, 2, 5))
     for where_axis in range(3):

time: 528 us -> 362 us (0.69)
  other arithmetic: 273 us -> 40.9 us
  Pallas kernels: 0 us -> 78.7 us
  starting transfers between devices: 48.6 us -> 60.3 us
  local copies, waits for them, and re-layouts: 83.5 us -> 73.6 us
  matrix products: 64.2 us -> 57.6 us
    reduce_sum x4 -> x0, other arithmetic: 159 us -> none  [the longest x2 82.6 us: pair_sum(): distance_sq = jnp.sum(separation * separation, axis=0)]
    pallas_call x0 -> x1, Pallas kernels: none -> 78.7 us  [short_forces(): pl.pallas_call(short_kernel, out_shape=jax.ShapeDtypeStruct((3,) + cells...]
    mul x3 -> x0, other arithmetic: 73.4 us -> none  [the longest x2 73.4 us: pair_sum(): reach_left * reach_left * reach_left / (distance_sq + soften_sq)]
    ppermute x12, starting transfers between devices: 32.5 us -> 44.5 us  [padded_2(): before = lax.ppermute(last, axis, up)]
    dot_general x2 -> x0, matrix products: 6.77 us -> none  [the longest x1 4 us: bond_force(): jnp.einsum('...sp,d...p->d...s', picker, positions, precision=highest)]
    unnamed x80 -> x45, local copies, waits for them, and re-layouts: 15.6 us -> 13.1 us
  transfers between devices with their start and end apart: 24 -> 24, of which waited for: 15 -> 15; matrix products, arithmetic and copies ran while one was open for 50% -> 5% of each run, Pallas kernels for 0% -> 22%
where the time goes in v1:
time: 362 us; the launch traced here: 355 us
  Pallas kernels  78.7 us (22%)
  local copies, waits for them, and re-layouts  73.6 us (20%)
  starting transfers between devices  60.3 us (17%)
  matrix products  57.6 us (16%)
  waiting for transfers between devices  42.2 us (12%)
  other arithmetic  40.9 us (11%)
    pallas_call x1, Pallas kernels, short_forces(): pl.pallas_call(short_kernel, out_shape=jax.ShapeDtypeStruct((3,) + cells...  78.7 us
    ppermute x12, starting transfers between devices, padded_2(): before = lax.ppermute(last, axis, up)  44.5 us
    ppermute x12, waiting for transfers between devices, padded_2(): after = lax.ppermute(initial, axis, down)  36.1 us
    dot_general x1, matrix products, charge_patches(): jnp.einsum('...sp,...sc->...pc', flattened, weight_z, precision=highest)  30.1 us
    ppermute x12, starting transfers between devices, padded_2(): after = lax.ppermute(initial, axis, down)  15.8 us
    dot_general x1, local copies, waits for them, and re-layouts, charge_patches(): jnp.einsum('...sp,...sc->...pc', flattened, weight_z, precision=highest)  13.9 us
    unnamed x45, local copies, waits for them, and re-layouts  13.1 us
    add x2, other arithmetic, assemble(): merged = jnp.pad(inner_part, inner_pad) + jnp.pad(overflow, over_pad)  12.1 us
  transfers between devices with their start and end apart: 24, of which 15 were waited for; matrix products, arithmetic and copies ran while one was open for 5% of the time, Pallas kernels for 22%

profile of v1, /device:TPU:0, one launch (start us, length us, event | category | flops | bytes accessed | tf_op | source)
XLA Modules:
  0.0 355.4 jit_solution(8947485217277160226)
XLA Ops:
  2.9 2.4 collective-permute-start
  10.2 4.7 %broadcast_multiply_fusion.1 = (f32[2,2,16,128,11,11]{3,2,5,4,1,0:T(8,128)}, f32[2,2,16,128,11,11]{3,2,5,4,1,0:T(8,128)}, f32[2,2,16,128,11,11]{3,2,5,4,1,0:T(8,128)}) fusion(f32[2,2,16,128,11]{3,2,4,1,0:T(8,128)S(1)} %copy.108, f32[2,2,16,128,11]{3,2,4,1,0:T(8,128)S(1)} %copy.107, f32[2,2,16,128,11]{3,2,4,1,0:T(8,128)S(1)} %copy.81, ...), kind=kLoop, calls=%fused_computation.39 | loop fusion | flops 2973696 | bytes 13336576 | tf_op jit(solution)/shard_map/mul | solution.py:200
  15.6 4.3 %collective-permute-start.2 = (f32[4,4,1,16,128]{4,3,2,1,0:T(8,128)S(1)}, f32[4,4,1,16,128]{4,3,2,1,0:T(8,128)S(1)}, u32[]{:S(2)}, u32[]{:S(2)}) collective-permute-start(f32[4,4,1,16,128]{4,3,2,1,0:T(8,128)S(1)} %get-tuple-element.29), channel_id=1, source_target_pairs={{0,2},{2,4},{4,6},{1,3},{3,5},{5,7},{8,10},{10,12},{12,14},{9,11},... | collective-permute-start | bytes 393224 | tf_op jit(solution)/shard_map/ppermute | solution.py:23
  22.4 4.6 %collective-permute-done.3 = f32[4,4,1,16,128]{4,3,2,1,0:T(8,128)S(1)} collective-permute-done((f32[4,4,1,16,128]{4,3,2,1,0:T(8,128)S(1)}, f32[4,4,1,16,128]{4,3,2,1,0:T(8,128)S(1)}, u32[]{:S(2)}, u32[]{:S(2)}) %collective-permute-start.3) | collective-permute-done | bytes 131104 | tf_op jit(solution)/shard_map/ppermute | solution.py:24
  27.0 3.4 collective-permute-start.4
  32.2 4.1 %collective-permute-done.5 = f32[4,4,4,1,128]{4,3,2,1,0:T(1,128)S(1)} collective-permute-done((f32[4,4,4,1,128]{4,3,2,1,0:T(1,128)S(1)}, f32[4,4,4,1,128]{4,3,2,1,0:T(1,128)S(1)}, u32[]{:S(2)}, u32[]{:S(2)}) %collective-permute-start.5) | collective-permute-done | bytes 32800 | tf_op jit(solution)/shard_map/ppermute | solution.py:24
  37.4 1.7 fusion.16
  41.1 3.6 %broadcast_multiply_fusion = f32[4,4,18,128,11,11]{3,1,5,4,2,0:T(4,128)S(1)} fusion(f32[4,4,18,128,11]{3,1,4,2,0:T(4,128)S(1)} %copy.83, f32[4,4,18,128,11]{3,1,4,2,0:T(4,128)S(1)} %copy.82), kind=kLoop, calls=%fused_computation.5 | loop fusion | flops 4460544 | bytes 21086208 | tf_op jit(solution)/shard_map/mul | solution.py:51
  44.7 30.1 %fusion = f32[4,4,18,121,11]{3,4,2,1,0:T(8,128)S(1)} fusion(f32[4,4,18,128,121]{3,1,4,2,0:T(4,128)S(1)} %bitcast.90, f32[4,4,18,128]{3,2,1,0:T(8,128)S(1)} %get-tuple-element.8, f32[11]{0:T(128)S(1)} %iota_convert_fusion), kind=kOutput, calls=%fused_computation | convolution fusion | flops 592846848 | bytes 19522988 | tf_op jit(solution)/shard_map/...sp,...sc->...pc/dot_general | solution.py:53
  74.8 13.9 %copy.85 = f32[4,4,18,121,11]{2,1,4,3,0:T(4,128)} copy(f32[4,4,18,121,11]{3,4,2,1,0:T(8,128)S(1)} %fusion) | data formatting | bytes 3066624 | tf_op jit(solution)/shard_map/...sp,...sc->...pc/dot_general | solution.py:53
  88.6 7.8 %slice.189 = f32[4,8,4,11,18,11]{4,2,5,3,1,0:T(4,128)} slice(f32[4,11,4,11,18,11]{4,2,5,3,1,0:T(4,128)} %bitcast.91), slice={[0:4], [0:8], [0:4], [0:11], [0:18], [0:11]} | slice | bytes 2230272 | tf_op jit(solution)/shard_map/slice | solution.py:59
  96.4 2.4 slice.190
  98.8 9.5 %pad_add_fusion = f32[5,8,4,11,18,11]{4,2,5,3,1,0:T(4,128)} fusion(f32[4,3,4,11,18,11]{4,2,5,3,1,0:T(4,128)S(1)} %slice.190, f32[4,8,4,11,18,11]{4,2,5,3,1,0:T(4,128)} %slice.189), kind=kLoop, calls=%fused_computation.3 | loop fusion | flops 348480 | bytes 2927232 | tf_op jit(solution)/shard_map/add | solution.py:66
  108.3 4.5 %copy.141 = f32[5,8,4,11,18,11]{4,1,0,5,3,2:T(8,128)S(1)} copy(f32[5,8,4,11,18,11]{4,2,5,3,1,0:T(4,128)} %pad_add_fusion) | data formatting | bytes 2787840 | tf_op jit(solution)/shard_map/add | solution.py:66
  113.2 1.7 slice.192
  114.9 2.6 pad_add_fusion.1
  117.5 3.6 %slice.193 = f32[40,40,18,8]{2,0,3,1:T(8,128)} slice(f32[40,40,18,11]{2,0,3,1:T(8,128)S(1)} %bitcast.95), slice={[0:40], [0:40], [0:18], [0:8]} | slice | bytes 1843200 | tf_op jit(solution)/shard_map/slice | solution.py:59
  121.1 1.7 slice.194
  122.8 6.2 %copy.112 = f32[40,40,18,8]{1,3,2,0:T(8,128)S(1)} copy(f32[40,40,18,8]{2,0,3,1:T(8,128)} %slice.193) | data formatting | bytes 1843200
  129.0 4.3 %copy.113 = f32[40,40,18,3]{1,3,2,0:T(4,128)} copy(f32[40,40,18,3]{2,0,3,1:T(8,128)} %slice.194) | data formatting | bytes 691200
  133.3 1.8 add_bitcast_fusion
  135.1 1.6 copy-done.2
  137.4 1.8 collective-permute-start.6
  142.7 3.5 collective-permute-done.7
  146.3 3.5 collective-permute-start.8
  151.4 1.7 collective-permute-done.8
  153.0 4.4 %collective-permute-done.9 = f32[36,10,128]{2,0,1:T(8,128)S(1)} collective-permute-done((f32[36,10,128]{2,0,1:T(8,128)S(1)}, f32[36,10,128]{2,0,1:T(8,128)S(1)}, u32[]{:S(2)}, u32[]{:S(2)}) %collective-permute-start.9) | collective-permute-done | bytes 184352 | tf_op jit(solution)/shard_map/ppermute | solution.py:24
  158.2 1.6 collective-permute-start.10
  161.5 2.6 collective-permute-done.10
  164.5 4.7 %collective-permute-done.11 = f32[36,36,10]{1,0,2:T(8,128)S(1)} collective-permute-done((f32[36,36,10]{1,0,2:T(8,128)S(1)}, f32[36,36,10]{1,0,2:T(8,128)S(1)}, u32[]{:S(2)}, u32[]{:S(2)}) %collective-permute-start.11) | collective-permute-done | bytes 51872 | tf_op jit(solution)/shard_map/ppermute | solution.py:24
  169.7 2.3 fusion.161
  172.7 2.6 collective-permute-start.12
  177.1 2.1 collective-permute-done.13
  179.3 3.5 collective-permute-start.14
  185.0 4.3 %collective-permute-done.15 = f32[24,8,64]{2,1,0:T(8,128)S(1)} collective-permute-done((f32[24,8,64]{2,1,0:T(8,128)S(1)}, f32[24,8,64]{2,1,0:T(8,128)S(1)}, u32[]{:S(2)}, u32[]{:S(2)}) %collective-permute-start.15) | collective-permute-done | bytes 49184 | tf_op jit(solution)/shard_map/ppermute | solution.py:24
  192.4 78.7 %shard_map.59 = f32[3,2,2,16,128]{4,3,2,1,0:T(8,128)} custom-call(s32[64]{0:T(128)S(1)} %reshape.315.counts_ref, f32[4,4,4,18,128]{4,3,2,1,0:T(8,128)S(1)} %pad_maximum_fusion.3.grown_ref, s32[2,2,16,128]{3,2,1,0:T(8,128)S(1)} %copy-done), custom_call_target="tpu_custom_call" | custom-call | flops 1000000000 | bytes 10000000 | tf_op jit(solution)/shard_map/pallas_call | solution.py:178
  272.0 7.9 %collective-permute-start.18 = (f32[2,8,64]{2,1,0:T(8,128)S(1)}, f32[2,8,64]{2,1,0:T(8,128)S(1)}, u32[]{:S(2)}, u32[]{:S(2)}) collective-permute-start(f32[2,8,64]{2,1,0:T(8,128)S(1)} %get-tuple-element.46), channel_id=1, source_target_pairs={{0,8},{8,16},{16,24},{1,9},{9,17},{17,25},{2,10},{10,18},{18,26},{... | collective-permute-start | bytes 12296 | tf_op jit(solution)/shard_map/ppermute | solution.py:23
  283.0 5.6 %collective-permute-start.20 = (f32[12,2,64]{2,1,0:T(2,128)S(1)}, f32[12,2,64]{2,1,0:T(2,128)S(1)}, u32[]{:S(2)}, u32[]{:S(2)}) collective-permute-start(f32[12,2,64]{2,1,0:T(2,128)S(1)} %get-tuple-element.38), channel_id=1, source_target_pairs={{0,2},{2,4},{4,6},{1,3},{3,5},{5,7},{8,10},{10,12},{12,14},{9,11},... | collective-permute-start | bytes 18440 | tf_op jit(solution)/shard_map/ppermute | solution.py:23
  290.8 3.5 collective-permute-done.21
  294.4 6.5 %collective-permute-start.22 = (f32[12,12,2]{2,1,0:T(8,128)S(1)}, f32[12,12,2]{2,1,0:T(8,128)S(1)}, u32[]{:S(2)}, u32[]{:S(2)}) collective-permute-start(f32[12,12,2]{2,1,0:T(8,128)S(1)} %get-tuple-element.36), channel_id=1, source_target_pairs={{0,1},{2,3},{4,5},{6,7},{8,9},{10,11},{12,13},{14,15},{16,17},{18,... | collective-permute-start | bytes 3464 | tf_op jit(solution)/shard_map/ppermute | solution.py:23
  303.7 4.7 %collective-permute-done.23 = f32[12,12,2]{2,1,0:T(8,128)S(1)} collective-permute-done((f32[12,12,2]{2,1,0:T(8,128)S(1)}, f32[12,12,2]{2,1,0:T(8,128)S(1)}, u32[]{:S(2)}, u32[]{:S(2)}) %collective-permute-start.23) | collective-permute-done | bytes 1184 | tf_op jit(solution)/shard_map/ppermute | solution.py:24
  310.7 3.9 %reshape.324 = f32[2,11,2,11,16,8]{5,4,2,3,1,0:T(8,128)} reshape(f32[2,11,2,11,128]{4,2,3,1,0:T(2,128)S(1)} %copy.102) | data formatting | bytes 495616 | tf_op jit(solution)/shard_map/reshape | solution.py:74
  314.9 3.6 %reshape.325 = f32[2,11,2,11,16,8]{5,4,2,3,1,0:T(8,128)} reshape(f32[2,11,2,11,128]{4,2,3,1,0:T(2,128)S(1)} %copy.103) | data formatting | bytes 495616 | tf_op jit(solution)/shard_map/reshape | solution.py:80
  318.5 6.3 %maximum_bitcast_fusion = f32[2,2,16,11,11,11]{5,2,1,4,3,0:T(8,128)} fusion(f32[2,11,2,11,16,3]{5,4,2,3,1,0:T(8,128)} %bitcast.100, f32[2,11,2,11,16,8]{5,4,2,3,1,0:T(8,128)} %reshape.324), kind=kLoop, calls=%fused_computation.12 | loop fusion | flops 85184 | bytes 681472 | tf_op jit(solution)/shard_map/transpose | solution.py:255
  324.8 7.2 %copy.104 = f32[2,2,16,11,11,11]{2,1,5,4,3,0:T(2,128)S(1)} copy(f32[2,2,16,11,11,11]{5,2,1,4,3,0:T(8,128)} %maximum_bitcast_fusion) | data formatting | bytes 681472 | tf_op jit(solution)/shard_map/transpose | solution.py:255
  332.0 2.6 copy.105
  334.6 9.6 %fusion.2 = f32[2,2,16,128]{3,2,1,0:T(8,128)S(1)} fusion(f32[2,2,16,128,121]{3,2,4,1,0:T(8,128)} %bitcast.99, f32[2,2,16,121,11]{3,4,2,1,0:T(8,128)S(1)} %copy.105, f32[2,2,16,128]{3,2,1,0:T(8,128)S(1)} %get-tuple-element.33, f32[11]{0:T(128)S(1)} %iota_convert_fusion), kind=kOutput, calls=%fused_computation.7 | convolution fusion | flops 133718016 | bytes 4371244 | tf_op jit(solution)/shard_map/...pc,...sc->...sp/dot_general | solution.py:196
  344.2 10.1 %fusion.4 = (f32[2,2,16,128]{3,2,1,0:T(8,128)S(1)}, f32[2,2,16,128]{3,2,1,0:T(8,128)S(1)}) fusion(f32[2,2,16,128,121]{3,2,4,1,0:T(8,128)} %bitcast.98, f32[2,2,16,128,121]{3,2,4,1,0:T(8,128)S(1)} %bitcast.97, f32[2,2,16,121,11]{3,4,2,1,0:T(8,128)S(1)} %copy.105, f32[2,2,16,128]{3,2,1,0:T(8,128)S(1)} %get-tuple-element.33, f32[11]{0:T(128)S(1)} %iota_convert_fusion), kind=kOutput, calls=%fused_computation.11 | convolution fusion | flops 135692288 | bytes 8368940 | tf_op jit(solution)/shard_map/...pc,...sc->...sp/dot_general | solution.py:195
  (142 shorter events, 44.7 us)
Async XLA Ops:
  2.9 12.6 %collective-permute-start = (f32[4,1,2,16,128]{4,3,2,1,0:T(8,128)S(1)}, f32[4,1,2,16,128]{4,3,2,1,0:T(8,128)S(1)}, u32[]{:S(2)}, u32[]{:S(2)}) collective-permute-start(f32[4,1,2,16,128]{4,3,2,1,0:T(8,128)S(1)} %get-tuple-element.31), channel_id=1, source_target_pairs={{0,8},{8,16},{16,24},{1,9},{9,17},{17,25},{2,10},{10,18},{18,26},{... | collective-permute-start | bytes 196616 | tf_op jit(solution)/shard_map/ppermute | solution.py:23
  5.3 10.2 %collective-permute-start.1 = (f32[4,1,2,16,128]{4,3,2,1,0:T(8,128)S(1)}, f32[4,1,2,16,128]{4,3,2,1,0:T(8,128)S(1)}, u32[]{:S(2)}, u32[]{:S(2)}) collective-permute-start(f32[4,1,2,16,128]{4,3,2,1,0:T(8,128)S(1)} %get-tuple-element.32), channel_id=1, source_target_pairs={{8,0},{16,8},{24,16},{9,1},{17,9},{25,17},{10,2},{18,10},{26,18},{... | collective-permute-start | bytes 196616 | tf_op jit(solution)/shard_map/ppermute | solution.py:24
  10.2 5.3 %copy-start.3 = (f32[3,2,2,16,128]{4,3,2,1,0:T(8,128)S(1)}, f32[3,2,2,16,128]{4,3,2,1,0:T(8,128)}, u32[]{:S(2)}) copy-start(f32[3,2,2,16,128]{4,3,2,1,0:T(8,128)} %param.4) | copy-start | bytes 294916
  15.6 6.8 %collective-permute-start.2 = (f32[4,4,1,16,128]{4,3,2,1,0:T(8,128)S(1)}, f32[4,4,1,16,128]{4,3,2,1,0:T(8,128)S(1)}, u32[]{:S(2)}, u32[]{:S(2)}) collective-permute-start(f32[4,4,1,16,128]{4,3,2,1,0:T(8,128)S(1)} %get-tuple-element.29), channel_id=1, source_target_pairs={{0,2},{2,4},{4,6},{1,3},{3,5},{5,7},{8,10},{10,12},{12,14},{9,11},... | collective-permute-start | bytes 393224 | tf_op jit(solution)/shard_map/ppermute | solution.py:23
  19.9 7.1 %collective-permute-start.3 = (f32[4,4,1,16,128]{4,3,2,1,0:T(8,128)S(1)}, f32[4,4,1,16,128]{4,3,2,1,0:T(8,128)S(1)}, u32[]{:S(2)}, u32[]{:S(2)}) collective-permute-start(f32[4,4,1,16,128]{4,3,2,1,0:T(8,128)S(1)} %get-tuple-element.30), channel_id=1, source_target_pairs={{2,0},{4,2},{6,4},{3,1},{5,3},{7,5},{10,8},{12,10},{14,12},{11,9},... | collective-permute-start | bytes 393224 | tf_op jit(solution)/shard_map/ppermute | solution.py:24
  27.0 5.2 %collective-permute-start.4 = (f32[4,4,4,1,128]{4,3,2,1,0:T(1,128)S(1)}, f32[4,4,4,1,128]{4,3,2,1,0:T(1,128)S(1)}, u32[]{:S(2)}, u32[]{:S(2)}) collective-permute-start(f32[4,4,4,1,128]{4,3,2,1,0:T(1,128)S(1)} %get-tuple-element.18), channel_id=1, source_target_pairs={{0,1},{2,3},{4,5},{6,7},{8,9},{10,11},{12,13},{14,15},{16,17},{18,... | collective-permute-start | bytes 98312 | tf_op jit(solution)/shard_map/ppermute | solution.py:23
  30.4 5.9 %collective-permute-start.5 = (f32[4,4,4,1,128]{4,3,2,1,0:T(1,128)S(1)}, f32[4,4,4,1,128]{4,3,2,1,0:T(1,128)S(1)}, u32[]{:S(2)}, u32[]{:S(2)}) collective-permute-start(f32[4,4,4,1,128]{4,3,2,1,0:T(1,128)S(1)} %get-tuple-element.19), channel_id=1, source_target_pairs={{1,0},{3,2},{5,4},{7,6},{9,8},{11,10},{13,12},{15,14},{17,16},{19,... | collective-permute-start | bytes 98312 | tf_op jit(solution)/shard_map/ppermute | solution.py:24
  135.1 1.6 copy-start.2
  137.4 5.3 %collective-permute-start.6 = (f32[10,16,128]{2,0,1:T(8,128)S(1)}, f32[10,16,128]{2,0,1:T(8,128)S(1)}, u32[]{:S(2)}, u32[]{:S(2)}) collective-permute-start(f32[10,16,128]{2,0,1:T(8,128)S(1)} %copy.114), channel_id=1, source_target_pairs={{0,8},{8,16},{16,24},{1,9},{9,17},{17,25},{2,10},{10,18},{18,26},{... | collective-permute-start | bytes 245768 | tf_op jit(solution)/shard_map/ppermute | solution.py:23
  139.5 6.7 %collective-permute-start.7 = (f32[10,16,128]{2,0,1:T(8,128)S(1)}, f32[10,16,128]{2,0,1:T(8,128)S(1)}, u32[]{:S(2)}, u32[]{:S(2)}) collective-permute-start(f32[10,16,128]{2,0,1:T(8,128)S(1)} %copy.116), channel_id=1, source_target_pairs={{8,0},{16,8},{24,16},{9,1},{17,9},{25,17},{10,2},{18,10},{26,18},{... | collective-permute-start | bytes 245768 | tf_op jit(solution)/shard_map/ppermute | solution.py:24
  140.8 10.5 %copy-start.12 = (f32[20]{0:T(128)S(1)}, f32[20]{0:T(128)}, u32[]{:S(2)}) copy-start(f32[20]{0:T(128)} %get-tuple-element.53) | copy-start | bytes 244
  146.3 6.7 %collective-permute-start.8 = (f32[36,10,128]{2,0,1:T(8,128)S(1)}, f32[36,10,128]{2,0,1:T(8,128)S(1)}, u32[]{:S(2)}, u32[]{:S(2)}) collective-permute-start(f32[36,10,128]{2,0,1:T(8,128)S(1)} %get-tuple-element.25), channel_id=1, source_target_pairs={{0,2},{2,4},{4,6},{1,3},{3,5},{5,7},{8,10},{10,12},{12,14},{9,11},... | collective-permute-start | bytes 552968 | tf_op jit(solution)/shard_map/ppermute | solution.py:23
  149.8 7.7 %collective-permute-start.9 = (f32[36,10,128]{2,0,1:T(8,128)S(1)}, f32[36,10,128]{2,0,1:T(8,128)S(1)}, u32[]{:S(2)}, u32[]{:S(2)}) collective-permute-start(f32[36,10,128]{2,0,1:T(8,128)S(1)} %get-tuple-element.26), channel_id=1, source_target_pairs={{2,0},{4,2},{6,4},{3,1},{5,3},{7,5},{10,8},{12,10},{14,12},{11,9},... | collective-permute-start | bytes 552968 | tf_op jit(solution)/shard_map/ppermute | solution.py:24
  153.0 5.1 %copy-start.6 = (f32[36,10,128]{2,0,1:T(8,128)}, f32[36,10,128]{2,0,1:T(8,128)S(1)}, u32[]{:S(2)}) copy-start(f32[36,10,128]{2,0,1:T(8,128)S(1)} %collective-permute-done.8) | copy-start | bytes 552964
  157.4 0.7 copy-start.8
  157.8 11.9 %copy-start.15 = (s32[36]{0:T(128)S(1)}, s32[36]{0:T(128)}, u32[]{:S(2)}) copy-start(s32[36]{0:T(128)} %iota_add_fusion.2) | copy-start | bytes 436
  157.8 11.9 %copy-start.16 = (s32[8]{0:T(128)S(1)}, s32[8]{0:T(128)}, u32[]{:S(2)}) copy-start(s32[8]{0:T(128)} %iota_multiply_fusion.1) | copy-start | bytes 100
  158.2 5.9 %collective-permute-start.10 = (f32[36,36,10]{1,0,2:T(8,128)S(1)}, f32[36,36,10]{1,0,2:T(8,128)S(1)}, u32[]{:S(2)}, u32[]{:S(2)}) collective-permute-start(f32[36,36,10]{1,0,2:T(8,128)S(1)} %copy.92), channel_id=1, source_target_pairs={{0,1},{2,3},{4,5},{6,7},{8,9},{10,11},{12,13},{14,15},{16,17},{18,... | collective-permute-start | bytes 155528 | tf_op jit(solution)/shard_map/ppermute | solution.py:23
  159.8 9.8 %copy-start.7 = (f32[36,10,128]{2,0,1:T(8,128)S(1)}, f32[36,10,128]{2,0,1:T(8,128)}, u32[]{:S(2)}) copy-start(f32[36,10,128]{2,0,1:T(8,128)} %copy-done.6) | copy-start | bytes 552964
  160.2 9.0 %collective-permute-start.11 = (f32[36,36,10]{1,0,2:T(8,128)S(1)}, f32[36,36,10]{1,0,2:T(8,128)S(1)}, u32[]{:S(2)}, u32[]{:S(2)}) collective-permute-start(f32[36,36,10]{1,0,2:T(8,128)S(1)} %copy.93), channel_id=1, source_target_pairs={{1,0},{3,2},{5,4},{7,6},{9,8},{11,10},{13,12},{15,14},{17,16},{19,... | collective-permute-start | bytes 155528 | tf_op jit(solution)/shard_map/ppermute | solution.py:24
  169.6 2.7 copy-start.18
  169.7 2.7 copy-start.19
  169.7 7.4 %copy-start.11 = (s32[2,2,16]{2,1,0:T(2,128)S(1)}, s32[2,2,16]{2,1,0:T(2,128)}, u32[]{:S(2)}) copy-start(s32[2,2,16]{2,1,0:T(2,128)} %param.6) | copy-start | bytes 772
  169.7 14.4 %copy-start.4 = (f32[1,4,4,18,128]{4,3,2,1,0:T(8,128)S(1)}, f32[1,4,4,18,128]{4,3,2,1,0:T(8,128)}, u32[]{:S(2)}) copy-start(f32[1,4,4,18,128]{4,3,2,1,0:T(8,128)} %get-tuple-element.14) | copy-start | bytes 442372
  169.7 14.4 %copy-start.5 = (f32[1,4,4,18,128]{4,3,2,1,0:T(8,128)S(1)}, f32[1,4,4,18,128]{4,3,2,1,0:T(8,128)}, u32[]{:S(2)}) copy-start(f32[1,4,4,18,128]{4,3,2,1,0:T(8,128)} %get-tuple-element.15) | copy-start | bytes 442372
  172.0 20.4 %copy-start = (s32[2,2,16,128]{3,2,1,0:T(8,128)S(1)}, s32[2,2,16,128]{3,2,1,0:T(8,128)}, u32[]{:S(2)}) copy-start(s32[2,2,16,128]{3,2,1,0:T(8,128)} %partners_ref.1) | copy-start | bytes 98308
  172.7 4.5 %collective-permute-start.12 = (f32[8,8,64]{2,1,0:T(8,128)S(1)}, f32[8,8,64]{2,1,0:T(8,128)S(1)}, u32[]{:S(2)}, u32[]{:S(2)}) collective-permute-start(f32[8,8,64]{2,1,0:T(8,128)S(1)} %fusion.99), channel_id=1, source_target_pairs={{0,8},{8,16},{16,24},{1,9},{9,17},{17,25},{2,10},{10,18},{18,26},{... | collective-permute-start | bytes 49160 | tf_op jit(solution)/shard_map/ppermute | solution.py:23
  175.3 4.0 %collective-permute-start.13 = (f32[8,8,64]{2,1,0:T(8,128)S(1)}, f32[8,8,64]{2,1,0:T(8,128)S(1)}, u32[]{:S(2)}, u32[]{:S(2)}) collective-permute-start(f32[8,8,64]{2,1,0:T(8,128)S(1)} %fusion.99), channel_id=1, source_target_pairs={{8,0},{16,8},{24,16},{9,1},{17,9},{25,17},{10,2},{18,10},{26,18},{... | collective-permute-start | bytes 49160 | tf_op jit(solution)/shard_map/ppermute | solution.py:24
  179.3 5.7 %collective-permute-start.14 = (f32[24,8,64]{2,1,0:T(8,128)S(1)}, f32[24,8,64]{2,1,0:T(8,128)S(1)}, u32[]{:S(2)}, u32[]{:S(2)}) collective-permute-start(f32[24,8,64]{2,1,0:T(8,128)S(1)} %pad_maximum_fusion.10), channel_id=1, source_target_pairs={{0,2},{2,4},{4,6},{1,3},{3,5},{5,7},{8,10},{10,12},{12,14},{9,11},... | collective-permute-start | bytes 147464 | tf_op jit(solution)/shard_map/ppermute | solution.py:23
  182.8 6.5 %collective-permute-start.15 = (f32[24,8,64]{2,1,0:T(8,128)S(1)}, f32[24,8,64]{2,1,0:T(8,128)S(1)}, u32[]{:S(2)}, u32[]{:S(2)}) collective-permute-start(f32[24,8,64]{2,1,0:T(8,128)S(1)} %pad_maximum_fusion.10), channel_id=1, source_target_pairs={{2,0},{4,2},{6,4},{3,1},{5,3},{7,5},{10,8},{12,10},{14,12},{11,9},... | collective-permute-start | bytes 147464 | tf_op jit(solution)/shard_map/ppermute | solution.py:24
  189.5 81.6 %collective-permute-start.16 = (f32[24,24,8]{2,1,0:T(8,128)S(1)}, f32[24,24,8]{2,1,0:T(8,128)S(1)}, u32[]{:S(2)}, u32[]{:S(2)}) collective-permute-start(f32[24,24,8]{2,1,0:T(8,128)S(1)} %get-tuple-element.27), channel_id=1, source_target_pairs={{0,1},{2,3},{4,5},{6,7},{8,9},{10,11},{12,13},{14,15},{16,17},{18,... | collective-permute-start | bytes 55304 | tf_op jit(solution)/shard_map/ppermute | solution.py:23
  190.9 90.3 %copy-start.9 = (f32[36,10,128]{2,0,1:T(8,128)S(1)}, f32[36,10,128]{2,0,1:T(8,128)}, u32[]{:S(2)}) copy-start(f32[36,10,128]{2,0,1:T(8,128)} %copy-done.8) | copy-start | bytes 552964
  190.9 80.1 %collective-permute-start.17 = (f32[24,24,8]{2,1,0:T(8,128)S(1)}, f32[24,24,8]{2,1,0:T(8,128)S(1)}, u32[]{:S(2)}, u32[]{:S(2)}) collective-permute-start(f32[24,24,8]{2,1,0:T(8,128)S(1)} %get-tuple-element.28), channel_id=1, source_target_pairs={{1,0},{3,2},{5,4},{7,6},{9,8},{11,10},{13,12},{15,14},{17,16},{19,... | collective-permute-start | bytes 55304 | tf_op jit(solution)/shard_map/ppermute | solution.py:24
  272.0 10.7 %collective-permute-start.18 = (f32[2,8,64]{2,1,0:T(8,128)S(1)}, f32[2,8,64]{2,1,0:T(8,128)S(1)}, u32[]{:S(2)}, u32[]{:S(2)}) collective-permute-start(f32[2,8,64]{2,1,0:T(8,128)S(1)} %get-tuple-element.46), channel_id=1, source_target_pairs={{0,8},{8,16},{16,24},{1,9},{9,17},{17,25},{2,10},{10,18},{18,26},{... | collective-permute-start | bytes 12296 | tf_op jit(solution)/shard_map/ppermute | solution.py:23
  279.9 3.1 collective-permute-start.19
  282.7 26.7 %copy-start.13 = (s32[132]{0:T(256)S(1)}, s32[132]{0:T(256)}, u32[]{:S(2)}) copy-start(s32[132]{0:T(256)} %iota_add_fusion) | copy-start | bytes 1588
  282.7 26.7 %copy-start.14 = (f32[132]{0:T(256)S(1)}, f32[132]{0:T(256)}, u32[]{:S(2)}) copy-start(f32[132]{0:T(256)} %and_convert_fusion) | copy-start | bytes 1588
  282.7 26.7 %copy-start.17 = (s32[68]{0:T(128)S(1)}, s32[68]{0:T(128)}, u32[]{:S(2)}) copy-start(s32[68]{0:T(128)} %add_multiply_fusion) | copy-start | bytes 820
  283.0 7.8 %collective-permute-start.20 = (f32[12,2,64]{2,1,0:T(2,128)S(1)}, f32[12,2,64]{2,1,0:T(2,128)S(1)}, u32[]{:S(2)}, u32[]{:S(2)}) collective-permute-start(f32[12,2,64]{2,1,0:T(2,128)S(1)} %get-tuple-element.38), channel_id=1, source_target_pairs={{0,2},{2,4},{4,6},{1,3},{3,5},{5,7},{8,10},{10,12},{12,14},{9,11},... | collective-permute-start | bytes 18440 | tf_op jit(solution)/shard_map/ppermute | solution.py:23
  288.6 5.6 %collective-permute-start.21 = (f32[12,2,64]{2,1,0:T(2,128)S(1)}, f32[12,2,64]{2,1,0:T(2,128)S(1)}, u32[]{:S(2)}, u32[]{:S(2)}) collective-permute-start(f32[12,2,64]{2,1,0:T(2,128)S(1)} %get-tuple-element.39), channel_id=1, source_target_pairs={{2,0},{4,2},{6,4},{3,1},{5,3},{7,5},{10,8},{12,10},{14,12},{11,9},... | collective-permute-start | bytes 18440 | tf_op jit(solution)/shard_map/ppermute | solution.py:24
  294.4 9.3 %collective-permute-start.22 = (f32[12,12,2]{2,1,0:T(8,128)S(1)}, f32[12,12,2]{2,1,0:T(8,128)S(1)}, u32[]{:S(2)}, u32[]{:S(2)}) collective-permute-start(f32[12,12,2]{2,1,0:T(8,128)S(1)} %get-tuple-element.36), channel_id=1, source_target_pairs={{0,1},{2,3},{4,5},{6,7},{8,9},{10,11},{12,13},{14,15},{16,17},{18,... | collective-permute-start | bytes 3464 | tf_op jit(solution)/shard_map/ppermute | solution.py:23
  300.8 7.6 %collective-permute-start.23 = (f32[12,12,2]{2,1,0:T(8,128)S(1)}, f32[12,12,2]{2,1,0:T(8,128)S(1)}, u32[]{:S(2)}, u32[]{:S(2)}) collective-permute-start(f32[12,12,2]{2,1,0:T(8,128)S(1)} %get-tuple-element.37), channel_id=1, source_target_pairs={{1,0},{3,2},{5,4},{7,6},{9,8},{11,10},{13,12},{15,14},{17,16},{19,... | collective-permute-start | bytes 3464 | tf_op jit(solution)/shard_map/ppermute | solution.py:24
  334.6 9.6 %copy-start.1 = (f32[2,2,16,128,11,11]{3,2,5,4,1,0:T(8,128)S(1)}, f32[2,2,16,128,11,11]{3,2,5,4,1,0:T(8,128)}, u32[]{:S(2)}) copy-start(f32[2,2,16,128,11,11]{3,2,5,4,1,0:T(8,128)} %get-tuple-element.22) | copy-start | bytes 11894788
  344.2 10.1 %copy-start.10 = (f32[2,2,16,128]{3,2,1,0:T(8,128)S(1)}, f32[2,2,16,128]{3,2,1,0:T(8,128)}, u32[]{:S(2)}) copy-start(f32[2,2,16,128]{3,2,1,0:T(8,128)} %get-tuple-element.40) | copy-start | bytes 98308

commit v2 on v1

--- a/solution.py
+++ b/solution.py
@@ -38,50 +38,152 @@
     return jnp.where(magnitude < 0.5, -2.0 * shifted, jnp.where(shifted > 0.0, -margin, margin))
 
 
-def patch_weights(offset):
-    points = jnp.arange(11).astype(jnp.float32)
-    shifted = 8.0 * offset[..., None] + 1.0 - points
-    return (spline(shifted), spline_slope(shifted))
-
-
-def charge_patches(weighted, offsets):
-    weight_x, _ = patch_weights(offsets[0])
-    weight_y, _ = patch_weights(offsets[1])
-    weight_z, _ = patch_weights(offsets[2])
-    plane_part = weighted[..., None, None] * weight_x[..., :, None] * weight_y[..., None, :]
-    flattened = plane_part.reshape(plane_part.shape[:-2] + (121,))
-    joined = jnp.einsum("...sp,...sc->...pc", flattened, weight_z, precision=highest)
-    return joined.reshape(joined.shape[:-2] + (11, 11, 11))
-
-
-def assemble(values, where_axis):
-    cell_count = values.shape[where_axis]
-    inner_part = lax.slice_in_dim(values, 0, 8, axis=where_axis + 1)
-    overflow = lax.slice_in_dim(values, 8, 11, axis=where_axis + 1)
-    inner_pad = [(0, 0)] * values.ndim
-    inner_pad[where_axis] = (0, 1)
-    over_pad = [(0, 0)] * values.ndim
-    over_pad[where_axis] = (1, 0)
-    over_pad[where_axis + 1] = (0, 5)
-    merged = jnp.pad(inner_part, inner_pad) + jnp.pad(overflow, over_pad)
-    new_shape = values.shape[:where_axis] + (8 * (cell_count + 1),) + values.shape[where_axis + 2 :]
-    return merged.reshape(new_shape)
-
-
-def cut_patches(values, where_axis):
-    cell_count = (values.shape[where_axis] - 4) // 8
-    split_shape = values.shape[:where_axis] + (cell_count, 8) + values.shape[where_axis + 1 :]
-    head_part = lax.slice_in_dim(values, 1, 8 * cell_count + 1, axis=where_axis).reshape(
-        split_shape
+def split_product(left, right, dims):
+    left_high, right_high = left.astype(jnp.bfloat16), right.astype(jnp.bfloat16)
+    left_low = (left - left_high.astype(jnp.float32)).astype(jnp.bfloat16)
+    right_low = (right - right_high.astype(jnp.float32)).astype(jnp.bfloat16)
+
+    def product(one, other):
+        return lax.dot_general(one, other, (dims, ((), ())), preferred_element_type=jnp.float32)
+
+    return product(left_high, right_high) + (
+        product(left_low, right_high) + product(left_high, right_low)
     )
-    widths = [(0, 0)] * values.ndim
-    widths[where_axis] = (0, 5)
-    padded = jnp.pad(values, widths)
-    tail_part = lax.slice_in_dim(padded, 9, 8 * cell_count + 9, axis=where_axis).reshape(
-        split_shape
-    )
-    tail_part = lax.slice_in_dim(tail_part, 0, 3, axis=where_axis + 1)
-    return jnp.concatenate([head_part, tail_part], axis=where_axis + 1)
+
+
+def row_of_cells(ref, lead, k):
+    return jnp.concatenate([ref[lead + (j, pl.ds(k, 1))] for j in range(ref.shape[-3])], axis=1)
+
+
+def point_gaps(offset, count, shift):
+    points = lax.broadcasted_iota(jnp.int32, (count, offset.shape[1]), 0).astype(jnp.float32)
+    return (8.0 * offset + 1.0 + shift) - points
+
+
+def cell_shift(cells_y, slots):
+    lane = lax.broadcasted_iota(jnp.int32, (1, cells_y * slots), 1)
+    return 8.0 * (lane // slots).astype(jnp.float32)
+
+
+def spread_kernel(offsets_ref, weighted_ref, grid_ref):
+    cells_x, cells_y, cells_z, slots = weighted_ref.shape
+    width = grid_ref.shape[-1]
+    grid_ref[...] = jnp.zeros_like(grid_ref)
+    shift_y = cell_shift(cells_y, slots)
+
+    def body(step, carry):
+        i, k = step // cells_z, step % cells_z
+        off_x, off_y, off_z = [row_of_cells(offsets_ref, (d, i), k) for d in range(3)]
+        charge = row_of_cells(weighted_ref, (i,), k)
+        weight_x = spline(point_gaps(off_x, 16, 0.0)) * charge
+        weight_z = spline(point_gaps(off_z, 16, 0.0))
+        weight_y = spline(point_gaps(off_y, width, shift_y))
+        plane = jnp.concatenate([weight_x[a : a + 1] * weight_z for a in range(11)], axis=0)
+        patch = split_product(plane, weight_y, ((1,), (1,)))
+        for a in range(11):
+            rows = pl.ds(pl.multiple_of(8 * k, 8), 16)
+            grid_ref[8 * i + a, rows, :] += patch[16 * a : 16 * a + 16]
+        return carry
+
+    lax.fori_loop(0, cells_x * cells_z, body, 0)
+
+
+def spread_charge(offsets, weighted):
+    cells_x, cells_y, cells_z, _ = weighted.shape
+    width = 8 * cells_y + 16
+    grid = pl.pallas_call(
+        spread_kernel,
+        out_shape=jax.ShapeDtypeStruct((8 * cells_x + 3, 8 * cells_z + 8, width), jnp.float32),
+        in_specs=[pl.BlockSpec(memory_space=pltpu.VMEM)] * 2,
+        out_specs=pl.BlockSpec(memory_space=pltpu.VMEM),
+        compiler_params=pltpu.CompilerParams(vmem_limit_bytes=24 * 2**20),
+        cost_estimate=pl.CostEstimate(flops=10**8, bytes_accessed=4 * 10**6, transcendentals=0),
+    )(offsets, weighted)
+    return jnp.transpose(grid[:, : 8 * cells_z + 3, : 8 * cells_y + 3], (0, 2, 1))
+
+
+def gather_kernel(offsets_ref, weighted_ref, grid_ref, out_ref):
+    cells_x, cells_y, cells_z, slots = weighted_ref.shape
+    width = grid_ref.shape[-1] // 3
+    shift_y = cell_shift(cells_y, slots)
+    lane = lax.broadcasted_iota(jnp.int32, (16, 3 * width), 1)
+    middle = (lane >= width) & (lane < 2 * width)
+
+    def body(step, carry):
+        i, k = step // cells_z, step % cells_z
+        off_x, off_y, off_z = [row_of_cells(offsets_ref, (d, i), k) for d in range(3)]
+        gap_x, gap_z = point_gaps(off_x, 16, 0.0), point_gaps(off_z, 16, 0.0)
+        gap_y = point_gaps(off_y, width, shift_y)
+        weight_x, slope_x = spline(gap_x), spline_slope(gap_x)
+        weight_z, slope_z = spline(gap_z), spline_slope(gap_z)
+        both_y = jnp.concatenate([spline(gap_y), spline_slope(gap_y)], axis=1)
+        y_high = both_y.astype(jnp.bfloat16)
+        y_low = (both_y - y_high.astype(jnp.float32)).astype(jnp.bfloat16)
+        parts = []
+        for a in range(11):
+            part = grid_ref[8 * i + a, pl.ds(pl.multiple_of(8 * k, 8), 16), :]
+            low = part - part.astype(jnp.bfloat16).astype(jnp.float32)
+            parts.append(jnp.where(middle, low, part).astype(jnp.bfloat16))
+        found = jnp.dot(
+            jnp.concatenate(parts, axis=0),
+            jnp.concatenate([y_high, y_high, y_low], axis=0),
+            preferred_element_type=jnp.float32,
+        )
+        lanes = cells_y * slots
+        totals = [jnp.zeros((16, lanes), jnp.float32) for _ in range(3)]
+        for a in range(11):
+            level = found[16 * a : 16 * a + 16, :lanes]
+            rising = found[16 * a : 16 * a + 16, lanes:]
+            totals[0] += slope_x[a : a + 1] * level
+            totals[1] += weight_x[a : a + 1] * rising
+            totals[2] += weight_x[a : a + 1] * level
+        charge = row_of_cells(weighted_ref, (i,), k)
+        for d, along_z in enumerate((weight_z, weight_z, slope_z)):
+            force = -charge * jnp.sum(totals[d] * along_z, axis=0, keepdims=True)
+            for j in range(cells_y):
+                out_ref[d, i, j, pl.ds(k, 1), :] = force[:, j * slots : (j + 1) * slots]
+        return carry
+
+    lax.fori_loop(0, cells_x * cells_z, body, 0)
+
+
+def grid_forces(offsets, weighted, potential):
+    cells_x, cells_y, cells_z, _ = weighted.shape
+    width = 8 * cells_y + 16
+    grid = jnp.transpose(potential[1:, 1:, 1:], (0, 2, 1))
+    grid = jnp.pad(grid, ((0, 0), (0, 8 * cells_z + 8 - grid.shape[1]), (0, width - grid.shape[2])))
+    grid = jnp.concatenate([grid] * 3, axis=2)
+    return pl.pallas_call(
+        gather_kernel,
+        out_shape=jax.ShapeDtypeStruct(offsets.shape, jnp.float32),
+        in_specs=[pl.BlockSpec(memory_space=pltpu.VMEM)] * 3,
+        out_specs=pl.BlockSpec(memory_space=pltpu.VMEM),
+        compiler_params=pltpu.CompilerParams(vmem_limit_bytes=24 * 2**20),
+        cost_estimate=pl.CostEstimate(flops=10**8, bytes_accessed=4 * 10**6, transcendentals=0),
+    )(offsets, weighted, grid)
+
+
+def spread_halo(value, sides, depth):
+    for axis, dim in sides:
+        size, length = (lax.axis_size(axis), value.shape[dim] - 3)
+        up = [(i, (i + 1) % size) for i in range(size - 1)]
+        down = [(j, i) for i, j in up]
+        last = lax.slice_in_dim(value, length - depth + 1, length + 3, axis=dim)
+        initial = lax.slice_in_dim(value, 0, depth + 1, axis=dim)
+        before = lax.ppermute(last, axis, up)
+        after = lax.ppermute(initial, axis, down)
+
+        def placed(part, low, high):
+            widths = [(0, 0)] * part.ndim
+            widths[dim] = (low, high)
+            return jnp.pad(part, widths)
+
+        value = (
+            placed(value, depth - 1, depth - 2)
+            + placed(before, 0, length + depth - 2)
+            + placed(after, length + depth - 1, 0)
+        )
+    return value
 
 
 def kernel_band(in_length, spread):
@@ -187,24 +289,17 @@
     )(counts.reshape(-1), grown, partners)
 
 
-def grid_force(patches, weighted, offsets):
-    weight_x, slope_x = patch_weights(offsets[0])
-    weight_y, slope_y = patch_weights(offsets[1])
-    weight_z, slope_z = patch_weights(offsets[2])
-    flattened = patches.reshape(patches.shape[:-3] + (121, 11))
-    level_part = jnp.einsum("...pc,...sc->...sp", flattened, weight_z, precision=highest)
-    rising = jnp.einsum("...pc,...sc->...sp", flattened, slope_z, precision=highest)
-    level_part = level_part.reshape(level_part.shape[:-1] + (11, 11))
-    rising = rising.reshape(rising.shape[:-1] + (11, 11))
-    force_x = jnp.sum(slope_x[..., :, None] * weight_y[..., None, :] * level_part, axis=(-2, -1))
-    force_y = jnp.sum(weight_x[..., :, None] * slope_y[..., None, :] * level_part, axis=(-2, -1))
-    force_z = jnp.sum(weight_x[..., :, None] * weight_y[..., None, :] * rising, axis=(-2, -1))
-    return -weighted * jnp.stack([force_x, force_y, force_z])
-
-
-def inside_grid(fine_length, first_point, device_count):
-    coordinate = jnp.arange(fine_length + 4) - 2 + first_point
-    return ((coordinate >= 0) & (coordinate < fine_length * device_count)).astype(jnp.float32)
+def inside_mask(lengths, depth):
+    mask = jnp.float32(1.0)
+    for dim, axis in enumerate(("gx", "gy", "ga")):
+        length = lengths[dim]
+        first = lax.axis_index(axis) * length - depth
+        point = jnp.arange(length + 2 * depth) + first
+        inside = (point >= 0) & (point < length * lax.axis_size(axis))
+        shape = [1, 1, 1]
+        shape[dim] = length + 2 * depth
+        mask = mask * inside.astype(jnp.float32).reshape(shape)
+    return mask
 
 
 def per_device(offsets, charge, counts, partners):
@@ -219,14 +314,12 @@
     cell_units = cell_positions(grown_offsets, -1.0)
     grown = jnp.concatenate([cell_units, grown_charge[None]], axis=0)
     short_force = short_forces(counts, grown, partners)
-    patches = charge_patches(grown_charge, grown_offsets)
-    spread_grid = jnp.transpose(patches, (0, 3, 1, 4, 2, 5))
-    for where_axis in range(3):
-        spread_grid = assemble(spread_grid, where_axis)
     grid_x, grid_y, grid_z = (8 * cells_x, 8 * cells_y, 8 * cells_z)
-    fine_charge = spread_grid[9 : 9 + grid_x, 9 : 9 + grid_y, 9 : 9 + grid_z]
+    lengths = (grid_x, grid_y, grid_z)
     halo_depth = 10
-    widened = padded_2(fine_charge, (("gx", 0), ("gy", 1), ("ga", 2)), halo_depth)
+    spread = spread_charge(offsets, weighted)
+    widened = spread_halo(spread, (("gx", 0), ("gy", 1), ("ga", 2)), halo_depth)
+    widened = widened * inside_mask(lengths, halo_depth)
     fine_potential = convolve(widened, fine_spread, fine_scale)
     coarse_charge = widened
     for where_axis, fine_length in enumerate((grid_x, grid_y, grid_z)):
@@ -245,15 +338,8 @@
             jnp.transpose(grid_map(fine_length + 4, fine_length // 2 + 4, -2, -2)),
             where_axis,
         )
-    inside_x = inside_grid(grid_x, lax.axis_index("gx") * grid_x, lax.axis_size("gx"))
-    inside_y = inside_grid(grid_y, lax.axis_index("gy") * grid_y, lax.axis_size("gy"))
-    inside_z = inside_grid(grid_z, lax.axis_index("ga") * grid_z, lax.axis_size("ga"))
-    inside_mask = inside_x[:, None, None] * inside_y[None, :, None] * inside_z[None, None, :]
-    potential = (potential + fine_potential) * inside_mask
-    for where_axis in range(3):
-        potential = cut_patches(potential, 2 * where_axis)
-    near_grid = jnp.transpose(potential, (0, 2, 4, 1, 3, 5))
-    long_force = grid_force(near_grid, weighted, offsets)
+    potential = (potential + fine_potential) * inside_mask(lengths, 2)
+    long_force = grid_forces(offsets, weighted, potential)
     return (short_force, long_force)
 
 

time: 362 us -> 242 us (0.67)
  matrix products: 57.6 us -> 7.59 us
  local copies, waits for them, and re-layouts: 73.6 us -> 23.7 us
  Pallas kernels: 78.7 us -> 102 us
  other arithmetic: 40.9 us -> 18.2 us
  waiting for transfers between devices: 42.2 us -> 31.6 us
  starting transfers between devices: 60.3 us -> 54.3 us
    dot_general x3 -> x0, matrix products: 49.7 us -> none  [the longest x1 30.1 us: charge_patches(): jnp.einsum('...sp,...sc->...pc', flattened, weight_z, precision=highest)]
    ppermute x12 -> x9, waiting for transfers between devices: 36.1 us -> 14.7 us  [padded_2(): after = lax.ppermute(initial, axis, down)]
    ppermute x12 -> x9, starting transfers between devices: 44.5 us -> 26.6 us  [padded_2(): before = lax.ppermute(last, axis, up)]
    ppermute x0 -> x6, starting transfers between devices: none -> 15.8 us  [the longest x3 12 us: spread_halo(): before = lax.ppermute(last, axis, up)]
    ppermute x0 -> x6, waiting for transfers between devices: none -> 15.8 us  [the longest x3 15.7 us: spread_halo(): after = lax.ppermute(initial, axis, down)]
    pallas_call x0 -> x2, Pallas kernels: none -> 15.6 us  [the longest x1 7.93 us: grid_forces(): pl.pallas_call(gather_kernel, out_shape=jax.ShapeDtypeStruct(offsets.shap...]
    dot_general x1 -> x0, local copies, waits for them, and re-layouts: 13.9 us -> none  [charge_patches(): jnp.einsum('...sp,...sc->...pc', flattened, weight_z, precision=highest)]
    unnamed x45 -> x36, local copies, waits for them, and re-layouts: 13.1 us -> 0.96 us
  transfers between devices with their start and end apart: 24 -> 24, of which waited for: 15 -> 9; matrix products, arithmetic and copies ran while one was open for 5% -> 15% of each run, Pallas kernels for 22% -> 36%
where the time goes in v2:
time: 242 us; the launch traced here: 239 us
  Pallas kernels  102 us (42%)
  starting transfers between devices  54.3 us (22%)
  waiting for transfers between devices  31.6 us (13%)
  local copies, waits for them, and re-layouts  23.7 us (10%)
  other arithmetic  18.2 us (8%)
  matrix products  7.59 us (3%)
    pallas_call x1, Pallas kernels, short_forces(): pl.pallas_call(short_kernel, out_shape=jax.ShapeDtypeStruct((3,) + cells...  86.3 us
    ppermute x9, starting transfers between devices, padded_2(): before = lax.ppermute(last, axis, up)  26.6 us
    ppermute x3, waiting for transfers between devices, spread_halo(): after = lax.ppermute(initial, axis, down)  15.7 us
    ppermute x9, waiting for transfers between devices, padded_2(): after = lax.ppermute(initial, axis, down)  14.7 us
    ppermute x3, starting transfers between devices, spread_halo(): before = lax.ppermute(last, axis, up)  12 us
    ppermute x9, starting transfers between devices, padded_2(): after = lax.ppermute(initial, axis, down)  11.8 us
    pallas_call x1, Pallas kernels, grid_forces(): pl.pallas_call(gather_kernel, out_shape=jax.ShapeDtypeStruct(offsets.shap...  7.93 us
    pallas_call x1, Pallas kernels, spread_charge(): pl.pallas_call(spread_kernel, out_shape=jax.ShapeDtypeStruct((8 * cells_x...  7.71 us
  transfers between devices with their start and end apart: 24, of which 9 were waited for; matrix products, arithmetic and copies ran while one was open for 15% of the time, Pallas kernels for 36%

profile of v2, /device:TPU:0, one launch (start us, length us, event | category | flops | bytes accessed | tf_op | source)
XLA Modules:
  0.0 238.7 jit_solution(2197926622570147055)
XLA Ops:
  2.4 7.7 %shard_map.60 = f32[19,136,32]{2,1,0:T(8,128)S(1)} custom-call(f32[3,2,2,16,128]{4,3,2,1,0:T(8,128)S(1)} %copy-done, f32[2,2,16,128]{3,2,1,0:T(8,128)S(1)} %fusion.62.weighted_ref), custom_call_target="tpu_custom_call" | custom-call | flops 100000000 | bytes 4000000 | tf_op jit(solution)/shard_map/pallas_call | solution.py:94
  10.8 3.3 %collective-permute-start.6 = (f32[12,19,131]{2,1,0:T(8,128)S(1)}, f32[12,19,131]{2,1,0:T(8,128)}, u32[]{:S(2)}, u32[]{:S(2)}) collective-permute-start(f32[12,19,131]{2,1,0:T(8,128)S(1)} %copy.18), channel_id=1, source_target_pairs={{0,8},{8,16},{16,24},{1,9},{9,17},{17,25},{2,10},{10,18},{18,26},{... | collective-permute-start | bytes 358424 | tf_op jit(solution)/shard_map/ppermute | solution.py:173
  14.5 1.3 collective-permute-start.7
  16.0 4.4 %collective-permute-start = (f32[4,1,2,16,128]{4,3,2,1,0:T(8,128)S(1)}, f32[4,1,2,16,128]{4,3,2,1,0:T(8,128)S(1)}, u32[]{:S(2)}, u32[]{:S(2)}) collective-permute-start(f32[4,1,2,16,128]{4,3,2,1,0:T(8,128)S(1)} %get-tuple-element.12), channel_id=1, source_target_pairs={{0,8},{8,16},{16,24},{1,9},{9,17},{17,25},{2,10},{10,18},{18,26},{... | collective-permute-start | bytes 196616 | tf_op jit(solution)/shard_map/ppermute | solution.py:23
  20.4 1.3 collective-permute-start.1
  27.2 4.2 %collective-permute-start.2 = (f32[4,4,1,16,128]{4,3,2,1,0:T(8,128)}, f32[4,4,1,16,128]{4,3,2,1,0:T(8,128)}, u32[]{:S(2)}, u32[]{:S(2)}) collective-permute-start(f32[4,4,1,16,128]{4,3,2,1,0:T(8,128)} %get-tuple-element.10), channel_id=1, source_target_pairs={{0,2},{2,4},{4,6},{1,3},{3,5},{5,7},{8,10},{10,12},{12,14},{9,11},... | collective-permute-start | bytes 393224 | tf_op jit(solution)/shard_map/ppermute | solution.py:23
  31.4 1.3 collective-permute-start.3
  32.7 1.2 copy.21
  33.9 1.3 copy.19
  35.2 1.8 pad_add_fusion.1
  37.0 2.1 slice.119
  39.2 3.2 %copy.22 = f32[36,12,131]{2,0,1:T(8,128)S(1)} copy(f32[36,12,131]{1,2,0:T(8,128)} %slice.119) | data formatting | bytes 452736 | tf_op jit(solution)/shard_map/slice | solution.py:171
  42.4 5.3 %collective-permute-start.8 = (f32[36,12,131]{2,0,1:T(8,128)S(1)}, f32[36,12,131]{2,0,1:T(8,128)}, u32[]{:S(2)}, u32[]{:S(2)}) collective-permute-start(f32[36,12,131]{2,0,1:T(8,128)S(1)} %copy.22), channel_id=1, source_target_pairs={{0,2},{2,4},{4,6},{1,3},{3,5},{5,7},{8,10},{10,12},{12,14},{9,11},... | collective-permute-start | bytes 679112 | tf_op jit(solution)/shard_map/ppermute | solution.py:173
  47.9 2.2 copy.24
  50.1 1.3 collective-permute-start.9
  51.4 1.6 pad_maximum_fusion.15
  53.0 3.3 %collective-permute-start.4 = (f32[4,4,4,1,128]{4,3,2,1,0:T(1,128)}, f32[4,4,4,1,128]{4,3,2,1,0:T(1,128)S(1)}, u32[]{:S(2)}, u32[]{:S(2)}) collective-permute-start(f32[4,4,4,1,128]{4,3,2,1,0:T(1,128)} %get-tuple-element.6), channel_id=1, source_target_pairs={{0,1},{2,3},{4,5},{6,7},{8,9},{10,11},{12,13},{14,15},{16,17},{18,... | collective-permute-start | bytes 98312 | tf_op jit(solution)/shard_map/ppermute | solution.py:23
  56.4 1.3 collective-permute-start.5
  57.7 7.3 %collective-permute-done.9 = f32[36,11,131]{2,0,1:T(8,128)} collective-permute-done((f32[36,11,131]{2,0,1:T(8,128)}, f32[36,11,131]{2,0,1:T(8,128)}, u32[]{:S(2)}, u32[]{:S(2)}) %collective-permute-start.9) | collective-permute-done | bytes 207536 | tf_op jit(solution)/shard_map/ppermute | solution.py:174
  65.0 3.3 %copy.25 = f32[36,11,131]{1,2,0:T(8,128)} copy(f32[36,11,131]{2,0,1:T(8,128)} %collective-permute-done.9) | data formatting | bytes 415008 | tf_op jit(solution)/shard_map/ppermute | solution.py:174
  68.3 3.4 %copy.23 = f32[36,12,131]{1,2,0:T(8,128)} copy(f32[36,12,131]{2,0,1:T(8,128)} %collective-permute-done.8) | data formatting | bytes 452736 | tf_op jit(solution)/shard_map/ppermute | solution.py:173
  71.7 3.8 %pad_add_fusion = f32[36,36,131]{1,2,0:T(8,128)S(1)} fusion(f32[36,11,131]{1,2,0:T(8,128)} %copy.25, f32[36,12,131]{1,2,0:T(8,128)} %copy.23, f32[36,19,131]{1,2,0:T(8,128)S(1)} %pad_add_fusion.1), kind=kLoop, calls=%fused_computation.1 | loop fusion | flops 339552 | bytes 1471392 | tf_op jit(solution)/shard_map/add | solution.py:182
  75.7 3.4 %collective-permute-start.10 = (f32[36,36,12]{1,2,0:T(8,128)S(1)}, f32[36,36,12]{1,2,0:T(8,128)S(1)}, u32[]{:S(2)}, u32[]{:S(2)}) collective-permute-start(f32[36,36,12]{1,2,0:T(8,128)S(1)} %slice.121), channel_id=1, source_target_pairs={{0,1},{2,3},{4,5},{6,7},{8,9},{10,11},{12,13},{14,15},{16,17},{18,... | collective-permute-start | bytes 186632 | tf_op jit(solution)/shard_map/ppermute | solution.py:173
  79.0 1.3 collective-permute-start.11
  80.4 1.1 pad_maximum_fusion.1
  81.5 8.4 %collective-permute-done.11 = f32[36,36,11]{1,2,0:T(8,128)S(1)} collective-permute-done((f32[36,36,11]{1,2,0:T(8,128)S(1)}, f32[36,36,11]{1,2,0:T(8,128)S(1)}, u32[]{:S(2)}, u32[]{:S(2)}) %collective-permute-start.11) | collective-permute-done | bytes 57056 | tf_op jit(solution)/shard_map/ppermute | solution.py:174
  89.9 2.1 multiply_multiply_fusion
  92.0 3.5 %copy.26 = f32[36,36,148]{2,0,1:T(8,128)S(1)} copy(f32[36,36,148]{1,2,0:T(8,128)} %multiply_multiply_fusion) | data formatting | bytes 1534464 | tf_op jit(solution)/shard_map/mul | solution.py:322
  97.1 1.3 collective-permute-start.12
  98.4 1.3 collective-permute-start.13
  99.8 1.7 collective-permute-done.13
  101.5 2.5 %collective-permute-start.14 = (f32[24,8,64]{2,1,0:T(8,128)S(1)}, f32[24,8,64]{2,1,0:T(8,128)S(1)}, u32[]{:S(2)}, u32[]{:S(2)}) collective-permute-start(f32[24,8,64]{2,1,0:T(8,128)S(1)} %pad_maximum_fusion.6), channel_id=1, source_target_pairs={{0,2},{2,4},{4,6},{1,3},{3,5},{5,7},{8,10},{10,12},{12,14},{9,11},... | collective-permute-start | bytes 147464 | tf_op jit(solution)/shard_map/ppermute | solution.py:23
  104.0 1.3 collective-permute-start.15
  106.2 4.4 %collective-permute-done.15 = f32[24,8,64]{2,1,0:T(8,128)S(1)} collective-permute-done((f32[24,8,64]{2,1,0:T(8,128)S(1)}, f32[24,8,64]{2,1,0:T(8,128)S(1)}, u32[]{:S(2)}, u32[]{:S(2)}) %collective-permute-start.15) | collective-permute-done | bytes 49184 | tf_op jit(solution)/shard_map/ppermute | solution.py:24
  110.8 1.5 collective-permute-start.16
  112.3 1.5 collective-permute-start.17
  113.8 86.3 %shard_map.59 = f32[3,2,2,16,128]{4,3,2,1,0:T(8,128)} custom-call(s32[64]{0:T(128)S(1)} %reshape.188.counts_ref, f32[4,4,4,18,128]{4,3,2,1,0:T(8,128)S(1)} %pad_maximum_fusion.2.grown_ref, s32[2,2,16,128]{3,2,1,0:T(8,128)S(1)} %copy-done.2), custom_call_target="tpu_custom_call" | custom-call | flops 1000000000 | bytes 10000000 | tf_op jit(solution)/shard_map/pallas_call | solution.py:280
  201.0 6.9 %collective-permute-start.18 = (f32[2,8,64]{2,1,0:T(8,128)S(1)}, f32[2,8,64]{2,1,0:T(8,128)S(1)}, u32[]{:S(2)}, u32[]{:S(2)}) collective-permute-start(f32[2,8,64]{2,1,0:T(8,128)S(1)} %get-tuple-element.18), channel_id=1, source_target_pairs={{0,8},{8,16},{16,24},{1,9},{9,17},{17,25},{2,10},{10,18},{18,26},{... | collective-permute-start | bytes 12296 | tf_op jit(solution)/shard_map/ppermute | solution.py:23
  207.9 1.3 collective-permute-start.19
  210.9 1.3 collective-permute-start.20
  212.2 1.3 collective-permute-start.21
  214.4 3.5 %collective-permute-done.21 = f32[12,2,64]{2,1,0:T(2,128)S(1)} collective-permute-done((f32[12,2,64]{2,1,0:T(2,128)S(1)}, f32[12,2,64]{2,1,0:T(2,128)S(1)}, u32[]{:S(2)}, u32[]{:S(2)}) %collective-permute-start.21) | collective-permute-done | bytes 6176 | tf_op jit(solution)/shard_map/ppermute | solution.py:24
  218.0 1.3 collective-permute-start.22
  219.3 1.3 collective-permute-start.23
  220.6 1.4 fusion.11
  222.4 4.3 %collective-permute-done.23 = f32[12,12,2]{2,1,0:T(8,128)S(1)} collective-permute-done((f32[12,12,2]{2,1,0:T(8,128)S(1)}, f32[12,12,2]{2,1,0:T(8,128)S(1)}, u32[]{:S(2)}, u32[]{:S(2)}) %collective-permute-start.23) | collective-permute-done | bytes 1184 | tf_op jit(solution)/shard_map/ppermute | solution.py:24
  227.7 1.4 fusion.22
  230.8 7.9 %shard_map.61 = f32[3,2,2,16,128]{4,3,2,1,0:T(8,128)} custom-call(f32[3,2,2,16,128]{4,3,2,1,0:T(8,128)S(1)} %copy-done.1, f32[2,2,16,128]{3,2,1,0:T(8,128)S(1)} %fusion.62.weighted_ref, f32[19,136,96]{2,1,0:T(8,128)S(1)} %pad_maximum_fusion.grid_ref), custom_call_target="tpu_custom_call" | custom-call | flops 100000000 | bytes 4000000 | tf_op jit(solution)/shard_map/pallas_call | solution.py:156
  (109 shorter events, 18.0 us)
Async XLA Ops:
  1.5 0.9 copy-start
  10.2 3.9 %copy-start.3 = (f32[19,19,131]{1,2,0:T(8,128)}, f32[19,19,131]{1,2,0:T(8,128)S(1)}, u32[]{:S(2)}) copy-start(f32[19,19,131]{1,2,0:T(8,128)S(1)} %slice_bitcast_fusion) | copy-start | bytes 567496
  10.7 5.1 %copy-start.8 = (f32[2,2,16,128]{3,2,1,0:T(8,128)S(1)}, f32[2,2,16,128]{3,2,1,0:T(8,128)}, u32[]{:S(2)}) copy-start(f32[2,2,16,128]{3,2,1,0:T(8,128)} %param.5) | copy-start | bytes 98308
  10.7 5.1 %copy-start.9 = (s32[2,2,16]{2,1,0:T(2,128)S(1)}, s32[2,2,16]{2,1,0:T(2,128)}, u32[]{:S(2)}) copy-start(s32[2,2,16]{2,1,0:T(2,128)} %param.6) | copy-start | bytes 772
  10.7 5.2 %copy-start.1 = (f32[3,2,2,16,128]{4,3,2,1,0:T(8,128)S(1)}, f32[3,2,2,16,128]{4,3,2,1,0:T(8,128)}, u32[]{:S(2)}) copy-start(f32[3,2,2,16,128]{4,3,2,1,0:T(8,128)} %offsets_ref.3) | copy-start | bytes 294916
  10.8 23.2 %collective-permute-start.6 = (f32[12,19,131]{2,1,0:T(8,128)S(1)}, f32[12,19,131]{2,1,0:T(8,128)}, u32[]{:S(2)}, u32[]{:S(2)}) collective-permute-start(f32[12,19,131]{2,1,0:T(8,128)S(1)} %copy.18), channel_id=1, source_target_pairs={{0,8},{8,16},{16,24},{1,9},{9,17},{17,25},{2,10},{10,18},{18,26},{... | collective-permute-start | bytes 358424 | tf_op jit(solution)/shard_map/ppermute | solution.py:173
  14.5 18.2 %collective-permute-start.7 = (f32[11,19,131]{2,1,0:T(8,128)S(1)}, f32[11,19,131]{2,1,0:T(8,128)S(1)}, u32[]{:S(2)}, u32[]{:S(2)}) collective-permute-start(f32[11,19,131]{2,1,0:T(8,128)S(1)} %copy.20), channel_id=1, source_target_pairs={{8,0},{16,8},{24,16},{9,1},{17,9},{25,17},{10,2},{18,10},{26,18},{... | collective-permute-start | bytes 328556 | tf_op jit(solution)/shard_map/ppermute | solution.py:174
  16.0 10.5 %collective-permute-start = (f32[4,1,2,16,128]{4,3,2,1,0:T(8,128)S(1)}, f32[4,1,2,16,128]{4,3,2,1,0:T(8,128)S(1)}, u32[]{:S(2)}, u32[]{:S(2)}) collective-permute-start(f32[4,1,2,16,128]{4,3,2,1,0:T(8,128)S(1)} %get-tuple-element.12), channel_id=1, source_target_pairs={{0,8},{8,16},{16,24},{1,9},{9,17},{17,25},{2,10},{10,18},{18,26},{... | collective-permute-start | bytes 196616 | tf_op jit(solution)/shard_map/ppermute | solution.py:23
  20.4 6.1 %collective-permute-start.1 = (f32[4,1,2,16,128]{4,3,2,1,0:T(8,128)S(1)}, f32[4,1,2,16,128]{4,3,2,1,0:T(8,128)S(1)}, u32[]{:S(2)}, u32[]{:S(2)}) collective-permute-start(f32[4,1,2,16,128]{4,3,2,1,0:T(8,128)S(1)} %get-tuple-element.13), channel_id=1, source_target_pairs={{8,0},{16,8},{24,16},{9,1},{17,9},{25,17},{10,2},{18,10},{26,18},{... | collective-permute-start | bytes 196616 | tf_op jit(solution)/shard_map/ppermute | solution.py:24
  26.5 7.5 %copy-start.4 = (f32[4,1,2,16,128]{4,3,2,1,0:T(8,128)}, f32[4,1,2,16,128]{4,3,2,1,0:T(8,128)S(1)}, u32[]{:S(2)}) copy-start(f32[4,1,2,16,128]{4,3,2,1,0:T(8,128)S(1)} %collective-permute-done) | copy-start | bytes 196612
  26.5 7.5 %copy-start.6 = (f32[4,1,2,16,128]{4,3,2,1,0:T(8,128)}, f32[4,1,2,16,128]{4,3,2,1,0:T(8,128)S(1)}, u32[]{:S(2)}) copy-start(f32[4,1,2,16,128]{4,3,2,1,0:T(8,128)S(1)} %collective-permute-done.1) | copy-start | bytes 196612
  27.2 24.2 %collective-permute-start.2 = (f32[4,4,1,16,128]{4,3,2,1,0:T(8,128)}, f32[4,4,1,16,128]{4,3,2,1,0:T(8,128)}, u32[]{:S(2)}, u32[]{:S(2)}) collective-permute-start(f32[4,4,1,16,128]{4,3,2,1,0:T(8,128)} %get-tuple-element.10), channel_id=1, source_target_pairs={{0,2},{2,4},{4,6},{1,3},{3,5},{5,7},{8,10},{10,12},{12,14},{9,11},... | collective-permute-start | bytes 393224 | tf_op jit(solution)/shard_map/ppermute | solution.py:23
  31.4 20.0 %collective-permute-start.3 = (f32[4,4,1,16,128]{4,3,2,1,0:T(8,128)}, f32[4,4,1,16,128]{4,3,2,1,0:T(8,128)}, u32[]{:S(2)}, u32[]{:S(2)}) collective-permute-start(f32[4,4,1,16,128]{4,3,2,1,0:T(8,128)} %get-tuple-element.11), channel_id=1, source_target_pairs={{2,0},{4,2},{6,4},{3,1},{5,3},{7,5},{10,8},{12,10},{14,12},{11,9},... | collective-permute-start | bytes 393224 | tf_op jit(solution)/shard_map/ppermute | solution.py:24
  39.2 8.6 %copy-start.11 = (f32[132]{0:T(256)S(1)}, f32[132]{0:T(256)}, u32[]{:S(2)}) copy-start(f32[132]{0:T(256)} %and_convert_fusion) | copy-start | bytes 1588
  42.4 26.0 %collective-permute-start.8 = (f32[36,12,131]{2,0,1:T(8,128)S(1)}, f32[36,12,131]{2,0,1:T(8,128)}, u32[]{:S(2)}, u32[]{:S(2)}) collective-permute-start(f32[36,12,131]{2,0,1:T(8,128)S(1)} %copy.22), channel_id=1, source_target_pairs={{0,2},{2,4},{4,6},{1,3},{3,5},{5,7},{8,10},{10,12},{12,14},{9,11},... | collective-permute-start | bytes 679112 | tf_op jit(solution)/shard_map/ppermute | solution.py:173
  47.9 3.6 %copy-start.5 = (f32[4,1,2,16,128]{4,3,2,1,0:T(8,128)S(1)}, f32[4,1,2,16,128]{4,3,2,1,0:T(8,128)}, u32[]{:S(2)}) copy-start(f32[4,1,2,16,128]{4,3,2,1,0:T(8,128)} %copy-done.4) | copy-start | bytes 196612
  47.9 3.6 %copy-start.7 = (f32[4,1,2,16,128]{4,3,2,1,0:T(8,128)S(1)}, f32[4,1,2,16,128]{4,3,2,1,0:T(8,128)}, u32[]{:S(2)}) copy-start(f32[4,1,2,16,128]{4,3,2,1,0:T(8,128)} %copy-done.6) | copy-start | bytes 196612
  50.1 14.9 %collective-permute-start.9 = (f32[36,11,131]{2,0,1:T(8,128)}, f32[36,11,131]{2,0,1:T(8,128)}, u32[]{:S(2)}, u32[]{:S(2)}) collective-permute-start(f32[36,11,131]{2,0,1:T(8,128)} %copy.24), channel_id=1, source_target_pairs={{2,0},{4,2},{6,4},{3,1},{5,3},{7,5},{10,8},{12,10},{14,12},{11,9},... | collective-permute-start | bytes 622520 | tf_op jit(solution)/shard_map/ppermute | solution.py:174
  53.0 27.3 %collective-permute-start.4 = (f32[4,4,4,1,128]{4,3,2,1,0:T(1,128)}, f32[4,4,4,1,128]{4,3,2,1,0:T(1,128)S(1)}, u32[]{:S(2)}, u32[]{:S(2)}) collective-permute-start(f32[4,4,4,1,128]{4,3,2,1,0:T(1,128)} %get-tuple-element.6), channel_id=1, source_target_pairs={{0,1},{2,3},{4,5},{6,7},{8,9},{10,11},{12,13},{14,15},{16,17},{18,... | collective-permute-start | bytes 98312 | tf_op jit(solution)/shard_map/ppermute | solution.py:23
  56.4 23.9 %collective-permute-start.5 = (f32[4,4,4,1,128]{4,3,2,1,0:T(1,128)S(1)}, f32[4,4,4,1,128]{4,3,2,1,0:T(1,128)S(1)}, u32[]{:S(2)}, u32[]{:S(2)}) collective-permute-start(f32[4,4,4,1,128]{4,3,2,1,0:T(1,128)S(1)} %get-tuple-element.7), channel_id=1, source_target_pairs={{1,0},{3,2},{5,4},{7,6},{9,8},{11,10},{13,12},{15,14},{17,16},{19,... | collective-permute-start | bytes 98312 | tf_op jit(solution)/shard_map/ppermute | solution.py:24
  75.6 14.3 %copy-start.13 = (f32[148]{0:T(256)S(1)}, f32[148]{0:T(256)}, u32[]{:S(2)}) copy-start(f32[148]{0:T(256)} %and_convert_fusion.3) | copy-start | bytes 1780
  75.7 14.2 %collective-permute-start.10 = (f32[36,36,12]{1,2,0:T(8,128)S(1)}, f32[36,36,12]{1,2,0:T(8,128)S(1)}, u32[]{:S(2)}, u32[]{:S(2)}) collective-permute-start(f32[36,36,12]{1,2,0:T(8,128)S(1)} %slice.121), channel_id=1, source_target_pairs={{0,1},{2,3},{4,5},{6,7},{8,9},{10,11},{12,13},{14,15},{16,17},{18,... | collective-permute-start | bytes 186632 | tf_op jit(solution)/shard_map/ppermute | solution.py:173
  79.0 10.8 %collective-permute-start.11 = (f32[36,36,11]{1,2,0:T(8,128)S(1)}, f32[36,36,11]{1,2,0:T(8,128)S(1)}, u32[]{:S(2)}, u32[]{:S(2)}) collective-permute-start(f32[36,36,11]{1,2,0:T(8,128)S(1)} %slice.122), channel_id=1, source_target_pairs={{1,0},{3,2},{5,4},{7,6},{9,8},{11,10},{13,12},{15,14},{17,16},{19,... | collective-permute-start | bytes 171080 | tf_op jit(solution)/shard_map/ppermute | solution.py:174
  92.0 3.5 %copy-start.10 = (s32[8]{0:T(128)S(1)}, s32[8]{0:T(128)}, u32[]{:S(2)}) copy-start(s32[8]{0:T(128)} %iota_multiply_fusion.1) | copy-start | bytes 100
  95.5 1.3 copy-start.16
  95.5 1.3 copy-start.17
  95.5 4.1 %copy-start.14 = (f32[18]{0:T(128)S(1)}, f32[18]{0:T(128)}, u32[]{:S(2)}) copy-start(f32[18]{0:T(128)} %convert_add_fusion) | copy-start | bytes 220
  97.1 2.7 %collective-permute-start.12 = (f32[8,8,64]{2,1,0:T(8,128)S(1)}, f32[8,8,64]{2,1,0:T(8,128)S(1)}, u32[]{:S(2)}, u32[]{:S(2)}) collective-permute-start(f32[8,8,64]{2,1,0:T(8,128)S(1)} %fusion.33), channel_id=1, source_target_pairs={{0,8},{8,16},{16,24},{1,9},{9,17},{17,25},{2,10},{10,18},{18,26},{... | collective-permute-start | bytes 49160 | tf_op jit(solution)/shard_map/ppermute | solution.py:23
  98.4 3.1 %collective-permute-start.13 = (f32[8,8,64]{2,1,0:T(8,128)S(1)}, f32[8,8,64]{2,1,0:T(8,128)S(1)}, u32[]{:S(2)}, u32[]{:S(2)}) collective-permute-start(f32[8,8,64]{2,1,0:T(8,128)S(1)} %fusion.33), channel_id=1, source_target_pairs={{8,0},{16,8},{24,16},{9,1},{17,9},{25,17},{10,2},{18,10},{26,18},{... | collective-permute-start | bytes 49160 | tf_op jit(solution)/shard_map/ppermute | solution.py:24
  101.5 4.7 %collective-permute-start.14 = (f32[24,8,64]{2,1,0:T(8,128)S(1)}, f32[24,8,64]{2,1,0:T(8,128)S(1)}, u32[]{:S(2)}, u32[]{:S(2)}) collective-permute-start(f32[24,8,64]{2,1,0:T(8,128)S(1)} %pad_maximum_fusion.6), channel_id=1, source_target_pairs={{0,2},{2,4},{4,6},{1,3},{3,5},{5,7},{8,10},{10,12},{12,14},{9,11},... | collective-permute-start | bytes 147464 | tf_op jit(solution)/shard_map/ppermute | solution.py:23
  104.0 6.6 %collective-permute-start.15 = (f32[24,8,64]{2,1,0:T(8,128)S(1)}, f32[24,8,64]{2,1,0:T(8,128)S(1)}, u32[]{:S(2)}, u32[]{:S(2)}) collective-permute-start(f32[24,8,64]{2,1,0:T(8,128)S(1)} %pad_maximum_fusion.6), channel_id=1, source_target_pairs={{2,0},{4,2},{6,4},{3,1},{5,3},{7,5},{10,8},{12,10},{14,12},{11,9},... | collective-permute-start | bytes 147464 | tf_op jit(solution)/shard_map/ppermute | solution.py:24
  105.3 8.5 %copy-start.2 = (s32[2,2,16,128]{3,2,1,0:T(8,128)S(1)}, s32[2,2,16,128]{3,2,1,0:T(8,128)}, u32[]{:S(2)}) copy-start(s32[2,2,16,128]{3,2,1,0:T(8,128)} %partners_ref.1) | copy-start | bytes 98308
  110.8 89.2 %collective-permute-start.16 = (f32[24,24,8]{2,1,0:T(8,128)S(1)}, f32[24,24,8]{2,1,0:T(8,128)S(1)}, u32[]{:S(2)}, u32[]{:S(2)}) collective-permute-start(f32[24,24,8]{2,1,0:T(8,128)S(1)} %get-tuple-element.8), channel_id=1, source_target_pairs={{0,1},{2,3},{4,5},{6,7},{8,9},{10,11},{12,13},{14,15},{16,17},{18,... | collective-permute-start | bytes 55304 | tf_op jit(solution)/shard_map/ppermute | solution.py:23
  112.3 87.7 %collective-permute-start.17 = (f32[24,24,8]{2,1,0:T(8,128)S(1)}, f32[24,24,8]{2,1,0:T(8,128)S(1)}, u32[]{:S(2)}, u32[]{:S(2)}) collective-permute-start(f32[24,24,8]{2,1,0:T(8,128)S(1)} %get-tuple-element.9), channel_id=1, source_target_pairs={{1,0},{3,2},{5,4},{7,6},{9,8},{11,10},{13,12},{15,14},{17,16},{19,... | collective-permute-start | bytes 55304 | tf_op jit(solution)/shard_map/ppermute | solution.py:24
  201.0 9.1 %collective-permute-start.18 = (f32[2,8,64]{2,1,0:T(8,128)S(1)}, f32[2,8,64]{2,1,0:T(8,128)S(1)}, u32[]{:S(2)}, u32[]{:S(2)}) collective-permute-start(f32[2,8,64]{2,1,0:T(8,128)S(1)} %get-tuple-element.18), channel_id=1, source_target_pairs={{0,8},{8,16},{16,24},{1,9},{9,17},{17,25},{2,10},{10,18},{18,26},{... | collective-permute-start | bytes 12296 | tf_op jit(solution)/shard_map/ppermute | solution.py:23
  207.9 3.1 %collective-permute-start.19 = (f32[2,8,64]{2,1,0:T(8,128)S(1)}, f32[2,8,64]{2,1,0:T(8,128)S(1)}, u32[]{:S(2)}, u32[]{:S(2)}) collective-permute-start(f32[2,8,64]{2,1,0:T(8,128)S(1)} %get-tuple-element.19), channel_id=1, source_target_pairs={{8,0},{16,8},{24,16},{9,1},{17,9},{25,17},{10,2},{18,10},{26,18},{... | collective-permute-start | bytes 12296 | tf_op jit(solution)/shard_map/ppermute | solution.py:24
  210.9 3.4 %collective-permute-start.20 = (f32[12,2,64]{2,1,0:T(2,128)S(1)}, f32[12,2,64]{2,1,0:T(2,128)S(1)}, u32[]{:S(2)}, u32[]{:S(2)}) collective-permute-start(f32[12,2,64]{2,1,0:T(2,128)S(1)} %get-tuple-element.16), channel_id=1, source_target_pairs={{0,2},{2,4},{4,6},{1,3},{3,5},{5,7},{8,10},{10,12},{12,14},{9,11},... | collective-permute-start | bytes 18440 | tf_op jit(solution)/shard_map/ppermute | solution.py:23
  212.2 5.6 %collective-permute-start.21 = (f32[12,2,64]{2,1,0:T(2,128)S(1)}, f32[12,2,64]{2,1,0:T(2,128)S(1)}, u32[]{:S(2)}, u32[]{:S(2)}) collective-permute-start(f32[12,2,64]{2,1,0:T(2,128)S(1)} %get-tuple-element.17), channel_id=1, source_target_pairs={{2,0},{4,2},{6,4},{3,1},{5,3},{7,5},{10,8},{12,10},{14,12},{11,9},... | collective-permute-start | bytes 18440 | tf_op jit(solution)/shard_map/ppermute | solution.py:24
  218.0 9.7 %copy-start.12 = (s32[132]{0:T(256)S(1)}, s32[132]{0:T(256)}, u32[]{:S(2)}) copy-start(s32[132]{0:T(256)} %iota_add_fusion) | copy-start | bytes 1588
  218.0 9.7 %copy-start.15 = (s32[68]{0:T(128)S(1)}, s32[68]{0:T(128)}, u32[]{:S(2)}) copy-start(s32[68]{0:T(128)} %add_multiply_fusion) | copy-start | bytes 820
  218.0 4.4 %collective-permute-start.22 = (f32[12,12,2]{2,1,0:T(8,128)S(1)}, f32[12,12,2]{2,1,0:T(8,128)S(1)}, u32[]{:S(2)}, u32[]{:S(2)}) collective-permute-start(f32[12,12,2]{2,1,0:T(8,128)S(1)} %get-tuple-element.14), channel_id=1, source_target_pairs={{0,1},{2,3},{4,5},{6,7},{8,9},{10,11},{12,13},{14,15},{16,17},{18,... | collective-permute-start | bytes 3464 | tf_op jit(solution)/shard_map/ppermute | solution.py:23
  219.3 7.4 %collective-permute-start.23 = (f32[12,12,2]{2,1,0:T(8,128)S(1)}, f32[12,12,2]{2,1,0:T(8,128)S(1)}, u32[]{:S(2)}, u32[]{:S(2)}) collective-permute-start(f32[12,12,2]{2,1,0:T(8,128)S(1)} %get-tuple-element.15), channel_id=1, source_target_pairs={{1,0},{3,2},{5,4},{7,6},{9,8},{11,10},{13,12},{15,14},{17,16},{19,... | collective-permute-start | bytes 3464 | tf_op jit(solution)/shard_map/ppermute | solution.py:24

commit v3 on v2

--- a/solution.py
+++ b/solution.py
@@ -186,6 +186,20 @@
     return value
 
 
+def coarse_halo(value, sides, known, depth):
+    for axis, dim in sides:
+        size, length = (lax.axis_size(axis), value.shape[dim] - 2 * known - 1)
+        up = [(i, (i + 1) % size) for i in range(size - 1)]
+        down = [(j, i) for i, j in up]
+        start = length - depth + known
+        last = lax.slice_in_dim(value, start, start + depth - known, axis=dim)
+        initial = lax.slice_in_dim(value, 2 * known + 1, depth + known, axis=dim)
+        before = lax.ppermute(last, axis, up)
+        after = lax.ppermute(initial, axis, down)
+        value = jnp.concatenate([before, value, after], axis=dim)
+    return value
+
+
 def kernel_band(in_length, spread):
     row_index = jnp.arange(in_length)[:, None]
     column_index = jnp.arange(in_length - 16)[None, :]
@@ -252,7 +266,6 @@
                         reach = jnp.maximum(1.0 - distance_sq, 0.0)
                         below = 1.015625 - reach
                         inverse = pl.reciprocal(below, approx=True)
-                        inverse = inverse * (2.0 - below * inverse)
                         strength = (reach * reach) * (reach * near[3]) * inverse
                         total = [total[d] + strength * gap[d] for d in range(3)]
             for d in range(3):
@@ -318,21 +331,28 @@
     lengths = (grid_x, grid_y, grid_z)
     halo_depth = 10
     spread = spread_charge(offsets, weighted)
-    widened = spread_halo(spread, (("gx", 0), ("gy", 1), ("ga", 2)), halo_depth)
+    widened = spread_halo(spread, (("ga", 2), ("gx", 0), ("gy", 1)), halo_depth)
     widened = widened * inside_mask(lengths, halo_depth)
     fine_potential = convolve(widened, fine_spread, fine_scale)
+    known, coarse_depth = ((halo_depth - 1) // 2, 10)
+    coarse_lengths = tuple(length // 2 for length in lengths)
     coarse_charge = widened
-    for where_axis, fine_length in enumerate((grid_x, grid_y, grid_z)):
+    for where_axis, fine_length in enumerate(lengths):
         coarse_charge = along_axis(
             coarse_charge,
-            grid_map(fine_length + 2 * halo_depth, fine_length // 2, -halo_depth, 0),
+            grid_map(
+                fine_length + 2 * halo_depth,
+                fine_length // 2 + 2 * known + 1,
+                -halo_depth,
+                -known,
+            ),
             where_axis,
         )
-    grown_coarse = padded_2(coarse_charge, (("gx", 0), ("gy", 1), ("ga", 2)), 8)
-    coarse_potential = convolve(grown_coarse, coarse_spread, coarse_scale)
-    coarse_near = padded_2(coarse_potential, (("gx", 0), ("gy", 1), ("ga", 2)), 2)
-    potential = coarse_near
-    for where_axis, fine_length in enumerate((grid_x, grid_y, grid_z)):
+    grown_coarse = coarse_halo(coarse_charge, (("ga", 2), ("gx", 0), ("gy", 1)), known, coarse_depth)
+    grown_coarse = grown_coarse * inside_mask(coarse_lengths, coarse_depth)
+    potential = convolve(grown_coarse, coarse_spread, coarse_scale)
+    potential = potential * inside_mask(coarse_lengths, 2)
+    for where_axis, fine_length in enumerate(lengths):
         potential = along_axis(
             potential,
             jnp.transpose(grid_map(fine_length + 4, fine_length // 2 + 4, -2, -2)),

time: 242 us -> 215 us (0.89)
  waiting for transfers between devices: 31.6 us -> 17.7 us
  Pallas kernels: 102 us -> 91.6 us
  starting transfers between devices: 54.3 us -> 48.3 us
    ppermute x0 -> x6, starting transfers between devices: none -> 17.3 us  [the longest x3 13.2 us: coarse_halo(): before = lax.ppermute(last, axis, up)]
    ppermute x9 -> x3, starting transfers between devices: 26.6 us -> 9.5 us  [padded_2(): before = lax.ppermute(last, axis, up)]
    ppermute x3, waiting for transfers between devices: 15.7 us -> 0.01 us  [spread_halo(): after = lax.ppermute(initial, axis, down)]
    ppermute x0 -> x6, waiting for transfers between devices: none -> 15.7 us  [the longest x3 15.7 us: coarse_halo(): after = lax.ppermute(initial, axis, down)]
    ppermute x9 -> x3, waiting for transfers between devices: 14.7 us -> 1.96 us  [padded_2(): after = lax.ppermute(initial, axis, down)]
    pallas_call x1, Pallas kernels: 86.3 us -> 75.9 us  [short_forces(): pl.pallas_call(short_kernel, out_shape=jax.ShapeDtypeStruct((3,) + cells...]
    ppermute x9 -> x3, starting transfers between devices: 11.8 us -> 3.88 us  [padded_2(): after = lax.ppermute(initial, axis, down)]
    mul x1, other arithmetic: 2.12 us -> 5.85 us  [per_device(): widened = widened * inside_mask(lengths, halo_depth)]
  transfers between devices with their start and end apart: 24 -> 18, of which waited for: 9 -> 4; matrix products, arithmetic and copies ran while one was open for 15% -> 14% of each run, Pallas kernels for 36% -> 36%
where the time goes in v3:
time: 215 us; the launch traced here: 212 us
  Pallas kernels  91.6 us (43%)
  starting transfers between devices  48.3 us (22%)
  local copies, waits for them, and re-layouts  25 us (12%)
  other arithmetic  19.7 us (9%)
  waiting for transfers between devices  17.7 us (8%)
  matrix products  8.81 us (4%)
    pallas_call x1, Pallas kernels, short_forces(): pl.pallas_call(short_kernel, out_shape=jax.ShapeDtypeStruct((3,) + cells...  75.9 us
    ppermute x3, waiting for transfers between devices, coarse_halo(): after = lax.ppermute(initial, axis, down)  15.7 us
    ppermute x3, starting transfers between devices, spread_halo(): before = lax.ppermute(last, axis, up)  13.8 us
    ppermute x3, starting transfers between devices, coarse_halo(): before = lax.ppermute(last, axis, up)  13.2 us
    ppermute x3, starting transfers between devices, padded_2(): before = lax.ppermute(last, axis, up)  9.5 us
    dot_general x12, matrix products, along_axis(): jnp.tensordot(values, matrix, axes=([where_axis], [0]), precision=highest)  8.81 us
    pallas_call x1, Pallas kernels, grid_forces(): pl.pallas_call(gather_kernel, out_shape=jax.ShapeDtypeStruct(offsets.shap...  7.92 us
    pallas_call x1, Pallas kernels, spread_charge(): pl.pallas_call(spread_kernel, out_shape=jax.ShapeDtypeStruct((8 * cells_x...  7.71 us
  transfers between devices with their start and end apart: 18, of which 4 were waited for; matrix products, arithmetic and copies ran while one was open for 14% of the time, Pallas kernels for 36%

profile of v3, /device:TPU:0, one launch (start us, length us, event | category | flops | bytes accessed | tf_op | source)
XLA Modules:
  0.0 212.4 jit_solution(1978362593857646200)
XLA Ops:
  0.6 0.8 fusion.63.weighted_ref
  1.5 0.9 copy-done
  2.4 7.7 %shard_map.60 = f32[19,136,32]{2,1,0:T(8,128)S(1)} custom-call(f32[3,2,2,16,128]{4,3,2,1,0:T(8,128)S(1)} %copy-done, f32[2,2,16,128]{3,2,1,0:T(8,128)S(1)} %fusion.63.weighted_ref), custom_call_target="tpu_custom_call" | custom-call | flops 100000000 | bytes 4000000 | tf_op jit(solution)/shard_map/pallas_call | solution.py:94
  10.2 4.9 %collective-permute-start.6 = (f32[19,19,12]{1,2,0:T(8,128)S(1)}, f32[19,19,12]{1,2,0:T(8,128)S(1)}, u32[]{:S(2)}, u32[]{:S(2)}) collective-permute-start(f32[19,19,12]{1,2,0:T(8,128)S(1)} %slice.109), channel_id=1, source_target_pairs={{0,1},{2,3},{4,5},{6,7},{8,9},{10,11},{12,13},{14,15},{16,17},{18,... | collective-permute-start | bytes 51992 | tf_op jit(solution)/shard_map/ppermute | solution.py:173
  15.1 1.3 collective-permute-start.7
  16.5 1.5 collective-permute-start
  18.0 1.3 collective-permute-start.1
  19.8 0.6 iota_add_fusion.2
  25.7 1.1 copy-done.3
  27.3 4.6 %collective-permute-start.8 = (f32[12,19,148]{2,1,0:T(8,128)S(1)}, f32[12,19,148]{2,1,0:T(8,128)S(1)}, u32[]{:S(2)}, u32[]{:S(2)}) collective-permute-start(f32[12,19,148]{2,1,0:T(8,128)S(1)} %copy.18), channel_id=1, source_target_pairs={{0,8},{8,16},{16,24},{1,9},{9,17},{17,25},{2,10},{10,18},{18,26},{... | collective-permute-start | bytes 404936 | tf_op jit(solution)/shard_map/ppermute | solution.py:173
  32.4 1.3 collective-permute-start.9
  33.8 3.5 %collective-permute-start.2 = (f32[4,4,1,16,128]{4,3,2,1,0:T(8,128)S(1)}, f32[4,4,1,16,128]{4,3,2,1,0:T(8,128)S(1)}, u32[]{:S(2)}, u32[]{:S(2)}) collective-permute-start(f32[4,4,1,16,128]{4,3,2,1,0:T(8,128)S(1)} %get-tuple-element.8), channel_id=1, source_target_pairs={{0,2},{2,4},{4,6},{1,3},{3,5},{5,7},{8,10},{10,12},{12,14},{9,11},... | collective-permute-start | bytes 393224 | tf_op jit(solution)/shard_map/ppermute | solution.py:23
  37.3 1.3 collective-permute-start.3
  39.9 1.2 copy.21
  41.2 1.3 copy.19
  42.5 2.0 collective-permute-done.3
  44.5 4.6 %collective-permute-start.4 = (f32[4,4,4,1,128]{4,3,2,1,0:T(1,128)S(1)}, f32[4,4,4,1,128]{4,3,2,1,0:T(1,128)S(1)}, u32[]{:S(2)}, u32[]{:S(2)}) collective-permute-start(f32[4,4,4,1,128]{4,3,2,1,0:T(1,128)S(1)} %get-tuple-element.6), channel_id=1, source_target_pairs={{0,1},{2,3},{4,5},{6,7},{8,9},{10,11},{12,13},{14,15},{16,17},{18,... | collective-permute-start | bytes 98312 | tf_op jit(solution)/shard_map/ppermute | solution.py:23
  49.1 1.3 collective-permute-start.5
  50.4 2.1 %pad_add_fusion = f32[36,19,148]{1,2,0:T(8,128)S(1)} fusion(f32[11,19,148]{1,2,0:T(8,128)} %copy.21, f32[12,19,148]{1,2,0:T(8,128)} %copy.19, f32[19,19,148]{1,2,0:T(8,128)} %copy-done.3), kind=kLoop, calls=%fused_computation.1 | loop fusion | flops 202464 | bytes 877344 | tf_op jit(solution)/shard_map/add | solution.py:182
  52.5 2.3 %slice.113 = f32[36,12,148]{1,2,0:T(8,128)} slice(f32[36,19,148]{1,2,0:T(8,128)S(1)} %pad_add_fusion), slice={[0:36], [7:19], [0:148]} | slice | bytes 511488 | tf_op jit(solution)/shard_map/slice | solution.py:171
  54.8 4.0 %copy.22 = f32[36,12,148]{2,0,1:T(8,128)} copy(f32[36,12,148]{1,2,0:T(8,128)} %slice.113) | data formatting | bytes 511488 | tf_op jit(solution)/shard_map/slice | solution.py:171
  58.9 4.3 %collective-permute-start.10 = (f32[36,12,148]{2,0,1:T(8,128)}, f32[36,12,148]{2,0,1:T(8,128)}, u32[]{:S(2)}, u32[]{:S(2)}) collective-permute-start(f32[36,12,148]{2,0,1:T(8,128)} %copy.22), channel_id=1, source_target_pairs={{0,2},{2,4},{4,6},{1,3},{3,5},{5,7},{8,10},{10,12},{12,14},{9,11},... | collective-permute-start | bytes 767240 | tf_op jit(solution)/shard_map/ppermute | solution.py:173
  63.1 2.5 %copy.24 = f32[36,11,148]{2,0,1:T(8,128)} copy(f32[36,11,148]{1,2,0:T(8,128)S(1)} %bitcast.51) | data formatting | bytes 468864 | tf_op jit(solution)/shard_map/slice | solution.py:172
  65.6 1.3 collective-permute-start.11
  67.1 0.8 slice_add_fusion.3
  68.0 75.9 %shard_map.59 = f32[3,2,2,16,128]{4,3,2,1,0:T(8,128)} custom-call(s32[64]{0:T(128)S(1)} %reshape.310.counts_ref, f32[4,4,4,18,128]{4,3,2,1,0:T(8,128)S(1)} %pad_maximum_fusion.2.grown_ref, s32[2,2,16,128]{3,2,1,0:T(8,128)S(1)} %copy-done.2), custom_call_target="tpu_custom_call" | custom-call | flops 1000000000 | bytes 10000000 | tf_op jit(solution)/shard_map/pallas_call | solution.py:293
  143.9 3.2 %copy.25 = f32[36,11,148]{1,2,0:T(8,128)} copy(f32[36,11,148]{2,0,1:T(8,128)} %collective-permute-done.11) | data formatting | bytes 468864 | tf_op jit(solution)/shard_map/ppermute | solution.py:174
  147.1 3.2 %copy.23 = f32[36,12,148]{1,2,0:T(8,128)} copy(f32[36,12,148]{2,0,1:T(8,128)} %collective-permute-done.10) | data formatting | bytes 511488 | tf_op jit(solution)/shard_map/ppermute | solution.py:173
  150.3 5.9 %multiply_multiply_fusion = f32[36,36,148]{1,2,0:T(8,128)} fusion(f32[36,11,148]{1,2,0:T(8,128)} %copy.25, f32[36,12,148]{1,2,0:T(8,128)} %copy.23, f32[36,19,148]{1,2,0:T(8,128)S(1)} %pad_add_fusion, f32[148]{0:T(256)S(1)} %copy-done.12, f32[36,36]{1,0:T(8,128)S(1)} %broadcast_multiply_fusion), kind=kLoop, calls=%fused_computation | loop fusion | flops 767232 | bytes 1668112 | tf_op jit(solution)/shard_map/mul | solution.py:335
  156.2 3.5 %copy.26 = f32[36,36,148]{2,0,1:T(8,128)S(1)} copy(f32[36,36,148]{1,2,0:T(8,128)} %multiply_multiply_fusion) | data formatting | bytes 1534464 | tf_op jit(solution)/shard_map/mul | solution.py:335
  159.7 1.0 fusion.74
  160.7 0.7 convolution_bitcast_fusion.1
  162.3 5.7 %collective-permute-start.12 = (f32[17,17,6]{2,1,0:T(8,128)S(1)}, f32[17,17,6]{2,1,0:T(8,128)S(1)}, u32[]{:S(2)}, u32[]{:S(2)}) collective-permute-start(f32[17,17,6]{2,1,0:T(8,128)S(1)} %slice.115), channel_id=1, source_target_pairs={{0,1},{2,3},{4,5},{6,7},{8,9},{10,11},{12,13},{14,15},{16,17},{18,... | collective-permute-start | bytes 20816 | tf_op jit(solution)/shard_map/ppermute | solution.py:197
  168.0 1.5 collective-permute-start.13
  169.4 0.9 fusion.77
  170.4 5.3 %collective-permute-done.13 = f32[17,17,5]{2,1,0:T(8,128)S(1)} collective-permute-done((f32[17,17,5]{2,1,0:T(8,128)S(1)}, f32[17,17,5]{2,1,0:T(8,128)S(1)}, u32[]{:S(2)}, u32[]{:S(2)}) %collective-permute-start.13) | collective-permute-done | bytes 5812 | tf_op jit(solution)/shard_map/ppermute | solution.py:198
  175.8 1.3 collective-permute-start.14
  177.2 1.3 collective-permute-start.15
  178.5 0.8 convolution_bitcast_fusion
  179.3 6.4 %collective-permute-done.15 = f32[5,17,84]{2,1,0:T(8,128)S(1)} collective-permute-done((f32[5,17,84]{2,1,0:T(8,128)S(1)}, f32[5,17,84]{2,1,0:T(8,128)S(1)}, u32[]{:S(2)}, u32[]{:S(2)}) %collective-permute-start.15) | collective-permute-done | bytes 28592 | tf_op jit(solution)/shard_map/ppermute | solution.py:198
  185.8 6.3 %collective-permute-start.16 = (f32[28,6,84]{2,1,0:T(8,128)S(1)}, f32[28,6,84]{2,1,0:T(8,128)S(1)}, u32[]{:S(2)}, u32[]{:S(2)}) collective-permute-start(f32[28,6,84]{2,1,0:T(8,128)S(1)} %pad_maximum_fusion.8), channel_id=1, source_target_pairs={{0,2},{2,4},{4,6},{1,3},{3,5},{5,7},{8,10},{10,12},{12,14},{9,11},... | collective-permute-start | bytes 169352 | tf_op jit(solution)/shard_map/ppermute | solution.py:197
  192.2 1.3 collective-permute-start.17
  193.5 1.4 fusion.13
  195.0 4.0 %collective-permute-done.17 = f32[28,5,84]{2,1,0:T(8,128)S(1)} collective-permute-done((f32[28,5,84]{2,1,0:T(8,128)S(1)}, f32[28,5,84]{2,1,0:T(8,128)S(1)}, u32[]{:S(2)}, u32[]{:S(2)}) %collective-permute-start.17) | collective-permute-done | bytes 47072 | tf_op jit(solution)/shard_map/ppermute | solution.py:198
  201.4 1.4 fusion.29
  202.8 0.8 fusion.1
  203.7 0.7 pad_maximum_fusion.grid_ref
  204.5 7.9 %shard_map.61 = f32[3,2,2,16,128]{4,3,2,1,0:T(8,128)} custom-call(f32[3,2,2,16,128]{4,3,2,1,0:T(8,128)S(1)} %copy-done.1, f32[2,2,16,128]{3,2,1,0:T(8,128)S(1)} %fusion.63.weighted_ref, f32[19,136,96]{2,1,0:T(8,128)S(1)} %pad_maximum_fusion.grid_ref), custom_call_target="tpu_custom_call" | custom-call | flops 100000000 | bytes 4000000 | tf_op jit(solution)/shard_map/pallas_call | solution.py:156
  (99 shorter events, 12.3 us)
Async XLA Ops:
  1.5 0.9 copy-start
  10.1 6.3 %copy-start.4 = (f32[2,2,16,128]{3,2,1,0:T(8,128)S(1)}, f32[2,2,16,128]{3,2,1,0:T(8,128)}, u32[]{:S(2)}) copy-start(f32[2,2,16,128]{3,2,1,0:T(8,128)} %param.5) | copy-start | bytes 98308
  10.1 6.3 %copy-start.5 = (s32[2,2,16]{2,1,0:T(2,128)S(1)}, s32[2,2,16]{2,1,0:T(2,128)}, u32[]{:S(2)}) copy-start(s32[2,2,16]{2,1,0:T(2,128)} %param.6) | copy-start | bytes 772
  10.2 15.2 %collective-permute-start.6 = (f32[19,19,12]{1,2,0:T(8,128)S(1)}, f32[19,19,12]{1,2,0:T(8,128)S(1)}, u32[]{:S(2)}, u32[]{:S(2)}) collective-permute-start(f32[19,19,12]{1,2,0:T(8,128)S(1)} %slice.109), channel_id=1, source_target_pairs={{0,1},{2,3},{4,5},{6,7},{8,9},{10,11},{12,13},{14,15},{16,17},{18,... | collective-permute-start | bytes 51992 | tf_op jit(solution)/shard_map/ppermute | solution.py:173
  15.1 10.3 %collective-permute-start.7 = (f32[19,19,11]{1,2,0:T(8,128)S(1)}, f32[19,19,11]{1,2,0:T(8,128)S(1)}, u32[]{:S(2)}, u32[]{:S(2)}) collective-permute-start(f32[19,19,11]{1,2,0:T(8,128)S(1)} %slice.110), channel_id=1, source_target_pairs={{1,0},{3,2},{5,4},{7,6},{9,8},{11,10},{13,12},{15,14},{17,16},{19,... | collective-permute-start | bytes 47660 | tf_op jit(solution)/shard_map/ppermute | solution.py:174
  16.5 17.2 %collective-permute-start = (f32[4,1,2,16,128]{4,3,2,1,0:T(8,128)S(1)}, f32[4,1,2,16,128]{4,3,2,1,0:T(8,128)S(1)}, u32[]{:S(2)}, u32[]{:S(2)}) collective-permute-start(f32[4,1,2,16,128]{4,3,2,1,0:T(8,128)S(1)} %get-tuple-element.10), channel_id=1, source_target_pairs={{0,8},{8,16},{16,24},{1,9},{9,17},{17,25},{2,10},{10,18},{18,26},{... | collective-permute-start | bytes 196616 | tf_op jit(solution)/shard_map/ppermute | solution.py:23
  18.0 15.7 %collective-permute-start.1 = (f32[4,1,2,16,128]{4,3,2,1,0:T(8,128)S(1)}, f32[4,1,2,16,128]{4,3,2,1,0:T(8,128)S(1)}, u32[]{:S(2)}, u32[]{:S(2)}) collective-permute-start(f32[4,1,2,16,128]{4,3,2,1,0:T(8,128)S(1)} %get-tuple-element.11), channel_id=1, source_target_pairs={{8,0},{16,8},{24,16},{9,1},{17,9},{25,17},{10,2},{18,10},{26,18},{... | collective-permute-start | bytes 196616 | tf_op jit(solution)/shard_map/ppermute | solution.py:24
  25.6 1.1 copy-start.3
  26.8 6.9 %copy-start.1 = (f32[3,2,2,16,128]{4,3,2,1,0:T(8,128)S(1)}, f32[3,2,2,16,128]{4,3,2,1,0:T(8,128)}, u32[]{:S(2)}) copy-start(f32[3,2,2,16,128]{4,3,2,1,0:T(8,128)} %offsets_ref.3) | copy-start | bytes 294916
  27.3 13.8 %collective-permute-start.8 = (f32[12,19,148]{2,1,0:T(8,128)S(1)}, f32[12,19,148]{2,1,0:T(8,128)S(1)}, u32[]{:S(2)}, u32[]{:S(2)}) collective-permute-start(f32[12,19,148]{2,1,0:T(8,128)S(1)} %copy.18), channel_id=1, source_target_pairs={{0,8},{8,16},{16,24},{1,9},{9,17},{17,25},{2,10},{10,18},{18,26},{... | collective-permute-start | bytes 404936 | tf_op jit(solution)/shard_map/ppermute | solution.py:173
  32.4 7.5 %collective-permute-start.9 = (f32[11,19,148]{2,1,0:T(8,128)S(1)}, f32[11,19,148]{2,1,0:T(8,128)S(1)}, u32[]{:S(2)}, u32[]{:S(2)}) collective-permute-start(f32[11,19,148]{2,1,0:T(8,128)S(1)} %copy.20), channel_id=1, source_target_pairs={{8,0},{16,8},{24,16},{9,1},{17,9},{25,17},{10,2},{18,10},{26,18},{... | collective-permute-start | bytes 371192 | tf_op jit(solution)/shard_map/ppermute | solution.py:174
  33.8 8.7 %collective-permute-start.2 = (f32[4,4,1,16,128]{4,3,2,1,0:T(8,128)S(1)}, f32[4,4,1,16,128]{4,3,2,1,0:T(8,128)S(1)}, u32[]{:S(2)}, u32[]{:S(2)}) collective-permute-start(f32[4,4,1,16,128]{4,3,2,1,0:T(8,128)S(1)} %get-tuple-element.8), channel_id=1, source_target_pairs={{0,2},{2,4},{4,6},{1,3},{3,5},{5,7},{8,10},{10,12},{12,14},{9,11},... | collective-permute-start | bytes 393224 | tf_op jit(solution)/shard_map/ppermute | solution.py:23
  37.3 7.2 %collective-permute-start.3 = (f32[4,4,1,16,128]{4,3,2,1,0:T(8,128)S(1)}, f32[4,4,1,16,128]{4,3,2,1,0:T(8,128)S(1)}, u32[]{:S(2)}, u32[]{:S(2)}) collective-permute-start(f32[4,4,1,16,128]{4,3,2,1,0:T(8,128)S(1)} %get-tuple-element.9), channel_id=1, source_target_pairs={{2,0},{4,2},{6,4},{3,1},{5,3},{7,5},{10,8},{12,10},{14,12},{11,9},... | collective-permute-start | bytes 393224 | tf_op jit(solution)/shard_map/ppermute | solution.py:24
  44.5 22.4 %collective-permute-start.4 = (f32[4,4,4,1,128]{4,3,2,1,0:T(1,128)S(1)}, f32[4,4,4,1,128]{4,3,2,1,0:T(1,128)S(1)}, u32[]{:S(2)}, u32[]{:S(2)}) collective-permute-start(f32[4,4,4,1,128]{4,3,2,1,0:T(1,128)S(1)} %get-tuple-element.6), channel_id=1, source_target_pairs={{0,1},{2,3},{4,5},{6,7},{8,9},{10,11},{12,13},{14,15},{16,17},{18,... | collective-permute-start | bytes 98312 | tf_op jit(solution)/shard_map/ppermute | solution.py:23
  49.1 17.9 %collective-permute-start.5 = (f32[4,4,4,1,128]{4,3,2,1,0:T(1,128)S(1)}, f32[4,4,4,1,128]{4,3,2,1,0:T(1,128)S(1)}, u32[]{:S(2)}, u32[]{:S(2)}) collective-permute-start(f32[4,4,4,1,128]{4,3,2,1,0:T(1,128)S(1)} %get-tuple-element.7), channel_id=1, source_target_pairs={{1,0},{3,2},{5,4},{7,6},{9,8},{11,10},{13,12},{15,14},{17,16},{19,... | collective-permute-start | bytes 98312 | tf_op jit(solution)/shard_map/ppermute | solution.py:24
  58.9 88.2 %collective-permute-start.10 = (f32[36,12,148]{2,0,1:T(8,128)}, f32[36,12,148]{2,0,1:T(8,128)}, u32[]{:S(2)}, u32[]{:S(2)}) collective-permute-start(f32[36,12,148]{2,0,1:T(8,128)} %copy.22), channel_id=1, source_target_pairs={{0,2},{2,4},{4,6},{1,3},{3,5},{5,7},{8,10},{10,12},{12,14},{9,11},... | collective-permute-start | bytes 767240 | tf_op jit(solution)/shard_map/ppermute | solution.py:173
  65.6 78.3 %collective-permute-start.11 = (f32[36,11,148]{2,0,1:T(8,128)}, f32[36,11,148]{2,0,1:T(8,128)}, u32[]{:S(2)}, u32[]{:S(2)}) collective-permute-start(f32[36,11,148]{2,0,1:T(8,128)} %copy.24), channel_id=1, source_target_pairs={{2,0},{4,2},{6,4},{3,1},{5,3},{7,5},{10,8},{12,10},{14,12},{11,9},... | collective-permute-start | bytes 703304 | tf_op jit(solution)/shard_map/ppermute | solution.py:174
  67.1 0.9 copy-start.2
  147.1 3.2 %copy-start.12 = (f32[148]{0:T(256)S(1)}, f32[148]{0:T(256)}, u32[]{:S(2)}) copy-start(f32[148]{0:T(256)} %and_convert_fusion.9) | copy-start | bytes 1780
  156.2 3.5 %copy-start.8 = (s32[17]{0:T(128)S(1)}, s32[17]{0:T(128)}, u32[]{:S(2)}) copy-start(s32[17]{0:T(128)} %add_multiply_fusion.2) | copy-start | bytes 208
  156.2 3.5 %copy-start.9 = (s32[36]{0:T(128)S(1)}, s32[36]{0:T(128)}, u32[]{:S(2)}) copy-start(s32[36]{0:T(128)} %iota_add_fusion.2) | copy-start | bytes 436
  159.7 1.8 copy-start.10
  159.7 1.8 copy-start.16
  162.3 13.4 %collective-permute-start.12 = (f32[17,17,6]{2,1,0:T(8,128)S(1)}, f32[17,17,6]{2,1,0:T(8,128)S(1)}, u32[]{:S(2)}, u32[]{:S(2)}) collective-permute-start(f32[17,17,6]{2,1,0:T(8,128)S(1)} %slice.115), channel_id=1, source_target_pairs={{0,1},{2,3},{4,5},{6,7},{8,9},{10,11},{12,13},{14,15},{16,17},{18,... | collective-permute-start | bytes 20816 | tf_op jit(solution)/shard_map/ppermute | solution.py:197
  168.0 7.7 %collective-permute-start.13 = (f32[17,17,5]{2,1,0:T(8,128)S(1)}, f32[17,17,5]{2,1,0:T(8,128)S(1)}, u32[]{:S(2)}, u32[]{:S(2)}) collective-permute-start(f32[17,17,5]{2,1,0:T(8,128)S(1)} %slice.116), channel_id=1, source_target_pairs={{1,0},{3,2},{5,4},{7,6},{9,8},{11,10},{13,12},{15,14},{17,16},{19,... | collective-permute-start | bytes 17348 | tf_op jit(solution)/shard_map/ppermute | solution.py:198
  175.8 9.9 %collective-permute-start.14 = (f32[6,17,84]{2,1,0:T(8,128)S(1)}, f32[6,17,84]{2,1,0:T(8,128)S(1)}, u32[]{:S(2)}, u32[]{:S(2)}) collective-permute-start(f32[6,17,84]{2,1,0:T(8,128)S(1)} %pad_maximum_fusion.9), channel_id=1, source_target_pairs={{0,8},{8,16},{16,24},{1,9},{9,17},{17,25},{2,10},{10,18},{18,26},{... | collective-permute-start | bytes 102824 | tf_op jit(solution)/shard_map/ppermute | solution.py:197
  177.2 8.5 %collective-permute-start.15 = (f32[5,17,84]{2,1,0:T(8,128)S(1)}, f32[5,17,84]{2,1,0:T(8,128)S(1)}, u32[]{:S(2)}, u32[]{:S(2)}) collective-permute-start(f32[5,17,84]{2,1,0:T(8,128)S(1)} %pad_maximum_fusion.11), channel_id=1, source_target_pairs={{8,0},{16,8},{24,16},{9,1},{17,9},{25,17},{10,2},{18,10},{26,18},{... | collective-permute-start | bytes 85688 | tf_op jit(solution)/shard_map/ppermute | solution.py:198
  185.8 13.2 %copy-start.14 = (f32[84]{0:T(128)S(1)}, f32[84]{0:T(128)}, u32[]{:S(2)}) copy-start(f32[84]{0:T(128)} %and_convert_fusion.6) | copy-start | bytes 1012
  185.8 13.2 %collective-permute-start.16 = (f32[28,6,84]{2,1,0:T(8,128)S(1)}, f32[28,6,84]{2,1,0:T(8,128)S(1)}, u32[]{:S(2)}, u32[]{:S(2)}) collective-permute-start(f32[28,6,84]{2,1,0:T(8,128)S(1)} %pad_maximum_fusion.8), channel_id=1, source_target_pairs={{0,2},{2,4},{4,6},{1,3},{3,5},{5,7},{8,10},{10,12},{12,14},{9,11},... | collective-permute-start | bytes 169352 | tf_op jit(solution)/shard_map/ppermute | solution.py:197
  192.2 6.7 %collective-permute-start.17 = (f32[28,5,84]{2,1,0:T(8,128)S(1)}, f32[28,5,84]{2,1,0:T(8,128)S(1)}, u32[]{:S(2)}, u32[]{:S(2)}) collective-permute-start(f32[28,5,84]{2,1,0:T(8,128)S(1)} %pad_maximum_fusion.4), channel_id=1, source_target_pairs={{2,0},{4,2},{6,4},{3,1},{5,3},{7,5},{10,8},{12,10},{14,12},{11,9},... | collective-permute-start | bytes 141128 | tf_op jit(solution)/shard_map/ppermute | solution.py:198
  194.9 5.3 %copy-start.15 = (f32[68]{0:T(128)S(1)}, f32[68]{0:T(128)}, u32[]{:S(2)}) copy-start(f32[68]{0:T(128)} %and_convert_fusion.3) | copy-start | bytes 820
  195.0 5.5 %copy-start.6 = (s32[12]{0:T(128)S(1)}, s32[12]{0:T(128)}, u32[]{:S(2)}) copy-start(s32[12]{0:T(128)} %add_multiply_fusion.3) | copy-start | bytes 148
  195.0 5.5 %copy-start.7 = (s32[20]{0:T(128)S(1)}, s32[20]{0:T(128)}, u32[]{:S(2)}) copy-start(s32[20]{0:T(128)} %iota_add_fusion.3) | copy-start | bytes 244
  195.0 6.4 %copy-start.11 = (s32[132]{0:T(256)S(1)}, s32[132]{0:T(256)}, u32[]{:S(2)}) copy-start(s32[132]{0:T(256)} %iota_add_fusion) | copy-start | bytes 1588
  195.0 6.4 %copy-start.13 = (s32[68]{0:T(128)S(1)}, s32[68]{0:T(128)}, u32[]{:S(2)}) copy-start(s32[68]{0:T(128)} %add_multiply_fusion) | copy-start | bytes 820

commit v4 on v3

--- a/solution.py
+++ b/solution.py
@@ -237,9 +237,18 @@
     return jnp.stack(coordinates)
 
 
-def short_kernel(counts_ref, grown_ref, partners_ref, out_ref, own_s, acc_s):
+def short_kernel(counts_ref, grown_ref, partners_ref, out_ref, own_s, acc_s, near_s):
     _, cells_x, cells_y, cells_z, slots = out_ref.shape
     lane = lax.broadcasted_iota(jnp.int32, (1, slots), 1)
+
+    def fill_body(column, carry):
+        i, j = column // (cells_y + 2), column % (cells_y + 2)
+        for k in range(cells_z + 2):
+            for d in range(4):
+                near_s[i, j, k, d] = jnp.broadcast_to(grown_ref[d, i, j, k : k + 1, :], (8, slots))
+        return carry
+
+    lax.fori_loop(0, (cells_x + 2) * (cells_y + 2), fill_body, 0)
 
     def cell_body(cell, carry):
         i = cell // (cells_y * cells_z)
@@ -258,7 +267,7 @@
                 for step_y in range(3):
                     for step_z in range(3):
                         near = [
-                            grown_ref[d, i + step_x, j + step_y, pl.ds(k + step_z, 1), :]
+                            near_s[i + step_x, j + step_y, k + step_z, d]
                             for d in range(4)
                         ]
                         gap = [own[d] - near[d] for d in range(3)]
@@ -296,7 +305,8 @@
         in_specs=[pl.BlockSpec(memory_space=pltpu.SMEM)]
         + [pl.BlockSpec(memory_space=pltpu.VMEM)] * 2,
         out_specs=pl.BlockSpec(memory_space=pltpu.VMEM),
-        scratch_shapes=[pltpu.VMEM((3, slots, slots), jnp.float32)] * 2,
+        scratch_shapes=[pltpu.VMEM((3, slots, slots), jnp.float32)] * 2
+        + [pltpu.VMEM(grown.shape[1:4] + (4, 8, slots), jnp.float32)],
         compiler_params=pltpu.CompilerParams(vmem_limit_bytes=24 * 2**20),
         cost_estimate=pl.CostEstimate(flops=10**9, bytes_accessed=10**7, transcendentals=10**7),
     )(counts.reshape(-1), grown, partners)

time: 215 us -> 212 us (0.986)
  starting transfers between devices: 48.3 us -> 51.4 us
  waiting for transfers between devices: 17.7 us -> 14.8 us
  Pallas kernels: 91.6 us -> 89.1 us
    ppermute x3, starting transfers between devices: 13.2 us -> 16.3 us  [coarse_halo(): before = lax.ppermute(last, axis, up)]
    ppermute x3, waiting for transfers between devices: 15.7 us -> 12.8 us  [coarse_halo(): after = lax.ppermute(initial, axis, down)]
    pallas_call x1, Pallas kernels: 75.9 us -> 73.4 us  [short_forces(): pl.pallas_call(short_kernel, out_shape=jax.ShapeDtypeStruct((3,) + cells...]
  transfers between devices with their start and end apart: 18 -> 18, of which waited for: 4 -> 4; matrix products, arithmetic and copies ran while one was open for 14% -> 14% of each run, Pallas kernels for 36% -> 35%
where the time goes in v4:
time: 212 us; the launch traced here: 210 us
  Pallas kernels  89.1 us (42%)
  starting transfers between devices  51.4 us (24%)
  local copies, waits for them, and re-layouts  25 us (12%)
  other arithmetic  19.7 us (9%)
  waiting for transfers between devices  14.8 us (7%)
  matrix products  8.81 us (4%)
    pallas_call x1, Pallas kernels, short_forces(): pl.pallas_call(short_kernel, out_shape=jax.ShapeDtypeStruct((3,) + cells...  73.4 us
    ppermute x3, starting transfers between devices, coarse_halo(): before = lax.ppermute(last, axis, up)  16.3 us
    ppermute x3, starting transfers between devices, spread_halo(): before = lax.ppermute(last, axis, up)  13.8 us
    ppermute x3, waiting for transfers between devices, coarse_halo(): after = lax.ppermute(initial, axis, down)  12.8 us
    ppermute x3, starting transfers between devices, padded_2(): before = lax.ppermute(last, axis, up)  9.5 us
    dot_general x12, matrix products, along_axis(): jnp.tensordot(values, matrix, axes=([where_axis], [0]), precision=highest)  8.81 us
    pallas_call x1, Pallas kernels, grid_forces(): pl.pallas_call(gather_kernel, out_shape=jax.ShapeDtypeStruct(offsets.shap...  7.93 us
    pallas_call x1, Pallas kernels, spread_charge(): pl.pallas_call(spread_kernel, out_shape=jax.ShapeDtypeStruct((8 * cells_x...  7.71 us
  transfers between devices with their start and end apart: 18, of which 4 were waited for; matrix products, arithmetic and copies ran while one was open for 14% of the time, Pallas kernels for 35%

profile of v4, /device:TPU:0, one launch (start us, length us, event | category | flops | bytes accessed | tf_op | source)
XLA Modules:
  0.0 210.1 jit_solution(13208105432175206178)
XLA Ops:
  0.6 0.8 fusion.63.weighted_ref
  1.5 0.9 copy-done
  2.4 7.7 %shard_map.60 = f32[19,136,32]{2,1,0:T(8,128)S(1)} custom-call(f32[3,2,2,16,128]{4,3,2,1,0:T(8,128)S(1)} %copy-done, f32[2,2,16,128]{3,2,1,0:T(8,128)S(1)} %fusion.63.weighted_ref), custom_call_target="tpu_custom_call" | custom-call | flops 100000000 | bytes 4000000 | tf_op jit(solution)/shard_map/pallas_call | solution.py:94
  10.2 4.9 %collective-permute-start.6 = (f32[19,19,12]{1,2,0:T(8,128)S(1)}, f32[19,19,12]{1,2,0:T(8,128)S(1)}, u32[]{:S(2)}, u32[]{:S(2)}) collective-permute-start(f32[19,19,12]{1,2,0:T(8,128)S(1)} %slice.109), channel_id=1, source_target_pairs={{0,1},{2,3},{4,5},{6,7},{8,9},{10,11},{12,13},{14,15},{16,17},{18,... | collective-permute-start | bytes 51992 | tf_op jit(solution)/shard_map/ppermute | solution.py:173
  15.1 1.3 collective-permute-start.7
  16.5 1.5 collective-permute-start
  18.0 1.3 collective-permute-start.1
  19.8 0.6 iota_add_fusion.2
  25.7 1.1 copy-done.3
  27.3 4.6 %collective-permute-start.8 = (f32[12,19,148]{2,1,0:T(8,128)S(1)}, f32[12,19,148]{2,1,0:T(8,128)S(1)}, u32[]{:S(2)}, u32[]{:S(2)}) collective-permute-start(f32[12,19,148]{2,1,0:T(8,128)S(1)} %copy.18), channel_id=1, source_target_pairs={{0,8},{8,16},{16,24},{1,9},{9,17},{17,25},{2,10},{10,18},{18,26},{... | collective-permute-start | bytes 404936 | tf_op jit(solution)/shard_map/ppermute | solution.py:173
  32.4 1.3 collective-permute-start.9
  33.8 3.5 %collective-permute-start.2 = (f32[4,4,1,16,128]{4,3,2,1,0:T(8,128)S(1)}, f32[4,4,1,16,128]{4,3,2,1,0:T(8,128)S(1)}, u32[]{:S(2)}, u32[]{:S(2)}) collective-permute-start(f32[4,4,1,16,128]{4,3,2,1,0:T(8,128)S(1)} %get-tuple-element.8), channel_id=1, source_target_pairs={{0,2},{2,4},{4,6},{1,3},{3,5},{5,7},{8,10},{10,12},{12,14},{9,11},... | collective-permute-start | bytes 393224 | tf_op jit(solution)/shard_map/ppermute | solution.py:23
  37.3 1.3 collective-permute-start.3
  39.9 1.2 copy.21
  41.2 1.3 copy.19
  42.5 2.0 collective-permute-done.3
  44.5 4.6 %collective-permute-start.4 = (f32[4,4,4,1,128]{4,3,2,1,0:T(1,128)S(1)}, f32[4,4,4,1,128]{4,3,2,1,0:T(1,128)S(1)}, u32[]{:S(2)}, u32[]{:S(2)}) collective-permute-start(f32[4,4,4,1,128]{4,3,2,1,0:T(1,128)S(1)} %get-tuple-element.6), channel_id=1, source_target_pairs={{0,1},{2,3},{4,5},{6,7},{8,9},{10,11},{12,13},{14,15},{16,17},{18,... | collective-permute-start | bytes 98312 | tf_op jit(solution)/shard_map/ppermute | solution.py:23
  49.1 1.3 collective-permute-start.5
  50.4 2.1 %pad_add_fusion = f32[36,19,148]{1,2,0:T(8,128)S(1)} fusion(f32[11,19,148]{1,2,0:T(8,128)} %copy.21, f32[12,19,148]{1,2,0:T(8,128)} %copy.19, f32[19,19,148]{1,2,0:T(8,128)} %copy-done.3), kind=kLoop, calls=%fused_computation.1 | loop fusion | flops 202464 | bytes 877344 | tf_op jit(solution)/shard_map/add | solution.py:182
  52.5 2.3 %slice.113 = f32[36,12,148]{1,2,0:T(8,128)} slice(f32[36,19,148]{1,2,0:T(8,128)S(1)} %pad_add_fusion), slice={[0:36], [7:19], [0:148]} | slice | bytes 511488 | tf_op jit(solution)/shard_map/slice | solution.py:171
  54.8 4.0 %copy.22 = f32[36,12,148]{2,0,1:T(8,128)} copy(f32[36,12,148]{1,2,0:T(8,128)} %slice.113) | data formatting | bytes 511488 | tf_op jit(solution)/shard_map/slice | solution.py:171
  58.9 4.3 %collective-permute-start.10 = (f32[36,12,148]{2,0,1:T(8,128)}, f32[36,12,148]{2,0,1:T(8,128)}, u32[]{:S(2)}, u32[]{:S(2)}) collective-permute-start(f32[36,12,148]{2,0,1:T(8,128)} %copy.22), channel_id=1, source_target_pairs={{0,2},{2,4},{4,6},{1,3},{3,5},{5,7},{8,10},{10,12},{12,14},{9,11},... | collective-permute-start | bytes 767240 | tf_op jit(solution)/shard_map/ppermute | solution.py:173
  63.1 2.5 %copy.24 = f32[36,11,148]{2,0,1:T(8,128)} copy(f32[36,11,148]{1,2,0:T(8,128)S(1)} %bitcast.51) | data formatting | bytes 468864 | tf_op jit(solution)/shard_map/slice | solution.py:172
  65.6 1.3 collective-permute-start.11
  67.1 0.8 slice_add_fusion.3
  68.0 73.4 %shard_map.59 = f32[3,2,2,16,128]{4,3,2,1,0:T(8,128)} custom-call(s32[64]{0:T(128)S(1)} %reshape.310.counts_ref, f32[4,4,4,18,128]{4,3,2,1,0:T(8,128)S(1)} %pad_maximum_fusion.2.grown_ref, s32[2,2,16,128]{3,2,1,0:T(8,128)S(1)} %copy-done.2), custom_call_target="tpu_custom_call" | custom-call | flops 1000000000 | bytes 10000000 | tf_op jit(solution)/shard_map/pallas_call | solution.py:302
  141.4 3.2 %copy.25 = f32[36,11,148]{1,2,0:T(8,128)} copy(f32[36,11,148]{2,0,1:T(8,128)} %collective-permute-done.11) | data formatting | bytes 468864 | tf_op jit(solution)/shard_map/ppermute | solution.py:174
  144.6 3.2 %copy.23 = f32[36,12,148]{1,2,0:T(8,128)} copy(f32[36,12,148]{2,0,1:T(8,128)} %collective-permute-done.10) | data formatting | bytes 511488 | tf_op jit(solution)/shard_map/ppermute | solution.py:173
  147.8 5.9 %multiply_multiply_fusion = f32[36,36,148]{1,2,0:T(8,128)} fusion(f32[36,11,148]{1,2,0:T(8,128)} %copy.25, f32[36,12,148]{1,2,0:T(8,128)} %copy.23, f32[36,19,148]{1,2,0:T(8,128)S(1)} %pad_add_fusion, f32[148]{0:T(256)S(1)} %copy-done.12, f32[36,36]{1,0:T(8,128)S(1)} %broadcast_multiply_fusion), kind=kLoop, calls=%fused_computation | loop fusion | flops 767232 | bytes 1668112 | tf_op jit(solution)/shard_map/mul | solution.py:345
  153.7 3.5 %copy.26 = f32[36,36,148]{2,0,1:T(8,128)S(1)} copy(f32[36,36,148]{1,2,0:T(8,128)} %multiply_multiply_fusion) | data formatting | bytes 1534464 | tf_op jit(solution)/shard_map/mul | solution.py:345
  157.2 1.0 fusion.74
  158.2 0.7 convolution_bitcast_fusion.1
  159.8 5.8 %collective-permute-start.12 = (f32[17,17,6]{2,1,0:T(8,128)S(1)}, f32[17,17,6]{2,1,0:T(8,128)S(1)}, u32[]{:S(2)}, u32[]{:S(2)}) collective-permute-start(f32[17,17,6]{2,1,0:T(8,128)S(1)} %slice.115), channel_id=1, source_target_pairs={{0,1},{2,3},{4,5},{6,7},{8,9},{10,11},{12,13},{14,15},{16,17},{18,... | collective-permute-start | bytes 20816 | tf_op jit(solution)/shard_map/ppermute | solution.py:197
  165.6 1.5 collective-permute-start.13
  167.1 0.9 fusion.77
  168.0 5.3 %collective-permute-done.13 = f32[17,17,5]{2,1,0:T(8,128)S(1)} collective-permute-done((f32[17,17,5]{2,1,0:T(8,128)S(1)}, f32[17,17,5]{2,1,0:T(8,128)S(1)}, u32[]{:S(2)}, u32[]{:S(2)}) %collective-permute-start.13) | collective-permute-done | bytes 5812 | tf_op jit(solution)/shard_map/ppermute | solution.py:198
  173.4 7.4 %collective-permute-start.14 = (f32[6,17,84]{2,1,0:T(8,128)S(1)}, f32[6,17,84]{2,1,0:T(8,128)S(1)}, u32[]{:S(2)}, u32[]{:S(2)}) collective-permute-start(f32[6,17,84]{2,1,0:T(8,128)S(1)} %pad_maximum_fusion.9), channel_id=1, source_target_pairs={{0,8},{8,16},{16,24},{1,9},{9,17},{17,25},{2,10},{10,18},{18,26},{... | collective-permute-start | bytes 102824 | tf_op jit(solution)/shard_map/ppermute | solution.py:197
  180.9 1.3 collective-permute-start.15
  182.2 0.8 convolution_bitcast_fusion
  183.1 3.3 %collective-permute-done.15 = f32[5,17,84]{2,1,0:T(8,128)S(1)} collective-permute-done((f32[5,17,84]{2,1,0:T(8,128)S(1)}, f32[5,17,84]{2,1,0:T(8,128)S(1)}, u32[]{:S(2)}, u32[]{:S(2)}) %collective-permute-start.15) | collective-permute-done | bytes 28592 | tf_op jit(solution)/shard_map/ppermute | solution.py:198
  186.5 3.1 %collective-permute-start.16 = (f32[28,6,84]{2,1,0:T(8,128)S(1)}, f32[28,6,84]{2,1,0:T(8,128)S(1)}, u32[]{:S(2)}, u32[]{:S(2)}) collective-permute-start(f32[28,6,84]{2,1,0:T(8,128)S(1)} %pad_maximum_fusion.8), channel_id=1, source_target_pairs={{0,2},{2,4},{4,6},{1,3},{3,5},{5,7},{8,10},{10,12},{12,14},{9,11},... | collective-permute-start | bytes 169352 | tf_op jit(solution)/shard_map/ppermute | solution.py:197
  189.8 1.3 collective-permute-start.17
  191.1 1.4 fusion.13
  192.5 4.2 %collective-permute-done.17 = f32[28,5,84]{2,1,0:T(8,128)S(1)} collective-permute-done((f32[28,5,84]{2,1,0:T(8,128)S(1)}, f32[28,5,84]{2,1,0:T(8,128)S(1)}, u32[]{:S(2)}, u32[]{:S(2)}) %collective-permute-start.17) | collective-permute-done | bytes 47072 | tf_op jit(solution)/shard_map/ppermute | solution.py:198
  199.1 1.4 fusion.29
  200.6 0.8 fusion.1
  201.4 0.7 pad_maximum_fusion.grid_ref
  202.2 7.9 %shard_map.61 = f32[3,2,2,16,128]{4,3,2,1,0:T(8,128)} custom-call(f32[3,2,2,16,128]{4,3,2,1,0:T(8,128)S(1)} %copy-done.1, f32[2,2,16,128]{3,2,1,0:T(8,128)S(1)} %fusion.63.weighted_ref, f32[19,136,96]{2,1,0:T(8,128)S(1)} %pad_maximum_fusion.grid_ref), custom_call_target="tpu_custom_call" | custom-call | flops 100000000 | bytes 4000000 | tf_op jit(solution)/shard_map/pallas_call | solution.py:156
  (99 shorter events, 12.3 us)
Async XLA Ops:
  1.5 0.9 copy-start
  10.1 6.3 %copy-start.4 = (f32[2,2,16,128]{3,2,1,0:T(8,128)S(1)}, f32[2,2,16,128]{3,2,1,0:T(8,128)}, u32[]{:S(2)}) copy-start(f32[2,2,16,128]{3,2,1,0:T(8,128)} %param.5) | copy-start | bytes 98308
  10.1 6.3 %copy-start.5 = (s32[2,2,16]{2,1,0:T(2,128)S(1)}, s32[2,2,16]{2,1,0:T(2,128)}, u32[]{:S(2)}) copy-start(s32[2,2,16]{2,1,0:T(2,128)} %param.6) | copy-start | bytes 772
  10.2 15.2 %collective-permute-start.6 = (f32[19,19,12]{1,2,0:T(8,128)S(1)}, f32[19,19,12]{1,2,0:T(8,128)S(1)}, u32[]{:S(2)}, u32[]{:S(2)}) collective-permute-start(f32[19,19,12]{1,2,0:T(8,128)S(1)} %slice.109), channel_id=1, source_target_pairs={{0,1},{2,3},{4,5},{6,7},{8,9},{10,11},{12,13},{14,15},{16,17},{18,... | collective-permute-start | bytes 51992 | tf_op jit(solution)/shard_map/ppermute | solution.py:173
  15.1 10.3 %collective-permute-start.7 = (f32[19,19,11]{1,2,0:T(8,128)S(1)}, f32[19,19,11]{1,2,0:T(8,128)S(1)}, u32[]{:S(2)}, u32[]{:S(2)}) collective-permute-start(f32[19,19,11]{1,2,0:T(8,128)S(1)} %slice.110), channel_id=1, source_target_pairs={{1,0},{3,2},{5,4},{7,6},{9,8},{11,10},{13,12},{15,14},{17,16},{19,... | collective-permute-start | bytes 47660 | tf_op jit(solution)/shard_map/ppermute | solution.py:174
  16.5 17.2 %collective-permute-start = (f32[4,1,2,16,128]{4,3,2,1,0:T(8,128)S(1)}, f32[4,1,2,16,128]{4,3,2,1,0:T(8,128)S(1)}, u32[]{:S(2)}, u32[]{:S(2)}) collective-permute-start(f32[4,1,2,16,128]{4,3,2,1,0:T(8,128)S(1)} %get-tuple-element.10), channel_id=1, source_target_pairs={{0,8},{8,16},{16,24},{1,9},{9,17},{17,25},{2,10},{10,18},{18,26},{... | collective-permute-start | bytes 196616 | tf_op jit(solution)/shard_map/ppermute | solution.py:23
  18.0 15.7 %collective-permute-start.1 = (f32[4,1,2,16,128]{4,3,2,1,0:T(8,128)S(1)}, f32[4,1,2,16,128]{4,3,2,1,0:T(8,128)S(1)}, u32[]{:S(2)}, u32[]{:S(2)}) collective-permute-start(f32[4,1,2,16,128]{4,3,2,1,0:T(8,128)S(1)} %get-tuple-element.11), channel_id=1, source_target_pairs={{8,0},{16,8},{24,16},{9,1},{17,9},{25,17},{10,2},{18,10},{26,18},{... | collective-permute-start | bytes 196616 | tf_op jit(solution)/shard_map/ppermute | solution.py:24
  25.6 1.1 copy-start.3
  26.8 6.9 %copy-start.1 = (f32[3,2,2,16,128]{4,3,2,1,0:T(8,128)S(1)}, f32[3,2,2,16,128]{4,3,2,1,0:T(8,128)}, u32[]{:S(2)}) copy-start(f32[3,2,2,16,128]{4,3,2,1,0:T(8,128)} %offsets_ref.3) | copy-start | bytes 294916
  27.3 13.8 %collective-permute-start.8 = (f32[12,19,148]{2,1,0:T(8,128)S(1)}, f32[12,19,148]{2,1,0:T(8,128)S(1)}, u32[]{:S(2)}, u32[]{:S(2)}) collective-permute-start(f32[12,19,148]{2,1,0:T(8,128)S(1)} %copy.18), channel_id=1, source_target_pairs={{0,8},{8,16},{16,24},{1,9},{9,17},{17,25},{2,10},{10,18},{18,26},{... | collective-permute-start | bytes 404936 | tf_op jit(solution)/shard_map/ppermute | solution.py:173
  32.4 7.5 %collective-permute-start.9 = (f32[11,19,148]{2,1,0:T(8,128)S(1)}, f32[11,19,148]{2,1,0:T(8,128)S(1)}, u32[]{:S(2)}, u32[]{:S(2)}) collective-permute-start(f32[11,19,148]{2,1,0:T(8,128)S(1)} %copy.20), channel_id=1, source_target_pairs={{8,0},{16,8},{24,16},{9,1},{17,9},{25,17},{10,2},{18,10},{26,18},{... | collective-permute-start | bytes 371192 | tf_op jit(solution)/shard_map/ppermute | solution.py:174
  33.8 8.7 %collective-permute-start.2 = (f32[4,4,1,16,128]{4,3,2,1,0:T(8,128)S(1)}, f32[4,4,1,16,128]{4,3,2,1,0:T(8,128)S(1)}, u32[]{:S(2)}, u32[]{:S(2)}) collective-permute-start(f32[4,4,1,16,128]{4,3,2,1,0:T(8,128)S(1)} %get-tuple-element.8), channel_id=1, source_target_pairs={{0,2},{2,4},{4,6},{1,3},{3,5},{5,7},{8,10},{10,12},{12,14},{9,11},... | collective-permute-start | bytes 393224 | tf_op jit(solution)/shard_map/ppermute | solution.py:23
  37.3 7.2 %collective-permute-start.3 = (f32[4,4,1,16,128]{4,3,2,1,0:T(8,128)S(1)}, f32[4,4,1,16,128]{4,3,2,1,0:T(8,128)S(1)}, u32[]{:S(2)}, u32[]{:S(2)}) collective-permute-start(f32[4,4,1,16,128]{4,3,2,1,0:T(8,128)S(1)} %get-tuple-element.9), channel_id=1, source_target_pairs={{2,0},{4,2},{6,4},{3,1},{5,3},{7,5},{10,8},{12,10},{14,12},{11,9},... | collective-permute-start | bytes 393224 | tf_op jit(solution)/shard_map/ppermute | solution.py:24
  44.5 22.4 %collective-permute-start.4 = (f32[4,4,4,1,128]{4,3,2,1,0:T(1,128)S(1)}, f32[4,4,4,1,128]{4,3,2,1,0:T(1,128)S(1)}, u32[]{:S(2)}, u32[]{:S(2)}) collective-permute-start(f32[4,4,4,1,128]{4,3,2,1,0:T(1,128)S(1)} %get-tuple-element.6), channel_id=1, source_target_pairs={{0,1},{2,3},{4,5},{6,7},{8,9},{10,11},{12,13},{14,15},{16,17},{18,... | collective-permute-start | bytes 98312 | tf_op jit(solution)/shard_map/ppermute | solution.py:23
  49.1 17.9 %collective-permute-start.5 = (f32[4,4,4,1,128]{4,3,2,1,0:T(1,128)S(1)}, f32[4,4,4,1,128]{4,3,2,1,0:T(1,128)S(1)}, u32[]{:S(2)}, u32[]{:S(2)}) collective-permute-start(f32[4,4,4,1,128]{4,3,2,1,0:T(1,128)S(1)} %get-tuple-element.7), channel_id=1, source_target_pairs={{1,0},{3,2},{5,4},{7,6},{9,8},{11,10},{13,12},{15,14},{17,16},{19,... | collective-permute-start | bytes 98312 | tf_op jit(solution)/shard_map/ppermute | solution.py:24
  58.9 85.7 %collective-permute-start.10 = (f32[36,12,148]{2,0,1:T(8,128)}, f32[36,12,148]{2,0,1:T(8,128)}, u32[]{:S(2)}, u32[]{:S(2)}) collective-permute-start(f32[36,12,148]{2,0,1:T(8,128)} %copy.22), channel_id=1, source_target_pairs={{0,2},{2,4},{4,6},{1,3},{3,5},{5,7},{8,10},{10,12},{12,14},{9,11},... | collective-permute-start | bytes 767240 | tf_op jit(solution)/shard_map/ppermute | solution.py:173
  65.6 75.8 %collective-permute-start.11 = (f32[36,11,148]{2,0,1:T(8,128)}, f32[36,11,148]{2,0,1:T(8,128)}, u32[]{:S(2)}, u32[]{:S(2)}) collective-permute-start(f32[36,11,148]{2,0,1:T(8,128)} %copy.24), channel_id=1, source_target_pairs={{2,0},{4,2},{6,4},{3,1},{5,3},{7,5},{10,8},{12,10},{14,12},{11,9},... | collective-permute-start | bytes 703304 | tf_op jit(solution)/shard_map/ppermute | solution.py:174
  67.1 0.9 copy-start.2
  144.6 3.2 %copy-start.12 = (f32[148]{0:T(256)S(1)}, f32[148]{0:T(256)}, u32[]{:S(2)}) copy-start(f32[148]{0:T(256)} %and_convert_fusion.9) | copy-start | bytes 1780
  153.7 3.5 %copy-start.8 = (s32[17]{0:T(128)S(1)}, s32[17]{0:T(128)}, u32[]{:S(2)}) copy-start(s32[17]{0:T(128)} %add_multiply_fusion.2) | copy-start | bytes 208
  153.7 3.5 %copy-start.9 = (s32[36]{0:T(128)S(1)}, s32[36]{0:T(128)}, u32[]{:S(2)}) copy-start(s32[36]{0:T(128)} %iota_add_fusion.2) | copy-start | bytes 436
  157.2 1.8 copy-start.10
  157.2 1.8 copy-start.16
  159.8 13.5 %collective-permute-start.12 = (f32[17,17,6]{2,1,0:T(8,128)S(1)}, f32[17,17,6]{2,1,0:T(8,128)S(1)}, u32[]{:S(2)}, u32[]{:S(2)}) collective-permute-start(f32[17,17,6]{2,1,0:T(8,128)S(1)} %slice.115), channel_id=1, source_target_pairs={{0,1},{2,3},{4,5},{6,7},{8,9},{10,11},{12,13},{14,15},{16,17},{18,... | collective-permute-start | bytes 20816 | tf_op jit(solution)/shard_map/ppermute | solution.py:197
  165.6 7.7 %collective-permute-start.13 = (f32[17,17,5]{2,1,0:T(8,128)S(1)}, f32[17,17,5]{2,1,0:T(8,128)S(1)}, u32[]{:S(2)}, u32[]{:S(2)}) collective-permute-start(f32[17,17,5]{2,1,0:T(8,128)S(1)} %slice.116), channel_id=1, source_target_pairs={{1,0},{3,2},{5,4},{7,6},{9,8},{11,10},{13,12},{15,14},{17,16},{19,... | collective-permute-start | bytes 17348 | tf_op jit(solution)/shard_map/ppermute | solution.py:198
  173.4 13.0 %collective-permute-start.14 = (f32[6,17,84]{2,1,0:T(8,128)S(1)}, f32[6,17,84]{2,1,0:T(8,128)S(1)}, u32[]{:S(2)}, u32[]{:S(2)}) collective-permute-start(f32[6,17,84]{2,1,0:T(8,128)S(1)} %pad_maximum_fusion.9), channel_id=1, source_target_pairs={{0,8},{8,16},{16,24},{1,9},{9,17},{17,25},{2,10},{10,18},{18,26},{... | collective-permute-start | bytes 102824 | tf_op jit(solution)/shard_map/ppermute | solution.py:197
  180.9 5.5 %collective-permute-start.15 = (f32[5,17,84]{2,1,0:T(8,128)S(1)}, f32[5,17,84]{2,1,0:T(8,128)S(1)}, u32[]{:S(2)}, u32[]{:S(2)}) collective-permute-start(f32[5,17,84]{2,1,0:T(8,128)S(1)} %pad_maximum_fusion.11), channel_id=1, source_target_pairs={{8,0},{16,8},{24,16},{9,1},{17,9},{25,17},{10,2},{18,10},{26,18},{... | collective-permute-start | bytes 85688 | tf_op jit(solution)/shard_map/ppermute | solution.py:198
  186.5 10.2 %copy-start.14 = (f32[84]{0:T(128)S(1)}, f32[84]{0:T(128)}, u32[]{:S(2)}) copy-start(f32[84]{0:T(128)} %and_convert_fusion.6) | copy-start | bytes 1012
  186.5 10.2 %collective-permute-start.16 = (f32[28,6,84]{2,1,0:T(8,128)S(1)}, f32[28,6,84]{2,1,0:T(8,128)S(1)}, u32[]{:S(2)}, u32[]{:S(2)}) collective-permute-start(f32[28,6,84]{2,1,0:T(8,128)S(1)} %pad_maximum_fusion.8), channel_id=1, source_target_pairs={{0,2},{2,4},{4,6},{1,3},{3,5},{5,7},{8,10},{10,12},{12,14},{9,11},... | collective-permute-start | bytes 169352 | tf_op jit(solution)/shard_map/ppermute | solution.py:197
  189.8 6.9 %collective-permute-start.17 = (f32[28,5,84]{2,1,0:T(8,128)S(1)}, f32[28,5,84]{2,1,0:T(8,128)S(1)}, u32[]{:S(2)}, u32[]{:S(2)}) collective-permute-start(f32[28,5,84]{2,1,0:T(8,128)S(1)} %pad_maximum_fusion.4), channel_id=1, source_target_pairs={{2,0},{4,2},{6,4},{3,1},{5,3},{7,5},{10,8},{12,10},{14,12},{11,9},... | collective-permute-start | bytes 141128 | tf_op jit(solution)/shard_map/ppermute | solution.py:198
  192.5 5.5 %copy-start.15 = (f32[68]{0:T(128)S(1)}, f32[68]{0:T(128)}, u32[]{:S(2)}) copy-start(f32[68]{0:T(128)} %and_convert_fusion.3) | copy-start | bytes 820
  192.5 5.7 %copy-start.6 = (s32[12]{0:T(128)S(1)}, s32[12]{0:T(128)}, u32[]{:S(2)}) copy-start(s32[12]{0:T(128)} %add_multiply_fusion.3) | copy-start | bytes 148
  192.5 5.7 %copy-start.7 = (s32[20]{0:T(128)S(1)}, s32[20]{0:T(128)}, u32[]{:S(2)}) copy-start(s32[20]{0:T(128)} %iota_add_fusion.3) | copy-start | bytes 244
  192.5 6.6 %copy-start.11 = (s32[132]{0:T(256)S(1)}, s32[132]{0:T(256)}, u32[]{:S(2)}) copy-start(s32[132]{0:T(256)} %iota_add_fusion) | copy-start | bytes 1588
  192.5 6.6 %copy-start.13 = (s32[68]{0:T(128)S(1)}, s32[68]{0:T(128)}, u32[]{:S(2)}) copy-start(s32[68]{0:T(128)} %add_multiply_fusion) | copy-start | bytes 820

commit v5 on v4

--- a/solution.py
+++ b/solution.py
@@ -241,6 +241,13 @@
     _, cells_x, cells_y, cells_z, slots = out_ref.shape
     lane = lax.broadcasted_iota(jnp.int32, (1, slots), 1)
 
+    part_row = lax.broadcasted_iota(jnp.int32, (16, slots), 0)
+    pick_row = lax.broadcasted_iota(jnp.int32, (16, 3 * slots), 0)
+    pick_lane = lax.broadcasted_iota(jnp.int32, (16, 3 * slots), 1)
+    picked = (pick_row < 9) & (pick_row % 3 == pick_lane // slots)
+    picker = jnp.where(picked, 1.0, 0.0).astype(jnp.bfloat16)
+    ones = jnp.ones((16, slots), jnp.bfloat16)
+
     def fill_body(column, carry):
         i, j = column // (cells_y + 2), column % (cells_y + 2)
         for k in range(cells_z + 2):
@@ -256,8 +263,19 @@
         k = cell % cells_z
         count = counts_ref[cell]
         own_rows = [grown_ref[d, i + 1, j + 1, pl.ds(k + 1, 1), :] for d in range(3)]
+        rest = jnp.concatenate(own_rows * 3 + [jnp.zeros((7, slots), jnp.float32)], axis=0)
+        high = rest.astype(jnp.bfloat16).astype(jnp.float32)
+        middle = (rest - high).astype(jnp.bfloat16).astype(jnp.float32)
+        low = rest - high - middle
+        parts = jnp.where(part_row < 3, high, jnp.where(part_row < 6, middle, low))
+        columns = lax.dot_general(
+            parts.astype(jnp.bfloat16),
+            picker,
+            (((0,), (0,)), ((), ())),
+            preferred_element_type=jnp.float32,
+        )
         for d in range(3):
-            own_s[d] = jnp.broadcast_to(own_rows[d], (slots, slots)).T
+            own_s[d] = columns[:, d * slots : (d + 1) * slots]
 
         def block_body(block, carry):
             row = pl.multiple_of(block * 8, 8)
@@ -286,8 +304,17 @@
         partner = partners_ref[i, j, pl.ds(k, 1), :]
         bonded = (lane < count) & (partner < count)
         index = jnp.broadcast_to(partner, (8, slots))
+        sums = acc_s[...].reshape(3 * slots, slots)
+        sums_high = sums.astype(jnp.bfloat16)
+        sums_low = (sums - sums_high.astype(jnp.float32)).astype(jnp.bfloat16)
+        sums_row = sum(
+            lax.dot_general(
+                ones, part, (((1,), (1,)), ((), ())), preferred_element_type=jnp.float32
+            )
+            for part in (sums_high, sums_low)
+        )
         for d in range(3):
-            pair = 0.125 * charge * jnp.sum(acc_s[d].T, axis=0, keepdims=True)
+            pair = 0.125 * charge * sums_row[0:1, d * slots : (d + 1) * slots]
             source = jnp.broadcast_to(own_rows[d], (8, slots))
             other = jnp.take_along_axis(source, index, axis=1)[0:1]
             bond = jnp.where(bonded, (-8.0 * bond_spring) * (own_rows[d] - other), 0.0)

time: 212 us -> 221 us (1.042)
  Pallas kernels: 89.1 us -> 99 us
  waiting for transfers between devices: 14.8 us -> 22.4 us
  starting transfers between devices: 51.4 us -> 44.5 us
    pallas_call x1, Pallas kernels: 73.4 us -> 83.4 us  [short_forces(): pl.pallas_call(short_kernel, out_shape=jax.ShapeDtypeStruct((3,) + cells...]
    ppermute x3, waiting for transfers between devices: 12.8 us -> 20.4 us  [coarse_halo(): after = lax.ppermute(initial, axis, down)]
    ppermute x3, starting transfers between devices: 16.3 us -> 9.48 us  [coarse_halo(): before = lax.ppermute(last, axis, up)]
  transfers between devices with their start and end apart: 18 -> 18, of which waited for: 4 -> 4; matrix products, arithmetic and copies ran while one was open for 14% -> 14% of each run, Pallas kernels for 35% -> 38%
where the time goes in v5:
time: 221 us
  Pallas kernels  99 us (45%)
  starting transfers between devices  44.5 us (20%)
  local copies, waits for them, and re-layouts  25 us (11%)
  waiting for transfers between devices  22.4 us (10%)
  other arithmetic  19.7 us (9%)
  matrix products  8.81 us (4%)
    pallas_call x1, Pallas kernels, short_forces(): pl.pallas_call(short_kernel, out_shape=jax.ShapeDtypeStruct((3,) + cells...  83.4 us
    ppermute x3, waiting for transfers between devices, coarse_halo(): after = lax.ppermute(initial, axis, down)  20.4 us
    ppermute x3, starting transfers between devices, spread_halo(): before = lax.ppermute(last, axis, up)  13.8 us
    ppermute x3, starting transfers between devices, padded_2(): before = lax.ppermute(last, axis, up)  9.5 us
    ppermute x3, starting transfers between devices, coarse_halo(): before = lax.ppermute(last, axis, up)  9.48 us
    dot_general x12, matrix products, along_axis(): jnp.tensordot(values, matrix, axes=([where_axis], [0]), precision=highest)  8.81 us
    pallas_call x1, Pallas kernels, grid_forces(): pl.pallas_call(gather_kernel, out_shape=jax.ShapeDtypeStruct(offsets.shap...  7.93 us
    pallas_call x1, Pallas kernels, spread_charge(): pl.pallas_call(spread_kernel, out_shape=jax.ShapeDtypeStruct((8 * cells_x...  7.71 us
  transfers between devices with their start and end apart: 18, of which 4 were waited for; matrix products, arithmetic and copies ran while one was open for 14% of the time, Pallas kernels for 38%

profile of v5, /device:TPU:0, one launch (start us, length us, event | category | flops | bytes accessed | tf_op | source)
XLA Modules:
  0.0 220.8 jit_solution(276461820749879320)
XLA Ops:
  0.6 0.8 fusion.63.weighted_ref
  1.5 0.9 copy-done
  2.4 7.7 %shard_map.60 = f32[19,136,32]{2,1,0:T(8,128)S(1)} custom-call(f32[3,2,2,16,128]{4,3,2,1,0:T(8,128)S(1)} %copy-done, f32[2,2,16,128]{3,2,1,0:T(8,128)S(1)} %fusion.63.weighted_ref), custom_call_target="tpu_custom_call" | custom-call | flops 100000000 | bytes 4000000 | tf_op jit(solution)/shard_map/pallas_call | solution.py:94
  10.2 4.9 %collective-permute-start.6 = (f32[19,19,12]{1,2,0:T(8,128)S(1)}, f32[19,19,12]{1,2,0:T(8,128)S(1)}, u32[]{:S(2)}, u32[]{:S(2)}) collective-permute-start(f32[19,19,12]{1,2,0:T(8,128)S(1)} %slice.109), channel_id=1, source_target_pairs={{0,1},{2,3},{4,5},{6,7},{8,9},{10,11},{12,13},{14,15},{16,17},{18,... | collective-permute-start | bytes 51992 | tf_op jit(solution)/shard_map/ppermute | solution.py:173
  15.1 1.3 collective-permute-start.7
  16.5 1.5 collective-permute-start
  18.0 1.3 collective-permute-start.1
  19.8 0.6 iota_add_fusion.2
  25.7 1.1 copy-done.3
  27.3 4.6 %collective-permute-start.8 = (f32[12,19,148]{2,1,0:T(8,128)S(1)}, f32[12,19,148]{2,1,0:T(8,128)S(1)}, u32[]{:S(2)}, u32[]{:S(2)}) collective-permute-start(f32[12,19,148]{2,1,0:T(8,128)S(1)} %copy.18), channel_id=1, source_target_pairs={{0,8},{8,16},{16,24},{1,9},{9,17},{17,25},{2,10},{10,18},{18,26},{... | collective-permute-start | bytes 404936 | tf_op jit(solution)/shard_map/ppermute | solution.py:173
  32.4 1.3 collective-permute-start.9
  33.8 3.5 %collective-permute-start.2 = (f32[4,4,1,16,128]{4,3,2,1,0:T(8,128)S(1)}, f32[4,4,1,16,128]{4,3,2,1,0:T(8,128)S(1)}, u32[]{:S(2)}, u32[]{:S(2)}) collective-permute-start(f32[4,4,1,16,128]{4,3,2,1,0:T(8,128)S(1)} %get-tuple-element.8), channel_id=1, source_target_pairs={{0,2},{2,4},{4,6},{1,3},{3,5},{5,7},{8,10},{10,12},{12,14},{9,11},... | collective-permute-start | bytes 393224 | tf_op jit(solution)/shard_map/ppermute | solution.py:23
  37.3 1.3 collective-permute-start.3
  39.9 1.2 copy.21
  41.2 1.3 copy.19
  42.5 2.0 collective-permute-done.3
  44.5 4.6 %collective-permute-start.4 = (f32[4,4,4,1,128]{4,3,2,1,0:T(1,128)S(1)}, f32[4,4,4,1,128]{4,3,2,1,0:T(1,128)S(1)}, u32[]{:S(2)}, u32[]{:S(2)}) collective-permute-start(f32[4,4,4,1,128]{4,3,2,1,0:T(1,128)S(1)} %get-tuple-element.6), channel_id=1, source_target_pairs={{0,1},{2,3},{4,5},{6,7},{8,9},{10,11},{12,13},{14,15},{16,17},{18,... | collective-permute-start | bytes 98312 | tf_op jit(solution)/shard_map/ppermute | solution.py:23
  49.1 1.3 collective-permute-start.5
  50.4 2.1 pad_add_fusion
  52.5 2.3 %slice.113 = f32[36,12,148]{1,2,0:T(8,128)} slice(f32[36,19,148]{1,2,0:T(8,128)S(1)} %pad_add_fusion), slice={[0:36], [7:19], [0:148]} | slice | bytes 511488 | tf_op jit(solution)/shard_map/slice | solution.py:171
  54.8 4.0 %copy.22 = f32[36,12,148]{2,0,1:T(8,128)} copy(f32[36,12,148]{1,2,0:T(8,128)} %slice.113) | data formatting | bytes 511488 | tf_op jit(solution)/shard_map/slice | solution.py:171
  58.9 4.3 %collective-permute-start.10 = (f32[36,12,148]{2,0,1:T(8,128)}, f32[36,12,148]{2,0,1:T(8,128)}, u32[]{:S(2)}, u32[]{:S(2)}) collective-permute-start(f32[36,12,148]{2,0,1:T(8,128)} %copy.22), channel_id=1, source_target_pairs={{0,2},{2,4},{4,6},{1,3},{3,5},{5,7},{8,10},{10,12},{12,14},{9,11},... | collective-permute-start | bytes 767240 | tf_op jit(solution)/shard_map/ppermute | solution.py:173
  63.1 2.5 %copy.24 = f32[36,11,148]{2,0,1:T(8,128)} copy(f32[36,11,148]{1,2,0:T(8,128)S(1)} %bitcast.51) | data formatting | bytes 468864 | tf_op jit(solution)/shard_map/slice | solution.py:172
  65.6 1.3 collective-permute-start.11
  67.1 0.8 slice_add_fusion.3
  68.0 83.4 %shard_map.59 = f32[3,2,2,16,128]{4,3,2,1,0:T(8,128)} custom-call(s32[64]{0:T(128)S(1)} %reshape.310.counts_ref, f32[4,4,4,18,128]{4,3,2,1,0:T(8,128)S(1)} %pad_maximum_fusion.2.grown_ref, s32[2,2,16,128]{3,2,1,0:T(8,128)S(1)} %copy-done.2), custom_call_target="tpu_custom_call" | custom-call | flops 1000000000 | bytes 10000000 | tf_op jit(solution)/shard_map/pallas_call | solution.py:329
  151.4 3.2 %copy.25 = f32[36,11,148]{1,2,0:T(8,128)} copy(f32[36,11,148]{2,0,1:T(8,128)} %collective-permute-done.11) | data formatting | bytes 468864 | tf_op jit(solution)/shard_map/ppermute | solution.py:174
  154.5 3.2 %copy.23 = f32[36,12,148]{1,2,0:T(8,128)} copy(f32[36,12,148]{2,0,1:T(8,128)} %collective-permute-done.10) | data formatting | bytes 511488 | tf_op jit(solution)/shard_map/ppermute | solution.py:173
  157.8 5.9 %multiply_multiply_fusion = f32[36,36,148]{1,2,0:T(8,128)} fusion(f32[36,11,148]{1,2,0:T(8,128)} %copy.25, f32[36,12,148]{1,2,0:T(8,128)} %copy.23, f32[36,19,148]{1,2,0:T(8,128)S(1)} %pad_add_fusion, f32[148]{0:T(256)S(1)} %copy-done.12, f32[36,36]{1,0:T(8,128)S(1)} %broadcast_multiply_fusion), kind=kLoop, calls=%fused_computation | loop fusion | flops 767232 | bytes 1668112 | tf_op jit(solution)/shard_map/mul | solution.py:372
  163.6 3.5 %copy.26 = f32[36,36,148]{2,0,1:T(8,128)S(1)} copy(f32[36,36,148]{1,2,0:T(8,128)} %multiply_multiply_fusion) | data formatting | bytes 1534464 | tf_op jit(solution)/shard_map/mul | solution.py:372
  167.2 1.0 fusion.74
  168.2 0.7 convolution_bitcast_fusion.1
  169.7 6.9 %collective-permute-start.12 = (f32[17,17,6]{2,1,0:T(8,128)S(1)}, f32[17,17,6]{2,1,0:T(8,128)S(1)}, u32[]{:S(2)}, u32[]{:S(2)}) collective-permute-start(f32[17,17,6]{2,1,0:T(8,128)S(1)} %slice.115), channel_id=1, source_target_pairs={{0,1},{2,3},{4,5},{6,7},{8,9},{10,11},{12,13},{14,15},{16,17},{18,... | collective-permute-start | bytes 20816 | tf_op jit(solution)/shard_map/ppermute | solution.py:197
  176.6 1.5 collective-permute-start.13
  178.1 0.9 fusion.77
  179.0 5.3 %collective-permute-done.13 = f32[17,17,5]{2,1,0:T(8,128)S(1)} collective-permute-done((f32[17,17,5]{2,1,0:T(8,128)S(1)}, f32[17,17,5]{2,1,0:T(8,128)S(1)}, u32[]{:S(2)}, u32[]{:S(2)}) %collective-permute-start.13) | collective-permute-done | bytes 5812 | tf_op jit(solution)/shard_map/ppermute | solution.py:198
  184.5 1.3 collective-permute-start.14
  185.9 1.3 collective-permute-start.15
  187.2 0.8 convolution_bitcast_fusion
  188.0 9.2 %collective-permute-done.15 = f32[5,17,84]{2,1,0:T(8,128)S(1)} collective-permute-done((f32[5,17,84]{2,1,0:T(8,128)S(1)}, f32[5,17,84]{2,1,0:T(8,128)S(1)}, u32[]{:S(2)}, u32[]{:S(2)}) %collective-permute-start.15) | collective-permute-done | bytes 28592 | tf_op jit(solution)/shard_map/ppermute | solution.py:198
  197.3 1.3 collective-permute-start.16
  198.7 1.3 collective-permute-start.17
  200.0 1.4 fusion.13
  201.5 5.9 %collective-permute-done.17 = f32[28,5,84]{2,1,0:T(8,128)S(1)} collective-permute-done((f32[28,5,84]{2,1,0:T(8,128)S(1)}, f32[28,5,84]{2,1,0:T(8,128)S(1)}, u32[]{:S(2)}, u32[]{:S(2)}) %collective-permute-start.17) | collective-permute-done | bytes 47072 | tf_op jit(solution)/shard_map/ppermute | solution.py:198
  209.8 1.4 fusion.29
  211.2 0.8 fusion.1
  212.1 0.7 pad_maximum_fusion.grid_ref
  212.9 7.9 %shard_map.61 = f32[3,2,2,16,128]{4,3,2,1,0:T(8,128)} custom-call(f32[3,2,2,16,128]{4,3,2,1,0:T(8,128)S(1)} %copy-done.1, f32[2,2,16,128]{3,2,1,0:T(8,128)S(1)} %fusion.63.weighted_ref, f32[19,136,96]{2,1,0:T(8,128)S(1)} %pad_maximum_fusion.grid_ref), custom_call_target="tpu_custom_call" | custom-call | flops 100000000 | bytes 4000000 | tf_op jit(solution)/shard_map/pallas_call | solution.py:156
  (99 shorter events, 12.3 us)
Async XLA Ops:
  1.5 0.9 copy-start
  10.1 6.3 %copy-start.4 = (f32[2,2,16,128]{3,2,1,0:T(8,128)S(1)}, f32[2,2,16,128]{3,2,1,0:T(8,128)}, u32[]{:S(2)}) copy-start(f32[2,2,16,128]{3,2,1,0:T(8,128)} %param.5) | copy-start | bytes 98308
  10.1 6.3 %copy-start.5 = (s32[2,2,16]{2,1,0:T(2,128)S(1)}, s32[2,2,16]{2,1,0:T(2,128)}, u32[]{:S(2)}) copy-start(s32[2,2,16]{2,1,0:T(2,128)} %param.6) | copy-start | bytes 772
  10.2 15.2 %collective-permute-start.6 = (f32[19,19,12]{1,2,0:T(8,128)S(1)}, f32[19,19,12]{1,2,0:T(8,128)S(1)}, u32[]{:S(2)}, u32[]{:S(2)}) collective-permute-start(f32[19,19,12]{1,2,0:T(8,128)S(1)} %slice.109), channel_id=1, source_target_pairs={{0,1},{2,3},{4,5},{6,7},{8,9},{10,11},{12,13},{14,15},{16,17},{18,... | collective-permute-start | bytes 51992 | tf_op jit(solution)/shard_map/ppermute | solution.py:173
  15.1 10.3 %collective-permute-start.7 = (f32[19,19,11]{1,2,0:T(8,128)S(1)}, f32[19,19,11]{1,2,0:T(8,128)S(1)}, u32[]{:S(2)}, u32[]{:S(2)}) collective-permute-start(f32[19,19,11]{1,2,0:T(8,128)S(1)} %slice.110), channel_id=1, source_target_pairs={{1,0},{3,2},{5,4},{7,6},{9,8},{11,10},{13,12},{15,14},{17,16},{19,... | collective-permute-start | bytes 47660 | tf_op jit(solution)/shard_map/ppermute | solution.py:174
  16.5 17.2 %collective-permute-start = (f32[4,1,2,16,128]{4,3,2,1,0:T(8,128)S(1)}, f32[4,1,2,16,128]{4,3,2,1,0:T(8,128)S(1)}, u32[]{:S(2)}, u32[]{:S(2)}) collective-permute-start(f32[4,1,2,16,128]{4,3,2,1,0:T(8,128)S(1)} %get-tuple-element.10), channel_id=1, source_target_pairs={{0,8},{8,16},{16,24},{1,9},{9,17},{17,25},{2,10},{10,18},{18,26},{... | collective-permute-start | bytes 196616 | tf_op jit(solution)/shard_map/ppermute | solution.py:23
  18.0 15.7 %collective-permute-start.1 = (f32[4,1,2,16,128]{4,3,2,1,0:T(8,128)S(1)}, f32[4,1,2,16,128]{4,3,2,1,0:T(8,128)S(1)}, u32[]{:S(2)}, u32[]{:S(2)}) collective-permute-start(f32[4,1,2,16,128]{4,3,2,1,0:T(8,128)S(1)} %get-tuple-element.11), channel_id=1, source_target_pairs={{8,0},{16,8},{24,16},{9,1},{17,9},{25,17},{10,2},{18,10},{26,18},{... | collective-permute-start | bytes 196616 | tf_op jit(solution)/shard_map/ppermute | solution.py:24
  25.6 1.1 copy-start.3
  26.8 6.9 %copy-start.1 = (f32[3,2,2,16,128]{4,3,2,1,0:T(8,128)S(1)}, f32[3,2,2,16,128]{4,3,2,1,0:T(8,128)}, u32[]{:S(2)}) copy-start(f32[3,2,2,16,128]{4,3,2,1,0:T(8,128)} %offsets_ref.3) | copy-start | bytes 294916
  27.3 13.8 %collective-permute-start.8 = (f32[12,19,148]{2,1,0:T(8,128)S(1)}, f32[12,19,148]{2,1,0:T(8,128)S(1)}, u32[]{:S(2)}, u32[]{:S(2)}) collective-permute-start(f32[12,19,148]{2,1,0:T(8,128)S(1)} %copy.18), channel_id=1, source_target_pairs={{0,8},{8,16},{16,24},{1,9},{9,17},{17,25},{2,10},{10,18},{18,26},{... | collective-permute-start | bytes 404936 | tf_op jit(solution)/shard_map/ppermute | solution.py:173
  32.4 7.5 %collective-permute-start.9 = (f32[11,19,148]{2,1,0:T(8,128)S(1)}, f32[11,19,148]{2,1,0:T(8,128)S(1)}, u32[]{:S(2)}, u32[]{:S(2)}) collective-permute-start(f32[11,19,148]{2,1,0:T(8,128)S(1)} %copy.20), channel_id=1, source_target_pairs={{8,0},{16,8},{24,16},{9,1},{17,9},{25,17},{10,2},{18,10},{26,18},{... | collective-permute-start | bytes 371192 | tf_op jit(solution)/shard_map/ppermute | solution.py:174
  33.8 8.7 %collective-permute-start.2 = (f32[4,4,1,16,128]{4,3,2,1,0:T(8,128)S(1)}, f32[4,4,1,16,128]{4,3,2,1,0:T(8,128)S(1)}, u32[]{:S(2)}, u32[]{:S(2)}) collective-permute-start(f32[4,4,1,16,128]{4,3,2,1,0:T(8,128)S(1)} %get-tuple-element.8), channel_id=1, source_target_pairs={{0,2},{2,4},{4,6},{1,3},{3,5},{5,7},{8,10},{10,12},{12,14},{9,11},... | collective-permute-start | bytes 393224 | tf_op jit(solution)/shard_map/ppermute | solution.py:23
  37.3 7.2 %collective-permute-start.3 = (f32[4,4,1,16,128]{4,3,2,1,0:T(8,128)S(1)}, f32[4,4,1,16,128]{4,3,2,1,0:T(8,128)S(1)}, u32[]{:S(2)}, u32[]{:S(2)}) collective-permute-start(f32[4,4,1,16,128]{4,3,2,1,0:T(8,128)S(1)} %get-tuple-element.9), channel_id=1, source_target_pairs={{2,0},{4,2},{6,4},{3,1},{5,3},{7,5},{10,8},{12,10},{14,12},{11,9},... | collective-permute-start | bytes 393224 | tf_op jit(solution)/shard_map/ppermute | solution.py:24
  44.5 22.4 %collective-permute-start.4 = (f32[4,4,4,1,128]{4,3,2,1,0:T(1,128)S(1)}, f32[4,4,4,1,128]{4,3,2,1,0:T(1,128)S(1)}, u32[]{:S(2)}, u32[]{:S(2)}) collective-permute-start(f32[4,4,4,1,128]{4,3,2,1,0:T(1,128)S(1)} %get-tuple-element.6), channel_id=1, source_target_pairs={{0,1},{2,3},{4,5},{6,7},{8,9},{10,11},{12,13},{14,15},{16,17},{18,... | collective-permute-start | bytes 98312 | tf_op jit(solution)/shard_map/ppermute | solution.py:23
  49.1 17.9 %collective-permute-start.5 = (f32[4,4,4,1,128]{4,3,2,1,0:T(1,128)S(1)}, f32[4,4,4,1,128]{4,3,2,1,0:T(1,128)S(1)}, u32[]{:S(2)}, u32[]{:S(2)}) collective-permute-start(f32[4,4,4,1,128]{4,3,2,1,0:T(1,128)S(1)} %get-tuple-element.7), channel_id=1, source_target_pairs={{1,0},{3,2},{5,4},{7,6},{9,8},{11,10},{13,12},{15,14},{17,16},{19,... | collective-permute-start | bytes 98312 | tf_op jit(solution)/shard_map/ppermute | solution.py:24
  58.9 95.7 %collective-permute-start.10 = (f32[36,12,148]{2,0,1:T(8,128)}, f32[36,12,148]{2,0,1:T(8,128)}, u32[]{:S(2)}, u32[]{:S(2)}) collective-permute-start(f32[36,12,148]{2,0,1:T(8,128)} %copy.22), channel_id=1, source_target_pairs={{0,2},{2,4},{4,6},{1,3},{3,5},{5,7},{8,10},{10,12},{12,14},{9,11},... | collective-permute-start | bytes 767240 | tf_op jit(solution)/shard_map/ppermute | solution.py:173
  65.6 85.8 %collective-permute-start.11 = (f32[36,11,148]{2,0,1:T(8,128)}, f32[36,11,148]{2,0,1:T(8,128)}, u32[]{:S(2)}, u32[]{:S(2)}) collective-permute-start(f32[36,11,148]{2,0,1:T(8,128)} %copy.24), channel_id=1, source_target_pairs={{2,0},{4,2},{6,4},{3,1},{5,3},{7,5},{10,8},{12,10},{14,12},{11,9},... | collective-permute-start | bytes 703304 | tf_op jit(solution)/shard_map/ppermute | solution.py:174
  67.1 0.9 copy-start.2
  154.5 3.2 %copy-start.12 = (f32[148]{0:T(256)S(1)}, f32[148]{0:T(256)}, u32[]{:S(2)}) copy-start(f32[148]{0:T(256)} %and_convert_fusion.9) | copy-start | bytes 1780
  163.6 3.5 %copy-start.8 = (s32[17]{0:T(128)S(1)}, s32[17]{0:T(128)}, u32[]{:S(2)}) copy-start(s32[17]{0:T(128)} %add_multiply_fusion.2) | copy-start | bytes 208
  163.6 3.5 %copy-start.9 = (s32[36]{0:T(128)S(1)}, s32[36]{0:T(128)}, u32[]{:S(2)}) copy-start(s32[36]{0:T(128)} %iota_add_fusion.2) | copy-start | bytes 436
  167.2 1.8 copy-start.10
  167.2 1.8 copy-start.16
  169.7 14.6 %collective-permute-start.12 = (f32[17,17,6]{2,1,0:T(8,128)S(1)}, f32[17,17,6]{2,1,0:T(8,128)S(1)}, u32[]{:S(2)}, u32[]{:S(2)}) collective-permute-start(f32[17,17,6]{2,1,0:T(8,128)S(1)} %slice.115), channel_id=1, source_target_pairs={{0,1},{2,3},{4,5},{6,7},{8,9},{10,11},{12,13},{14,15},{16,17},{18,... | collective-permute-start | bytes 20816 | tf_op jit(solution)/shard_map/ppermute | solution.py:197
  176.6 7.7 %collective-permute-start.13 = (f32[17,17,5]{2,1,0:T(8,128)S(1)}, f32[17,17,5]{2,1,0:T(8,128)S(1)}, u32[]{:S(2)}, u32[]{:S(2)}) collective-permute-start(f32[17,17,5]{2,1,0:T(8,128)S(1)} %slice.116), channel_id=1, source_target_pairs={{1,0},{3,2},{5,4},{7,6},{9,8},{11,10},{13,12},{15,14},{17,16},{19,... | collective-permute-start | bytes 17348 | tf_op jit(solution)/shard_map/ppermute | solution.py:198
  184.5 12.7 %collective-permute-start.14 = (f32[6,17,84]{2,1,0:T(8,128)S(1)}, f32[6,17,84]{2,1,0:T(8,128)S(1)}, u32[]{:S(2)}, u32[]{:S(2)}) collective-permute-start(f32[6,17,84]{2,1,0:T(8,128)S(1)} %pad_maximum_fusion.9), channel_id=1, source_target_pairs={{0,8},{8,16},{16,24},{1,9},{9,17},{17,25},{2,10},{10,18},{18,26},{... | collective-permute-start | bytes 102824 | tf_op jit(solution)/shard_map/ppermute | solution.py:197
  185.9 11.3 %collective-permute-start.15 = (f32[5,17,84]{2,1,0:T(8,128)S(1)}, f32[5,17,84]{2,1,0:T(8,128)S(1)}, u32[]{:S(2)}, u32[]{:S(2)}) collective-permute-start(f32[5,17,84]{2,1,0:T(8,128)S(1)} %pad_maximum_fusion.11), channel_id=1, source_target_pairs={{8,0},{16,8},{24,16},{9,1},{17,9},{25,17},{10,2},{18,10},{26,18},{... | collective-permute-start | bytes 85688 | tf_op jit(solution)/shard_map/ppermute | solution.py:198
  197.3 10.1 %copy-start.14 = (f32[84]{0:T(128)S(1)}, f32[84]{0:T(128)}, u32[]{:S(2)}) copy-start(f32[84]{0:T(128)} %and_convert_fusion.6) | copy-start | bytes 1012
  197.3 10.1 %collective-permute-start.16 = (f32[28,6,84]{2,1,0:T(8,128)S(1)}, f32[28,6,84]{2,1,0:T(8,128)S(1)}, u32[]{:S(2)}, u32[]{:S(2)}) collective-permute-start(f32[28,6,84]{2,1,0:T(8,128)S(1)} %pad_maximum_fusion.8), channel_id=1, source_target_pairs={{0,2},{2,4},{4,6},{1,3},{3,5},{5,7},{8,10},{10,12},{12,14},{9,11},... | collective-permute-start | bytes 169352 | tf_op jit(solution)/shard_map/ppermute | solution.py:197
  198.7 8.7 %collective-permute-start.17 = (f32[28,5,84]{2,1,0:T(8,128)S(1)}, f32[28,5,84]{2,1,0:T(8,128)S(1)}, u32[]{:S(2)}, u32[]{:S(2)}) collective-permute-start(f32[28,5,84]{2,1,0:T(8,128)S(1)} %pad_maximum_fusion.4), channel_id=1, source_target_pairs={{2,0},{4,2},{6,4},{3,1},{5,3},{7,5},{10,8},{12,10},{14,12},{11,9},... | collective-permute-start | bytes 141128 | tf_op jit(solution)/shard_map/ppermute | solution.py:198
  201.4 7.2 %copy-start.15 = (f32[68]{0:T(128)S(1)}, f32[68]{0:T(128)}, u32[]{:S(2)}) copy-start(f32[68]{0:T(128)} %and_convert_fusion.3) | copy-start | bytes 820
  201.4 7.5 %copy-start.6 = (s32[12]{0:T(128)S(1)}, s32[12]{0:T(128)}, u32[]{:S(2)}) copy-start(s32[12]{0:T(128)} %add_multiply_fusion.3) | copy-start | bytes 148
  201.4 7.5 %copy-start.7 = (s32[20]{0:T(128)S(1)}, s32[20]{0:T(128)}, u32[]{:S(2)}) copy-start(s32[20]{0:T(128)} %iota_add_fusion.3) | copy-start | bytes 244
  201.4 8.4 %copy-start.11 = (s32[132]{0:T(256)S(1)}, s32[132]{0:T(256)}, u32[]{:S(2)}) copy-start(s32[132]{0:T(256)} %iota_add_fusion) | copy-start | bytes 1588
  201.4 8.4 %copy-start.13 = (s32[68]{0:T(128)S(1)}, s32[68]{0:T(128)}, u32[]{:S(2)}) copy-start(s32[68]{0:T(128)} %add_multiply_fusion) | copy-start | bytes 820

commit v6 on v4

--- a/solution.py
+++ b/solution.py
@@ -260,28 +260,28 @@
             own_s[d] = jnp.broadcast_to(own_rows[d], (slots, slots)).T
 
         def block_body(block, carry):
-            row = pl.multiple_of(block * 8, 8)
-            own = [own_s[d, pl.ds(row, 8), :] for d in range(3)]
-            total = [jnp.zeros((8, slots), jnp.float32) for _ in range(3)]
+            rows = [pl.ds(pl.multiple_of(block * 16 + 8 * h, 8), 8) for h in range(2)]
+            own = [[own_s[d, rows[h], :] for d in range(3)] for h in range(2)]
+            total = [[jnp.zeros((8, slots), jnp.float32)] * 3 for _ in range(2)]
             for step_x in range(3):
                 for step_y in range(3):
                     for step_z in range(3):
                         near = [
-                            near_s[i + step_x, j + step_y, k + step_z, d]
-                            for d in range(4)
+                            near_s[i + step_x, j + step_y, k + step_z, d] for d in range(4)
                         ]
-                        gap = [own[d] - near[d] for d in range(3)]
-                        distance_sq = gap[0] * gap[0] + gap[1] * gap[1] + gap[2] * gap[2]
-                        reach = jnp.maximum(1.0 - distance_sq, 0.0)
-                        below = 1.015625 - reach
-                        inverse = pl.reciprocal(below, approx=True)
-                        strength = (reach * reach) * (reach * near[3]) * inverse
-                        total = [total[d] + strength * gap[d] for d in range(3)]
-            for d in range(3):
-                acc_s[d, pl.ds(row, 8), :] = total[d]
+                        for h in range(2):
+                            gap = [own[h][d] - near[d] for d in range(3)]
+                            distance_sq = gap[0] * gap[0] + gap[1] * gap[1] + gap[2] * gap[2]
+                            reach = jnp.maximum(1.0 - distance_sq, 0.0)
+                            inverse = pl.reciprocal(1.015625 - reach, approx=True)
+                            strength = (reach * reach) * (reach * near[3]) * inverse
+                            total[h] = [total[h][d] + strength * gap[d] for d in range(3)]
+            for h in range(2):
+                for d in range(3):
+                    acc_s[d, rows[h], :] = total[h][d]
             return carry
 
-        lax.fori_loop(0, (count + 7) // 8, block_body, 0)
+        lax.fori_loop(0, (count + 15) // 16, block_body, 0)
         charge = grown_ref[3, i + 1, j + 1, pl.ds(k + 1, 1), :]
         partner = partners_ref[i, j, pl.ds(k, 1), :]
         bonded = (lane < count) & (partner < count)

time: 212 us -> 211 us (level)
  Pallas kernels: 89.1 us -> 93.5 us
  starting transfers between devices: 51.4 us -> 47.5 us
    pallas_call x1, Pallas kernels: 73.4 us -> 77.9 us  [short_forces(): pl.pallas_call(short_kernel, out_shape=jax.ShapeDtypeStruct((3,) + cells...]
    ppermute x3, starting transfers between devices: 16.3 us -> 12.4 us  [coarse_halo(): before = lax.ppermute(last, axis, up)]
  transfers between devices with their start and end apart: 18 -> 18, of which waited for: 4 -> 4; matrix products, arithmetic and copies ran while one was open for 14% -> 14% of each run, Pallas kernels for 35% -> 37%
where the time goes in v6:
time: 211 us; the launch traced here: 210 us
  Pallas kernels  93.5 us (44%)
  starting transfers between devices  47.5 us (23%)
  local copies, waits for them, and re-layouts  25 us (12%)
  other arithmetic  19.7 us (9%)
  waiting for transfers between devices  14 us (7%)
  matrix products  8.81 us (4%)
    pallas_call x1, Pallas kernels, short_forces(): pl.pallas_call(short_kernel, out_shape=jax.ShapeDtypeStruct((3,) + cells...  77.9 us
    ppermute x3, starting transfers between devices, spread_halo(): before = lax.ppermute(last, axis, up)  13.8 us
    ppermute x3, starting transfers between devices, coarse_halo(): before = lax.ppermute(last, axis, up)  12.4 us
    ppermute x3, waiting for transfers between devices, coarse_halo(): after = lax.ppermute(initial, axis, down)  12 us
    ppermute x3, starting transfers between devices, padded_2(): before = lax.ppermute(last, axis, up)  9.5 us
    dot_general x12, matrix products, along_axis(): jnp.tensordot(values, matrix, axes=([where_axis], [0]), precision=highest)  8.81 us
    pallas_call x1, Pallas kernels, grid_forces(): pl.pallas_call(gather_kernel, out_shape=jax.ShapeDtypeStruct(offsets.shap...  7.93 us
    pallas_call x1, Pallas kernels, spread_charge(): pl.pallas_call(spread_kernel, out_shape=jax.ShapeDtypeStruct((8 * cells_x...  7.71 us
  transfers between devices with their start and end apart: 18, of which 4 were waited for; matrix products, arithmetic and copies ran while one was open for 14% of the time, Pallas kernels for 37%

profile of v6, /device:TPU:0, one launch (start us, length us, event | category | flops | bytes accessed | tf_op | source)
XLA Modules:
  0.0 209.9 jit_solution(9519181864742326010)
XLA Ops:
  0.6 0.8 fusion.63.weighted_ref
  1.5 0.9 copy-done
  2.4 7.7 %shard_map.60 = f32[19,136,32]{2,1,0:T(8,128)S(1)} custom-call(f32[3,2,2,16,128]{4,3,2,1,0:T(8,128)S(1)} %copy-done, f32[2,2,16,128]{3,2,1,0:T(8,128)S(1)} %fusion.63.weighted_ref), custom_call_target="tpu_custom_call" | custom-call | flops 100000000 | bytes 4000000 | tf_op jit(solution)/shard_map/pallas_call | solution.py:94
  10.2 4.9 %collective-permute-start.6 = (f32[19,19,12]{1,2,0:T(8,128)S(1)}, f32[19,19,12]{1,2,0:T(8,128)S(1)}, u32[]{:S(2)}, u32[]{:S(2)}) collective-permute-start(f32[19,19,12]{1,2,0:T(8,128)S(1)} %slice.109), channel_id=1, source_target_pairs={{0,1},{2,3},{4,5},{6,7},{8,9},{10,11},{12,13},{14,15},{16,17},{18,... | collective-permute-start | bytes 51992 | tf_op jit(solution)/shard_map/ppermute | solution.py:173
  15.1 1.3 collective-permute-start.7
  16.5 1.5 collective-permute-start
  18.0 1.3 collective-permute-start.1
  19.8 0.6 iota_add_fusion.2
  25.7 1.1 copy-done.3
  27.3 4.6 %collective-permute-start.8 = (f32[12,19,148]{2,1,0:T(8,128)S(1)}, f32[12,19,148]{2,1,0:T(8,128)S(1)}, u32[]{:S(2)}, u32[]{:S(2)}) collective-permute-start(f32[12,19,148]{2,1,0:T(8,128)S(1)} %copy.18), channel_id=1, source_target_pairs={{0,8},{8,16},{16,24},{1,9},{9,17},{17,25},{2,10},{10,18},{18,26},{... | collective-permute-start | bytes 404936 | tf_op jit(solution)/shard_map/ppermute | solution.py:173
  32.4 1.3 collective-permute-start.9
  33.8 3.5 %collective-permute-start.2 = (f32[4,4,1,16,128]{4,3,2,1,0:T(8,128)S(1)}, f32[4,4,1,16,128]{4,3,2,1,0:T(8,128)S(1)}, u32[]{:S(2)}, u32[]{:S(2)}) collective-permute-start(f32[4,4,1,16,128]{4,3,2,1,0:T(8,128)S(1)} %get-tuple-element.8), channel_id=1, source_target_pairs={{0,2},{2,4},{4,6},{1,3},{3,5},{5,7},{8,10},{10,12},{12,14},{9,11},... | collective-permute-start | bytes 393224 | tf_op jit(solution)/shard_map/ppermute | solution.py:23
  37.3 1.3 collective-permute-start.3
  39.9 1.2 copy.21
  41.2 1.3 copy.19
  42.5 2.0 collective-permute-done.3
  44.5 4.6 %collective-permute-start.4 = (f32[4,4,4,1,128]{4,3,2,1,0:T(1,128)S(1)}, f32[4,4,4,1,128]{4,3,2,1,0:T(1,128)S(1)}, u32[]{:S(2)}, u32[]{:S(2)}) collective-permute-start(f32[4,4,4,1,128]{4,3,2,1,0:T(1,128)S(1)} %get-tuple-element.6), channel_id=1, source_target_pairs={{0,1},{2,3},{4,5},{6,7},{8,9},{10,11},{12,13},{14,15},{16,17},{18,... | collective-permute-start | bytes 98312 | tf_op jit(solution)/shard_map/ppermute | solution.py:23
  49.1 1.3 collective-permute-start.5
  50.4 2.1 %pad_add_fusion = f32[36,19,148]{1,2,0:T(8,128)S(1)} fusion(f32[11,19,148]{1,2,0:T(8,128)} %copy.21, f32[12,19,148]{1,2,0:T(8,128)} %copy.19, f32[19,19,148]{1,2,0:T(8,128)} %copy-done.3), kind=kLoop, calls=%fused_computation.1 | loop fusion | flops 202464 | bytes 877344 | tf_op jit(solution)/shard_map/add | solution.py:182
  52.5 2.3 %slice.113 = f32[36,12,148]{1,2,0:T(8,128)} slice(f32[36,19,148]{1,2,0:T(8,128)S(1)} %pad_add_fusion), slice={[0:36], [7:19], [0:148]} | slice | bytes 511488 | tf_op jit(solution)/shard_map/slice | solution.py:171
  54.8 4.0 %copy.22 = f32[36,12,148]{2,0,1:T(8,128)} copy(f32[36,12,148]{1,2,0:T(8,128)} %slice.113) | data formatting | bytes 511488 | tf_op jit(solution)/shard_map/slice | solution.py:171
  58.9 4.3 %collective-permute-start.10 = (f32[36,12,148]{2,0,1:T(8,128)}, f32[36,12,148]{2,0,1:T(8,128)}, u32[]{:S(2)}, u32[]{:S(2)}) collective-permute-start(f32[36,12,148]{2,0,1:T(8,128)} %copy.22), channel_id=1, source_target_pairs={{0,2},{2,4},{4,6},{1,3},{3,5},{5,7},{8,10},{10,12},{12,14},{9,11},... | collective-permute-start | bytes 767240 | tf_op jit(solution)/shard_map/ppermute | solution.py:173
  63.1 2.5 %copy.24 = f32[36,11,148]{2,0,1:T(8,128)} copy(f32[36,11,148]{1,2,0:T(8,128)S(1)} %bitcast.51) | data formatting | bytes 468864 | tf_op jit(solution)/shard_map/slice | solution.py:172
  65.6 1.3 collective-permute-start.11
  67.1 0.8 slice_add_fusion.3
  68.0 77.9 %shard_map.59 = f32[3,2,2,16,128]{4,3,2,1,0:T(8,128)} custom-call(s32[64]{0:T(128)S(1)} %reshape.310.counts_ref, f32[4,4,4,18,128]{4,3,2,1,0:T(8,128)S(1)} %pad_maximum_fusion.2.grown_ref, s32[2,2,16,128]{3,2,1,0:T(8,128)S(1)} %copy-done.2), custom_call_target="tpu_custom_call" | custom-call | flops 1000000000 | bytes 10000000 | tf_op jit(solution)/shard_map/pallas_call | solution.py:302
  145.9 3.2 %copy.25 = f32[36,11,148]{1,2,0:T(8,128)} copy(f32[36,11,148]{2,0,1:T(8,128)} %collective-permute-done.11) | data formatting | bytes 468864 | tf_op jit(solution)/shard_map/ppermute | solution.py:174
  149.0 3.2 %copy.23 = f32[36,12,148]{1,2,0:T(8,128)} copy(f32[36,12,148]{2,0,1:T(8,128)} %collective-permute-done.10) | data formatting | bytes 511488 | tf_op jit(solution)/shard_map/ppermute | solution.py:173
  152.3 5.9 %multiply_multiply_fusion = f32[36,36,148]{1,2,0:T(8,128)} fusion(f32[36,11,148]{1,2,0:T(8,128)} %copy.25, f32[36,12,148]{1,2,0:T(8,128)} %copy.23, f32[36,19,148]{1,2,0:T(8,128)S(1)} %pad_add_fusion, f32[148]{0:T(256)S(1)} %copy-done.12, f32[36,36]{1,0:T(8,128)S(1)} %broadcast_multiply_fusion), kind=kLoop, calls=%fused_computation | loop fusion | flops 767232 | bytes 1668112 | tf_op jit(solution)/shard_map/mul | solution.py:345
  158.1 3.5 %copy.26 = f32[36,36,148]{2,0,1:T(8,128)S(1)} copy(f32[36,36,148]{1,2,0:T(8,128)} %multiply_multiply_fusion) | data formatting | bytes 1534464 | tf_op jit(solution)/shard_map/mul | solution.py:345
  161.7 1.0 fusion.74
  162.7 0.7 convolution_bitcast_fusion.1
  164.2 6.3 %collective-permute-start.12 = (f32[17,17,6]{2,1,0:T(8,128)S(1)}, f32[17,17,6]{2,1,0:T(8,128)S(1)}, u32[]{:S(2)}, u32[]{:S(2)}) collective-permute-start(f32[17,17,6]{2,1,0:T(8,128)S(1)} %slice.115), channel_id=1, source_target_pairs={{0,1},{2,3},{4,5},{6,7},{8,9},{10,11},{12,13},{14,15},{16,17},{18,... | collective-permute-start | bytes 20816 | tf_op jit(solution)/shard_map/ppermute | solution.py:197
  170.6 1.5 collective-permute-start.13
  172.1 0.9 fusion.77
  173.0 5.3 %collective-permute-done.13 = f32[17,17,5]{2,1,0:T(8,128)S(1)} collective-permute-done((f32[17,17,5]{2,1,0:T(8,128)S(1)}, f32[17,17,5]{2,1,0:T(8,128)S(1)}, u32[]{:S(2)}, u32[]{:S(2)}) %collective-permute-start.13) | collective-permute-done | bytes 5812 | tf_op jit(solution)/shard_map/ppermute | solution.py:198
  178.4 1.3 collective-permute-start.14
  179.8 1.3 collective-permute-start.15
  181.1 0.8 convolution_bitcast_fusion
  181.9 1.0 collective-permute-done.15
  183.1 4.8 %collective-permute-start.16 = (f32[28,6,84]{2,1,0:T(8,128)S(1)}, f32[28,6,84]{2,1,0:T(8,128)S(1)}, u32[]{:S(2)}, u32[]{:S(2)}) collective-permute-start(f32[28,6,84]{2,1,0:T(8,128)S(1)} %pad_maximum_fusion.8), channel_id=1, source_target_pairs={{0,2},{2,4},{4,6},{1,3},{3,5},{5,7},{8,10},{10,12},{12,14},{9,11},... | collective-permute-start | bytes 169352 | tf_op jit(solution)/shard_map/ppermute | solution.py:197
  188.0 1.3 collective-permute-start.17
  189.3 1.4 fusion.13
  190.7 5.7 %collective-permute-done.17 = f32[28,5,84]{2,1,0:T(8,128)S(1)} collective-permute-done((f32[28,5,84]{2,1,0:T(8,128)S(1)}, f32[28,5,84]{2,1,0:T(8,128)S(1)}, u32[]{:S(2)}, u32[]{:S(2)}) %collective-permute-start.17) | collective-permute-done | bytes 47072 | tf_op jit(solution)/shard_map/ppermute | solution.py:198
  198.9 1.4 fusion.29
  200.3 0.8 fusion.1
  201.2 0.7 pad_maximum_fusion.grid_ref
  201.9 7.9 %shard_map.61 = f32[3,2,2,16,128]{4,3,2,1,0:T(8,128)} custom-call(f32[3,2,2,16,128]{4,3,2,1,0:T(8,128)S(1)} %copy-done.1, f32[2,2,16,128]{3,2,1,0:T(8,128)S(1)} %fusion.63.weighted_ref, f32[19,136,96]{2,1,0:T(8,128)S(1)} %pad_maximum_fusion.grid_ref), custom_call_target="tpu_custom_call" | custom-call | flops 100000000 | bytes 4000000 | tf_op jit(solution)/shard_map/pallas_call | solution.py:156
  (99 shorter events, 12.3 us)
Async XLA Ops:
  1.5 0.9 copy-start
  10.1 6.3 %copy-start.4 = (f32[2,2,16,128]{3,2,1,0:T(8,128)S(1)}, f32[2,2,16,128]{3,2,1,0:T(8,128)}, u32[]{:S(2)}) copy-start(f32[2,2,16,128]{3,2,1,0:T(8,128)} %param.5) | copy-start | bytes 98308
  10.1 6.3 %copy-start.5 = (s32[2,2,16]{2,1,0:T(2,128)S(1)}, s32[2,2,16]{2,1,0:T(2,128)}, u32[]{:S(2)}) copy-start(s32[2,2,16]{2,1,0:T(2,128)} %param.6) | copy-start | bytes 772
  10.2 15.2 %collective-permute-start.6 = (f32[19,19,12]{1,2,0:T(8,128)S(1)}, f32[19,19,12]{1,2,0:T(8,128)S(1)}, u32[]{:S(2)}, u32[]{:S(2)}) collective-permute-start(f32[19,19,12]{1,2,0:T(8,128)S(1)} %slice.109), channel_id=1, source_target_pairs={{0,1},{2,3},{4,5},{6,7},{8,9},{10,11},{12,13},{14,15},{16,17},{18,... | collective-permute-start | bytes 51992 | tf_op jit(solution)/shard_map/ppermute | solution.py:173
  15.1 10.3 %collective-permute-start.7 = (f32[19,19,11]{1,2,0:T(8,128)S(1)}, f32[19,19,11]{1,2,0:T(8,128)S(1)}, u32[]{:S(2)}, u32[]{:S(2)}) collective-permute-start(f32[19,19,11]{1,2,0:T(8,128)S(1)} %slice.110), channel_id=1, source_target_pairs={{1,0},{3,2},{5,4},{7,6},{9,8},{11,10},{13,12},{15,14},{17,16},{19,... | collective-permute-start | bytes 47660 | tf_op jit(solution)/shard_map/ppermute | solution.py:174
  16.5 17.2 %collective-permute-start = (f32[4,1,2,16,128]{4,3,2,1,0:T(8,128)S(1)}, f32[4,1,2,16,128]{4,3,2,1,0:T(8,128)S(1)}, u32[]{:S(2)}, u32[]{:S(2)}) collective-permute-start(f32[4,1,2,16,128]{4,3,2,1,0:T(8,128)S(1)} %get-tuple-element.10), channel_id=1, source_target_pairs={{0,8},{8,16},{16,24},{1,9},{9,17},{17,25},{2,10},{10,18},{18,26},{... | collective-permute-start | bytes 196616 | tf_op jit(solution)/shard_map/ppermute | solution.py:23
  18.0 15.7 %collective-permute-start.1 = (f32[4,1,2,16,128]{4,3,2,1,0:T(8,128)S(1)}, f32[4,1,2,16,128]{4,3,2,1,0:T(8,128)S(1)}, u32[]{:S(2)}, u32[]{:S(2)}) collective-permute-start(f32[4,1,2,16,128]{4,3,2,1,0:T(8,128)S(1)} %get-tuple-element.11), channel_id=1, source_target_pairs={{8,0},{16,8},{24,16},{9,1},{17,9},{25,17},{10,2},{18,10},{26,18},{... | collective-permute-start | bytes 196616 | tf_op jit(solution)/shard_map/ppermute | solution.py:24
  25.6 1.1 copy-start.3
  26.8 6.9 %copy-start.1 = (f32[3,2,2,16,128]{4,3,2,1,0:T(8,128)S(1)}, f32[3,2,2,16,128]{4,3,2,1,0:T(8,128)}, u32[]{:S(2)}) copy-start(f32[3,2,2,16,128]{4,3,2,1,0:T(8,128)} %offsets_ref.3) | copy-start | bytes 294916
  27.3 13.8 %collective-permute-start.8 = (f32[12,19,148]{2,1,0:T(8,128)S(1)}, f32[12,19,148]{2,1,0:T(8,128)S(1)}, u32[]{:S(2)}, u32[]{:S(2)}) collective-permute-start(f32[12,19,148]{2,1,0:T(8,128)S(1)} %copy.18), channel_id=1, source_target_pairs={{0,8},{8,16},{16,24},{1,9},{9,17},{17,25},{2,10},{10,18},{18,26},{... | collective-permute-start | bytes 404936 | tf_op jit(solution)/shard_map/ppermute | solution.py:173
  32.4 7.5 %collective-permute-start.9 = (f32[11,19,148]{2,1,0:T(8,128)S(1)}, f32[11,19,148]{2,1,0:T(8,128)S(1)}, u32[]{:S(2)}, u32[]{:S(2)}) collective-permute-start(f32[11,19,148]{2,1,0:T(8,128)S(1)} %copy.20), channel_id=1, source_target_pairs={{8,0},{16,8},{24,16},{9,1},{17,9},{25,17},{10,2},{18,10},{26,18},{... | collective-permute-start | bytes 371192 | tf_op jit(solution)/shard_map/ppermute | solution.py:174
  33.8 8.7 %collective-permute-start.2 = (f32[4,4,1,16,128]{4,3,2,1,0:T(8,128)S(1)}, f32[4,4,1,16,128]{4,3,2,1,0:T(8,128)S(1)}, u32[]{:S(2)}, u32[]{:S(2)}) collective-permute-start(f32[4,4,1,16,128]{4,3,2,1,0:T(8,128)S(1)} %get-tuple-element.8), channel_id=1, source_target_pairs={{0,2},{2,4},{4,6},{1,3},{3,5},{5,7},{8,10},{10,12},{12,14},{9,11},... | collective-permute-start | bytes 393224 | tf_op jit(solution)/shard_map/ppermute | solution.py:23
  37.3 7.2 %collective-permute-start.3 = (f32[4,4,1,16,128]{4,3,2,1,0:T(8,128)S(1)}, f32[4,4,1,16,128]{4,3,2,1,0:T(8,128)S(1)}, u32[]{:S(2)}, u32[]{:S(2)}) collective-permute-start(f32[4,4,1,16,128]{4,3,2,1,0:T(8,128)S(1)} %get-tuple-element.9), channel_id=1, source_target_pairs={{2,0},{4,2},{6,4},{3,1},{5,3},{7,5},{10,8},{12,10},{14,12},{11,9},... | collective-permute-start | bytes 393224 | tf_op jit(solution)/shard_map/ppermute | solution.py:24
  44.5 22.4 %collective-permute-start.4 = (f32[4,4,4,1,128]{4,3,2,1,0:T(1,128)S(1)}, f32[4,4,4,1,128]{4,3,2,1,0:T(1,128)S(1)}, u32[]{:S(2)}, u32[]{:S(2)}) collective-permute-start(f32[4,4,4,1,128]{4,3,2,1,0:T(1,128)S(1)} %get-tuple-element.6), channel_id=1, source_target_pairs={{0,1},{2,3},{4,5},{6,7},{8,9},{10,11},{12,13},{14,15},{16,17},{18,... | collective-permute-start | bytes 98312 | tf_op jit(solution)/shard_map/ppermute | solution.py:23
  49.1 17.9 %collective-permute-start.5 = (f32[4,4,4,1,128]{4,3,2,1,0:T(1,128)S(1)}, f32[4,4,4,1,128]{4,3,2,1,0:T(1,128)S(1)}, u32[]{:S(2)}, u32[]{:S(2)}) collective-permute-start(f32[4,4,4,1,128]{4,3,2,1,0:T(1,128)S(1)} %get-tuple-element.7), channel_id=1, source_target_pairs={{1,0},{3,2},{5,4},{7,6},{9,8},{11,10},{13,12},{15,14},{17,16},{19,... | collective-permute-start | bytes 98312 | tf_op jit(solution)/shard_map/ppermute | solution.py:24
  58.9 90.2 %collective-permute-start.10 = (f32[36,12,148]{2,0,1:T(8,128)}, f32[36,12,148]{2,0,1:T(8,128)}, u32[]{:S(2)}, u32[]{:S(2)}) collective-permute-start(f32[36,12,148]{2,0,1:T(8,128)} %copy.22), channel_id=1, source_target_pairs={{0,2},{2,4},{4,6},{1,3},{3,5},{5,7},{8,10},{10,12},{12,14},{9,11},... | collective-permute-start | bytes 767240 | tf_op jit(solution)/shard_map/ppermute | solution.py:173
  65.6 80.3 %collective-permute-start.11 = (f32[36,11,148]{2,0,1:T(8,128)}, f32[36,11,148]{2,0,1:T(8,128)}, u32[]{:S(2)}, u32[]{:S(2)}) collective-permute-start(f32[36,11,148]{2,0,1:T(8,128)} %copy.24), channel_id=1, source_target_pairs={{2,0},{4,2},{6,4},{3,1},{5,3},{7,5},{10,8},{12,10},{14,12},{11,9},... | collective-permute-start | bytes 703304 | tf_op jit(solution)/shard_map/ppermute | solution.py:174
  67.1 0.9 copy-start.2
  149.0 3.2 %copy-start.12 = (f32[148]{0:T(256)S(1)}, f32[148]{0:T(256)}, u32[]{:S(2)}) copy-start(f32[148]{0:T(256)} %and_convert_fusion.9) | copy-start | bytes 1780
  158.1 3.5 %copy-start.8 = (s32[17]{0:T(128)S(1)}, s32[17]{0:T(128)}, u32[]{:S(2)}) copy-start(s32[17]{0:T(128)} %add_multiply_fusion.2) | copy-start | bytes 208
  158.1 3.5 %copy-start.9 = (s32[36]{0:T(128)S(1)}, s32[36]{0:T(128)}, u32[]{:S(2)}) copy-start(s32[36]{0:T(128)} %iota_add_fusion.2) | copy-start | bytes 436
  161.7 1.8 copy-start.10
  161.7 1.8 copy-start.16
  164.2 14.0 %collective-permute-start.12 = (f32[17,17,6]{2,1,0:T(8,128)S(1)}, f32[17,17,6]{2,1,0:T(8,128)S(1)}, u32[]{:S(2)}, u32[]{:S(2)}) collective-permute-start(f32[17,17,6]{2,1,0:T(8,128)S(1)} %slice.115), channel_id=1, source_target_pairs={{0,1},{2,3},{4,5},{6,7},{8,9},{10,11},{12,13},{14,15},{16,17},{18,... | collective-permute-start | bytes 20816 | tf_op jit(solution)/shard_map/ppermute | solution.py:197
  170.6 7.7 %collective-permute-start.13 = (f32[17,17,5]{2,1,0:T(8,128)S(1)}, f32[17,17,5]{2,1,0:T(8,128)S(1)}, u32[]{:S(2)}, u32[]{:S(2)}) collective-permute-start(f32[17,17,5]{2,1,0:T(8,128)S(1)} %slice.116), channel_id=1, source_target_pairs={{1,0},{3,2},{5,4},{7,6},{9,8},{11,10},{13,12},{15,14},{17,16},{19,... | collective-permute-start | bytes 17348 | tf_op jit(solution)/shard_map/ppermute | solution.py:198
  178.4 4.6 %collective-permute-start.14 = (f32[6,17,84]{2,1,0:T(8,128)S(1)}, f32[6,17,84]{2,1,0:T(8,128)S(1)}, u32[]{:S(2)}, u32[]{:S(2)}) collective-permute-start(f32[6,17,84]{2,1,0:T(8,128)S(1)} %pad_maximum_fusion.9), channel_id=1, source_target_pairs={{0,8},{8,16},{16,24},{1,9},{9,17},{17,25},{2,10},{10,18},{18,26},{... | collective-permute-start | bytes 102824 | tf_op jit(solution)/shard_map/ppermute | solution.py:197
  179.8 3.1 %collective-permute-start.15 = (f32[5,17,84]{2,1,0:T(8,128)S(1)}, f32[5,17,84]{2,1,0:T(8,128)S(1)}, u32[]{:S(2)}, u32[]{:S(2)}) collective-permute-start(f32[5,17,84]{2,1,0:T(8,128)S(1)} %pad_maximum_fusion.11), channel_id=1, source_target_pairs={{8,0},{16,8},{24,16},{9,1},{17,9},{25,17},{10,2},{18,10},{26,18},{... | collective-permute-start | bytes 85688 | tf_op jit(solution)/shard_map/ppermute | solution.py:198
  183.1 13.4 %copy-start.14 = (f32[84]{0:T(128)S(1)}, f32[84]{0:T(128)}, u32[]{:S(2)}) copy-start(f32[84]{0:T(128)} %and_convert_fusion.6) | copy-start | bytes 1012
  183.1 13.4 %collective-permute-start.16 = (f32[28,6,84]{2,1,0:T(8,128)S(1)}, f32[28,6,84]{2,1,0:T(8,128)S(1)}, u32[]{:S(2)}, u32[]{:S(2)}) collective-permute-start(f32[28,6,84]{2,1,0:T(8,128)S(1)} %pad_maximum_fusion.8), channel_id=1, source_target_pairs={{0,2},{2,4},{4,6},{1,3},{3,5},{5,7},{8,10},{10,12},{12,14},{9,11},... | collective-permute-start | bytes 169352 | tf_op jit(solution)/shard_map/ppermute | solution.py:197
  188.0 8.5 %collective-permute-start.17 = (f32[28,5,84]{2,1,0:T(8,128)S(1)}, f32[28,5,84]{2,1,0:T(8,128)S(1)}, u32[]{:S(2)}, u32[]{:S(2)}) collective-permute-start(f32[28,5,84]{2,1,0:T(8,128)S(1)} %pad_maximum_fusion.4), channel_id=1, source_target_pairs={{2,0},{4,2},{6,4},{3,1},{5,3},{7,5},{10,8},{12,10},{14,12},{11,9},... | collective-permute-start | bytes 141128 | tf_op jit(solution)/shard_map/ppermute | solution.py:198
  190.7 7.0 %copy-start.15 = (f32[68]{0:T(128)S(1)}, f32[68]{0:T(128)}, u32[]{:S(2)}) copy-start(f32[68]{0:T(128)} %and_convert_fusion.3) | copy-start | bytes 820
  190.7 7.3 %copy-start.6 = (s32[12]{0:T(128)S(1)}, s32[12]{0:T(128)}, u32[]{:S(2)}) copy-start(s32[12]{0:T(128)} %add_multiply_fusion.3) | copy-start | bytes 148
  190.7 7.3 %copy-start.7 = (s32[20]{0:T(128)S(1)}, s32[20]{0:T(128)}, u32[]{:S(2)}) copy-start(s32[20]{0:T(128)} %iota_add_fusion.3) | copy-start | bytes 244
  190.7 8.2 %copy-start.11 = (s32[132]{0:T(256)S(1)}, s32[132]{0:T(256)}, u32[]{:S(2)}) copy-start(s32[132]{0:T(256)} %iota_add_fusion) | copy-start | bytes 1588
  190.7 8.2 %copy-start.13 = (s32[68]{0:T(128)S(1)}, s32[68]{0:T(128)}, u32[]{:S(2)}) copy-start(s32[68]{0:T(128)} %add_multiply_fusion) | copy-start | bytes 820
